TPU v7x, 32 devices: a whole 2x2x4 slice. The times are simulated.
32 devices in a mesh: segment: 2 (over core), expert: 16 (over z, y, x).
Axes of the slice: x: 2, y: 2, z: 4, core: 2. Of those that a mesh axis runs over, the one named last changes fastest.
Arguments:
- fwd_input: bfloat16 [2, 1024, 1024], P('segment', 'expert'), may hold values from -6 to 6
- fwd_routes: int32 [2, 1024, 8], P('segment', 'expert'), may hold values from 0 to 15, all different within a row; in each aligned block of 64 rows (0 to 63, 64 to 127, ..., all dimensions but the last counted through in order) at most 32 rows name the same one
- fwd_gates: float32 [2, 1024, 8], P('segment', 'expert'), may hold values from 0.05 to 0.3
- bwd_input: bfloat16 [2, 1024, 1024], P('segment', 'expert'), may hold values from -6 to 6
- bwd_grad: bfloat16 [2, 1024, 1024], P('segment', 'expert'), may hold values from -6 to 6
- bwd_routes: int32 [2, 1024, 8], P('segment', 'expert'), may hold values from 0 to 15, all different within a row; in each aligned block of 64 rows (0 to 63, 64 to 127, ..., all dimensions but the last counted through in order) at most 32 rows name the same one
- bwd_gates: float32 [2, 1024, 8], P('segment', 'expert'), may hold values from 0.05 to 0.3
- norm_gain: float32 [2, 1024], P('segment'), may hold values from 0.25 to 1.75
- w_gate: bfloat16 [2, 16, 1024, 768], P('segment', 'expert'), may hold values from -0.1875 to 0.1875
- w_up: bfloat16 [2, 16, 1024, 768], P('segment', 'expert'), may hold values from -0.1875 to 0.1875
- w_down: bfloat16 [2, 16, 768, 1024], P('segment', 'expert'), may hold values from -0.21875 to 0.21875
Outputs:
- fwd_out: bfloat16 [2, 1024, 1024], P('segment', 'expert')
- bwd_out: bfloat16 [2, 1024, 1024], P('segment', 'expert')
Inputs may be any that keep to these rules, and one draw needn't show every extreme that they name: `fwd_routes`: each token names 8 different experts; within the 64 rows of one device (aligned blocks) no expert is named by more than 32 rows, a bound that some block reaches. `bwd_routes`: as for fwd_routes.
All inputs are finite; a program needn't handle non-finite values.
Results may differ from a plain program's by a relative error of at most 0.0051.
Values may be sent and summed in bfloat16 or wider, within the bound.
No kernel may reach another device: no remote copies, remote signals or barrier semaphores. Data moves between devices by JAX's collectives and lax.ppermute only.
A program may use at most 64 MiB of HBM per device.

v0:
```python
import jax
import jax.numpy as jnp
from jax import lax
from jax.sharding import PartitionSpec as P

EPSILON = 1e-06


def passed_along(block, axis, distance):
    devices = range(lax.axis_size(axis))
    route = [((i - distance) % len(devices), i) for i in devices]
    return lax.ppermute(block, axis, route)


def norm_scale(stream):
    return lax.rsqrt(jnp.mean(stream * stream, axis=-1, keepdims=True) + EPSILON)


def slot_target(routes, capacity, experts):
    flat_routes = routes.reshape(-1)
    onehot = (flat_routes[:, None] == jnp.arange(experts, dtype=jnp.int32)[None, :]).astype(
        jnp.int32
    )
    before = jnp.cumsum(onehot, axis=0) - onehot
    position = jnp.sum(before * onehot, axis=1)
    return flat_routes * capacity + position


def to_slots(values, target, experts, capacity):
    width = values.shape[-1]
    buffer = jnp.zeros((experts * capacity, width), values.dtype).at[target].set(values)
    return buffer.reshape(experts, capacity, width)


def transposed(left, right):
    return lax.dot_general(
        left, right, (((1,), (1,)), ((), ())), preferred_element_type=jnp.float32
    )


def expert_forward(inputs, gate_matrix, up_matrix, down_matrix):
    token_rows = inputs.reshape(-1, inputs.shape[-1])
    gate = jnp.dot(token_rows, gate_matrix, preferred_element_type=jnp.float32)
    upward = jnp.dot(token_rows, up_matrix, preferred_element_type=jnp.float32)
    hidden = (gate * jax.nn.sigmoid(gate) * upward).astype(jnp.bfloat16)
    result = jnp.dot(hidden, down_matrix, preferred_element_type=jnp.float32).astype(jnp.bfloat16)
    return result.reshape(inputs.shape)


def expert_backward(inputs, grads, gate_matrix, up_matrix, down_matrix):
    token_rows = inputs.reshape(-1, inputs.shape[-1])
    grad_rows = grads.reshape(-1, grads.shape[-1])
    gate = jnp.dot(token_rows, gate_matrix, preferred_element_type=jnp.float32)
    upward = jnp.dot(token_rows, up_matrix, preferred_element_type=jnp.float32)
    d_hidden = transposed(grad_rows, down_matrix)
    sigma = jax.nn.sigmoid(gate)
    d_gate = (d_hidden * upward * sigma * (1.0 + gate * (1.0 - sigma))).astype(jnp.bfloat16)
    d_up = (d_hidden * gate * sigma).astype(jnp.bfloat16)
    result = (transposed(d_gate, gate_matrix) + transposed(d_up, up_matrix)).astype(jnp.bfloat16)
    return result.reshape(inputs.shape)


def on_device(
    fwd_input,
    fwd_routes,
    fwd_gates,
    bwd_input,
    bwd_grad,
    bwd_routes,
    bwd_gates,
    norm_gain,
    w_gate,
    w_up,
    w_down,
):
    experts = lax.axis_size("expert")
    tokens_here = fwd_input.shape[1]
    width = fwd_input.shape[2]
    top_count = fwd_routes.shape[2]
    capacity = min(tokens_here, tokens_here * top_count // experts)
    gain = norm_gain[0]
    gate_matrix = w_gate[0, 0]
    up_matrix = w_up[0, 0]
    down_matrix = w_down[0, 0]
    fwd_stream = fwd_input[0].astype(jnp.float32)
    fwd_normed = (fwd_stream * norm_scale(fwd_stream) * gain).astype(jnp.bfloat16)
    fwd_target = slot_target(fwd_routes[0], capacity, experts)
    fwd_send = to_slots(jnp.repeat(fwd_normed, top_count, axis=0), fwd_target, experts, capacity)
    bwd_stream = bwd_input[0].astype(jnp.float32)
    bwd_scale = norm_scale(bwd_stream)
    bwd_normed = (bwd_stream * bwd_scale * gain).astype(jnp.bfloat16)
    grad_stream = bwd_grad[0].astype(jnp.float32)
    scaled = (
        (bwd_gates[0][:, :, None] * grad_stream[:, None, :]).astype(jnp.bfloat16).reshape(-1, width)
    )
    bwd_target = slot_target(bwd_routes[0], capacity, experts)
    bwd_rows = to_slots(jnp.repeat(bwd_normed, top_count, axis=0), bwd_target, experts, capacity)
    bwd_grads = to_slots(scaled, bwd_target, experts, capacity)
    fwd_result = expert_forward(
        lax.all_to_all(fwd_send, "expert", split_axis=0, concat_axis=0, tiled=True),
        gate_matrix,
        up_matrix,
        down_matrix,
    )
    fwd_back = lax.all_to_all(fwd_result, "expert", split_axis=0, concat_axis=0, tiled=True)
    bwd_result = expert_backward(
        lax.all_to_all(bwd_rows, "expert", split_axis=0, concat_axis=0, tiled=True),
        lax.all_to_all(bwd_grads, "expert", split_axis=0, concat_axis=0, tiled=True),
        gate_matrix,
        up_matrix,
        down_matrix,
    )
    bwd_back = lax.all_to_all(bwd_result, "expert", split_axis=0, concat_axis=0, tiled=True)
    fwd_picked = (
        fwd_back.reshape(-1, width)[fwd_target]
        .reshape(tokens_here, top_count, width)
        .astype(jnp.float32)
    )
    layer_out = (fwd_stream + jnp.sum(fwd_gates[0][:, :, None] * fwd_picked, axis=1)).astype(
        jnp.bfloat16
    )
    bwd_picked = (
        bwd_back.reshape(-1, width)[bwd_target]
        .reshape(tokens_here, top_count, width)
        .astype(jnp.float32)
    )
    summed = gain * jnp.sum(bwd_picked, axis=1)
    inner = jnp.mean(summed * bwd_stream, axis=-1, keepdims=True)
    d_input = (
        grad_stream + bwd_scale * summed - bwd_stream * bwd_scale * bwd_scale * bwd_scale * inner
    ).astype(jnp.bfloat16)
    forward_next = passed_along(layer_out[None], "segment", 1)
    backward_next = passed_along(d_input[None], "segment", -1)
    return (forward_next, backward_next)


def solution(mesh):
    placed = (
        P("segment", "expert", None),
        P("segment", "expert", None),
        P("segment", "expert", None),
        P("segment", "expert", None),
        P("segment", "expert", None),
        P("segment", "expert", None),
        P("segment", "expert", None),
        P("segment", None),
        P("segment", "expert", None, None),
        P("segment", "expert", None, None),
        P("segment", "expert", None, None),
    )
    return jax.shard_map(
        on_device,
        mesh=mesh,
        in_specs=placed,
        out_specs=(P("segment", "expert", None), P("segment", "expert", None)),
        check_vma=False,
    )
```

profile of v0, /device:TPU:0, one launch (start us, length us, event | category | flops | bytes accessed | tf_op | source)
XLA Modules:
  0.0 196.5 jit_solution(9912179530055783991)
XLA Ops:
  6.2 3.6 %scatter_custom_fusion.2 = bf16[512,1024]{1,0:T(8,128)(2,1)} fusion(s32[512]{0:T(512)S(1)} %bitcast.155, bf16[64,1024]{1,0:T(8,128)(2,1)S(1)} %fusion.57, bf16[]{:T(256)} %constant.8.clone.1), kind=kCustom, calls=%fused_computation.32 | custom fusion | bytes 1179650 | tf_op jit(solution)/shard_map/scatter | solution.py:31
  9.8 8.3 %all-to-all-start.3 = ((bf16[16,32,1024]{2,1,0:T(8,128)(2,1)}), bf16[16,32,1024]{2,1,0:T(8,128)(2,1)S(1)}, u32[]{:S(2)}, u32[]{:S(2)}) async-start(bf16[16,32,1024]{2,1,0:T(8,128)(2,1)} %bitcast.25), calls=%async_computation.3 | async-start | bytes 2097152 | tf_op jit(solution)/shard_map/all_to_all | solution.py:107
  18.3 3.7 %scatter_custom_fusion.1 = bf16[512,1024]{1,0:T(8,128)(2,1)} fusion(s32[512]{0:T(512)S(1)} %bitcast.156, f32[64,1024]{1,0:T(8,128)S(1)} %convert_bitcast_fusion.1, f32[512]{0:T(512)S(1)} %mul.207, bf16[]{:T(256)} %constant.8.clone.1), kind=kCustom, calls=%fused_computation.31 | custom fusion | flops 1048576 | bytes 1312770 | tf_op jit(solution)/shard_map/scatter | solution.py:31
  22.0 20.6 %all-to-all-done.3 = bf16[16,32,1024]{2,1,0:T(8,128)(2,1)S(1)} async-done(((bf16[16,32,1024]{2,1,0:T(8,128)(2,1)}), bf16[16,32,1024]{2,1,0:T(8,128)(2,1)S(1)}, u32[]{:S(2)}, u32[]{:S(2)}) %all-to-all-start.3) | async-done | bytes 1048608 | tf_op jit(solution)/shard_map/all_to_all | solution.py:107
  42.5 5.9 %all-to-all-start.2 = ((bf16[16,32,1024]{2,1,0:T(8,128)(2,1)}), bf16[16,32,1024]{2,1,0:T(8,128)(2,1)}, u32[]{:S(2)}, u32[]{:S(2)}) async-start(bf16[16,32,1024]{2,1,0:T(8,128)(2,1)} %bitcast.22), calls=%async_computation.2 | async-start | bytes 2097152 | tf_op jit(solution)/shard_map/all_to_all | solution.py:108
  48.4 3.5 %fusion.13 = f32[512,768]{1,0:T(8,128)} fusion(bf16[512,1024]{1,0:T(8,128)(2,1)S(1)} %bitcast.147, bf16[1,1,1024,768]{3,2,1,0:T(8,128)(2,1)} %param.19), kind=kOutput, calls=%fused_computation.22 | convolution fusion | flops 805306368 | bytes 4194304 | tf_op jit(solution)/shard_map/dot_general | solution.py:53
  51.9 19.5 %all-to-all-done.2 = bf16[16,32,1024]{2,1,0:T(8,128)(2,1)} async-done(((bf16[16,32,1024]{2,1,0:T(8,128)(2,1)}), bf16[16,32,1024]{2,1,0:T(8,128)(2,1)}, u32[]{:S(2)}, u32[]{:S(2)}) %all-to-all-start.2) | async-done | bytes 1048608 | tf_op jit(solution)/shard_map/all_to_all | solution.py:108
  71.4 3.9 %fusion.2 = f32[512,768]{1,0:T(8,128)} fusion(bf16[512,1024]{1,0:T(8,128)(2,1)} %bitcast.23, bf16[1,1,768,1024]{3,2,1,0:T(8,128)(2,1)} %param.21), kind=kOutput, calls=%fused_computation.11 | convolution fusion | flops 805306368 | bytes 4194304 | tf_op jit(solution)/shard_map/dot_general | solution.py:36
  75.4 6.1 %fusion.11 = f32[512,1024]{1,0:T(8,128)} fusion(bf16[1,1,1024,768]{3,2,1,0:T(8,128)(2,1)} %param.19, f32[512,768]{1,0:T(8,128)} %fusion.13, f32[512,768]{1,0:T(8,128)} %fusion.2, bf16[512,1024]{1,0:T(8,128)(2,1)S(1)} %bitcast.148, bf16[1,1,1024,768]{3,2,1,0:T(8,128)(2,1)S(1)} %copy-done), kind=kOutput, calls=%fused_computation.20 | convolution fusion | flops 1614544896 | bytes 9437184 | tf_op jit(solution)/shard_map/dot_general | solution.py:36
  81.4 4.6 %add_convert_fusion = bf16[512,1024]{1,0:T(8,128)(2,1)} fusion(f32[512,1024]{1,0:T(8,128)} %fusion.11, bf16[1,1,1024,768]{3,2,1,0:T(8,128)(2,1)S(1)} %copy-done, f32[512,768]{1,0:T(8,128)} %fusion.2, f32[512,768]{1,0:T(8,128)} %fusion.13), kind=kOutput, calls=%fused_computation.10 | convolution fusion | flops 808714240 | bytes 7864320 | tf_op jit(solution)/shard_map/dot_general | solution.py:36
  86.0 6.1 %all-to-all-start.4 = ((bf16[16,32,1024]{2,1,0:T(8,128)(2,1)}), bf16[16,32,1024]{2,1,0:T(8,128)(2,1)S(1)}, u32[]{:S(2)}, u32[]{:S(2)}) async-start(bf16[16,32,1024]{2,1,0:T(8,128)(2,1)} %bitcast.146), calls=%async_computation.4 | async-start | bytes 2097152 | tf_op jit(solution)/shard_map/all_to_all | solution.py:113
  92.5 1.2 reduce-window.14
  94.3 20.7 %all-to-all-done.4 = bf16[16,32,1024]{2,1,0:T(8,128)(2,1)S(1)} async-done(((bf16[16,32,1024]{2,1,0:T(8,128)(2,1)}), bf16[16,32,1024]{2,1,0:T(8,128)(2,1)S(1)}, u32[]{:S(2)}, u32[]{:S(2)}) %all-to-all-start.4) | async-done | bytes 1048608 | tf_op jit(solution)/shard_map/all_to_all | solution.py:113
  115.0 2.8 %gather_fusion.1 = bf16[512,1024]{1,0:T(8,128)(2,1)} fusion(bf16[512,1024]{1,0:T(8,128)(2,1)S(1)} %bitcast.143, s32[1024]{0:T(1024)S(1)} %pad_clamp_fusion), kind=kCustom, calls=%fused_computation.1 | custom fusion | bytes 2099200 | tf_op jit(solution)/shard_map/gather | solution.py:123
  117.8 1.9 convert_reduce_fusion
  119.8 2.8 %scatter_custom_fusion = bf16[512,1024]{1,0:T(8,128)(2,1)S(1)} fusion(s32[512]{0:T(512)S(1)} %bitcast.158, bf16[64,1024]{1,0:T(8,128)(2,1)S(1)} %get-tuple-element.3, bf16[]{:T(256)} %constant.8.clone.1), kind=kCustom, calls=%fused_computation.34 | custom fusion | bytes 1179650 | tf_op jit(solution)/shard_map/scatter | solution.py:31
  122.7 30.8 %all_to_all.25 = bf16[16,32,1024]{2,1,0:T(8,128)(2,1)S(1)} all-to-all(bf16[16,32,1024]{2,1,0:T(8,128)(2,1)S(1)} %bitcast.145), channel_id=1, replica_groups=mesh['segment'=2,'expert'=16] {'expert'}, dimensions={0} | all-to-all | bytes 2097152 | tf_op jit(solution)/shard_map/all_to_all | solution.py:100
  154.5 2.1 %fusion.15 = f32[512,768]{1,0:T(8,128)} fusion(bf16[512,1024]{1,0:T(8,128)(2,1)S(1)} %bitcast.150, bf16[1,1,1024,768]{3,2,1,0:T(8,128)(2,1)S(1)} %copy-done.9), kind=kOutput, calls=%fused_computation.24 | convolution fusion | flops 805306368 | bytes 4194304 | tf_op jit(solution)/shard_map/dot_general | solution.py:43
  156.6 5.5 %fusion.17 = bf16[512,1024]{1,0:T(8,128)(2,1)} fusion(bf16[1,1,768,1024]{3,2,1,0:T(8,128)(2,1)} %param.21, f32[512,768]{1,0:T(8,128)} %fusion.15, bf16[512,1024]{1,0:T(8,128)(2,1)} %bitcast.151, bf16[1,1,1024,768]{3,2,1,0:T(8,128)(2,1)S(1)} %copy-done), kind=kOutput, calls=%fused_computation.30 | convolution fusion | flops 1613496320 | bytes 6815744 | tf_op jit(solution)/shard_map/dot_general | solution.py:46
  162.1 4.0 %all-to-all-start.1 = ((bf16[16,32,1024]{2,1,0:T(8,128)(2,1)}), bf16[16,32,1024]{2,1,0:T(8,128)(2,1)S(1)}, u32[]{:S(2)}, u32[]{:S(2)}) async-start(bf16[16,32,1024]{2,1,0:T(8,128)(2,1)} %bitcast.149), calls=%async_computation.1 | async-start | bytes 2097152 | tf_op jit(solution)/shard_map/all_to_all | solution.py:105
  166.5 22.5 %all-to-all-done.1 = bf16[16,32,1024]{2,1,0:T(8,128)(2,1)S(1)} async-done(((bf16[16,32,1024]{2,1,0:T(8,128)(2,1)}), bf16[16,32,1024]{2,1,0:T(8,128)(2,1)S(1)}, u32[]{:S(2)}, u32[]{:S(2)}) %all-to-all-start.1) | async-done | bytes 1048608 | tf_op jit(solution)/shard_map/all_to_all | solution.py:105
  189.0 2.8 %gather_fusion = bf16[512,1024]{1,0:T(8,128)(2,1)} fusion(bf16[512,1024]{1,0:T(8,128)(2,1)S(1)} %bitcast.144, s32[1024]{0:T(1024)S(1)} %pad_clamp_fusion.1), kind=kCustom, calls=%fused_computation | custom fusion | bytes 2099200 | tf_op jit(solution)/shard_map/gather | solution.py:115
  191.8 1.9 fusion
  193.9 1.3 collective-permute-done
  (65 shorter events, 9.5 us)
Async XLA Ops:
  0.6 74.7 %copy-start = (bf16[1,1,1024,768]{3,2,1,0:T(8,128)(2,1)S(1)}, bf16[1,1,1024,768]{3,2,1,0:T(8,128)(2,1)}, u32[]{:S(2)}) copy-start(bf16[1,1,1024,768]{3,2,1,0:T(8,128)(2,1)} %param.20) | copy-start | bytes 4718596
  6.2 11.9 %copy-start.7 = (f32[1,64,8]{1,2,0:T(8,128)S(1)}, f32[1,64,8]{1,2,0:T(8,128)}, u32[]{:S(2)}) copy-start(f32[1,64,8]{1,2,0:T(8,128)} %param.17) | copy-start | bytes 6148
  6.2 12.1 %copy-start.4 = (bf16[1,64,1024]{2,1,0:T(8,128)(2,1)S(1)}, bf16[1,64,1024]{2,1,0:T(8,128)(2,1)}, u32[]{:S(2)}) copy-start(bf16[1,64,1024]{2,1,0:T(8,128)(2,1)} %param.15) | copy-start | bytes 393220
  9.8 32.8 %all-to-all-start.3 = ((bf16[16,32,1024]{2,1,0:T(8,128)(2,1)}), bf16[16,32,1024]{2,1,0:T(8,128)(2,1)S(1)}, u32[]{:S(2)}, u32[]{:S(2)}) async-start(bf16[16,32,1024]{2,1,0:T(8,128)(2,1)} %bitcast.25), calls=%async_computation.3 | async-start | bytes 2097152 | tf_op jit(solution)/shard_map/all_to_all | solution.py:107
  42.5 28.9 %all-to-all-start.2 = ((bf16[16,32,1024]{2,1,0:T(8,128)(2,1)}), bf16[16,32,1024]{2,1,0:T(8,128)(2,1)}, u32[]{:S(2)}, u32[]{:S(2)}) async-start(bf16[16,32,1024]{2,1,0:T(8,128)(2,1)} %bitcast.22), calls=%async_computation.2 | async-start | bytes 2097152 | tf_op jit(solution)/shard_map/all_to_all | solution.py:108
  86.0 6.2 %copy-start.6 = (s32[1,64,8]{1,2,0:T(8,128)S(1)}, s32[1,64,8]{1,2,0:T(8,128)}, u32[]{:S(2)}) copy-start(s32[1,64,8]{1,2,0:T(8,128)} %param.12) | copy-start | bytes 6148
  86.0 8.1 %copy-start.2 = (bf16[1,64,1024]{2,1,0:T(8,128)(2,1)S(1)}, bf16[1,64,1024]{2,1,0:T(8,128)(2,1)}, u32[]{:S(2)}) copy-start(bf16[1,64,1024]{2,1,0:T(8,128)(2,1)} %param.11) | copy-start | bytes 393220
  86.0 29.0 %all-to-all-start.4 = ((bf16[16,32,1024]{2,1,0:T(8,128)(2,1)}), bf16[16,32,1024]{2,1,0:T(8,128)(2,1)S(1)}, u32[]{:S(2)}, u32[]{:S(2)}) async-start(bf16[16,32,1024]{2,1,0:T(8,128)(2,1)} %bitcast.146), calls=%async_computation.4 | async-start | bytes 2097152 | tf_op jit(solution)/shard_map/all_to_all | solution.py:113
  115.0 4.7 %copy-start.1 = (bf16[1,64,1024]{2,1,0:T(8,128)(2,1)S(1)}, bf16[1,64,1024]{2,1,0:T(8,128)(2,1)}, u32[]{:S(2)}) copy-start(bf16[1,64,1024]{2,1,0:T(8,128)(2,1)} %param.14) | copy-start | bytes 393220
  115.0 4.7 %copy-start.5 = (f32[1,1024]{1,0:T(1,128)S(1)}, f32[1,1024]{1,0:T(1,128)}, u32[]{:S(2)}) copy-start(f32[1,1024]{1,0:T(1,128)} %param.18) | copy-start | bytes 12292
  122.7 31.8 %copy-start.9 = (bf16[1,1,1024,768]{3,2,1,0:T(8,128)(2,1)S(1)}, bf16[1,1,1024,768]{3,2,1,0:T(8,128)(2,1)}, u32[]{:S(2)}) copy-start(bf16[1,1,1024,768]{3,2,1,0:T(8,128)(2,1)} %param.19) | copy-start | bytes 4718596
  153.5 1.0 copy-start.3
  162.1 4.0 %copy-start.8 = (f32[1,64,8]{1,2,0:T(8,128)S(1)}, f32[1,64,8]{1,2,0:T(8,128)}, u32[]{:S(2)}) copy-start(f32[1,64,8]{1,2,0:T(8,128)} %param.13) | copy-start | bytes 6148
  162.1 26.9 %all-to-all-start.1 = ((bf16[16,32,1024]{2,1,0:T(8,128)(2,1)}), bf16[16,32,1024]{2,1,0:T(8,128)(2,1)S(1)}, u32[]{:S(2)}, u32[]{:S(2)}) async-start(bf16[16,32,1024]{2,1,0:T(8,128)(2,1)} %bitcast.149), calls=%async_computation.1 | async-start | bytes 2097152 | tf_op jit(solution)/shard_map/all_to_all | solution.py:105
  166.4 27.4 %collective-permute-start.1 = (bf16[1,64,1024]{2,1,0:T(8,128)(2,1)S(1)}, bf16[1,64,1024]{2,1,0:T(8,128)(2,1)S(1)}, u32[]{:S(2)}, u32[]{:S(2)}) collective-permute-start(bf16[1,64,1024]{2,1,0:T(8,128)(2,1)S(1)} %fusion.54), channel_id=1, source_target_pairs={{16,0},{0,16},{17,1},{1,17},{18,2},{2,18},{19,3},{3,19},{20,4},{4,... | collective-permute-start | bytes 393224 | tf_op jit(solution)/shard_map/ppermute | solution.py:12
  193.8 1.4 collective-permute-start
where the time goes:
time: 198 us; the launch traced here: 197 us
  waiting for transfers between devices  84.6 us (43%)
  blocking collectives  30.8 us (16%)
  matrix products  25.8 us (13%)
  starting transfers between devices  24.5 us (12%)
  local copies, waits for them, and re-layouts  16.7 us (8%)
  other arithmetic  13.3 us (7%)
    all_to_all x1, blocking collectives, on_device(): lax.all_to_all(fwd_send, 'expert', split_axis=0, concat_axis=0, tiled=True)  30.8 us
    all_to_all x1, waiting for transfers between devices, on_device(): lax.all_to_all(fwd_result, 'expert', split_axis=0, concat_axis=0, tiled=T...  22.5 us
    all_to_all x1, waiting for transfers between devices, on_device(): lax.all_to_all(bwd_result, 'expert', split_axis=0, concat_axis=0, tiled=T...  20.7 us
    all_to_all x1, waiting for transfers between devices, on_device(): lax.all_to_all(bwd_rows, 'expert', split_axis=0, concat_axis=0, tiled=True)  20.6 us
    all_to_all x1, waiting for transfers between devices, on_device(): lax.all_to_all(bwd_grads, 'expert', split_axis=0, concat_axis=0, tiled=True)  19.5 us
    dot_general x3, matrix products, transposed(): lax.dot_general(left, right, (((1,), (1,)), ((), ())), preferred_element_...  14.6 us
    all_to_all x1, starting transfers between devices, on_device(): lax.all_to_all(bwd_rows, 'expert', split_axis=0, concat_axis=0, tiled=True)  8.31 us
    scatter x2, local copies, waits for them, and re-layouts, to_slots(): jnp.zeros((experts * capacity, width), values.dtype).at[target].set(values)  6.36 us
  transfers between devices with their start and end apart: 6, of which 5 were waited for; matrix products, arithmetic and copies ran while one was open for 7% of the time, Pallas kernels for 0%

commit v1 on v0

v1 whole, which is shorter than its diff:
```python
import functools

import jax
import jax.numpy as jnp
from jax import lax
from jax.experimental import pallas as pl
from jax.experimental.pallas import tpu as pltpu
from jax.sharding import PartitionSpec as P

EPSILON = 1e-06
BF16 = jnp.bfloat16
F32 = jnp.float32


def inner_size(experts):
    inner = 1
    while inner * inner * 4 <= experts and experts % (inner * 2) == 0:
        inner *= 2
    return inner


def partner(place, step, size, back=False):
    if size & (size - 1) == 0:
        return place ^ step
    return (place + (size - step if back else step)) % size


def over_outer(block, step, outer, inner):
    route = [
        (o * inner + i, partner(o, step, outer) * inner + i)
        for o in range(outer)
        for i in range(inner)
    ]
    return lax.ppermute(block, "expert", route)


def over_inner(block, step, outer, inner, back=False):
    route = [
        (o * inner + i, o * inner + partner(i, step, inner, back))
        for o in range(outer)
        for i in range(inner)
    ]
    return lax.ppermute(block, "expert", route)


def home_and_along(block, step, outer, inner, distance):
    segments = lax.axis_size("segment")
    experts = outer * inner
    route = [
        (
            s * experts + o * inner + i,
            (s + distance) % segments * experts + partner(o, step, outer, True) * inner + i,
        )
        for s in range(segments)
        for o in range(outer)
        for i in range(inner)
    ]
    return lax.ppermute(block, ("segment", "expert"), route)


def along(block, distance):
    segments = lax.axis_size("segment")
    return lax.ppermute(
        block, "segment", [(s, (s + distance) % segments) for s in range(segments)]
    )


def norm_scale(stream):
    return lax.rsqrt(jnp.mean(stream * stream, axis=-1, keepdims=True) + EPSILON)


def dot(left, right):
    return jnp.dot(left, right, preferred_element_type=F32)


def dot_nt(left, right):
    return lax.dot_general(left, right, (((1,), (1,)), ((), ())), preferred_element_type=F32)


def call(kernel, out_shape, args, scratch=(), smem=(), cost=None, limit=32 * 2**20):
    return pl.pallas_call(
        kernel,
        out_shape=out_shape,
        in_specs=[pl.BlockSpec(memory_space=pltpu.VMEM)] * len(args),
        out_specs=jax.tree.map(lambda _: pl.BlockSpec(memory_space=pltpu.VMEM), out_shape),
        scratch_shapes=list(scratch),
        compiler_params=pltpu.CompilerParams(vmem_limit_bytes=limit),
        cost_estimate=cost,
    )(*args)


def shape(*dims, dtype=BF16):
    return jax.ShapeDtypeStruct(dims, dtype)


def prepare_kernel(experts, fr, fg, br, bg, fx, bx, gain, info, fn, bn):
    tokens, width = info.shape
    lane = lax.broadcasted_iota(jnp.int32, (tokens, width), 1)
    gates = jnp.zeros((tokens, width), F32)
    chosen = jnp.zeros((tokens, width), jnp.bool_)
    for base, routes, values in ((0, fr, fg), (2 * experts, br, bg)):
        for k in range(routes.shape[1]):
            route = routes[:, k : k + 1]
            gates = jnp.where(lane == route + base, values[:, k : k + 1], gates)
            chosen = chosen | (lane == route + (base + experts))
    below = lax.broadcasted_iota(jnp.int32, (tokens, tokens), 1) < lax.broadcasted_iota(
        jnp.int32, (tokens, tokens), 0
    )
    rank = dot(below.astype(BF16), chosen.astype(F32).astype(BF16))
    is_slot = (lane // experts) % 2 == 1
    info[...] = jnp.where(is_slot, jnp.where(chosen, rank, -1.0), gates)
    for source, target in ((fx, fn), (bx, bn)):
        stream = source[...].astype(F32)
        target[...] = (stream * norm_scale(stream) * gain[...]).astype(BF16)


def prepare(experts, *args):
    tokens, width = args[4].shape
    lanes = -(-4 * experts // 128) * 128
    row = shape(tokens, width)
    return call(
        functools.partial(prepare_kernel, experts),
        (shape(tokens, lanes, dtype=F32), row, row),
        args,
    )


def my_expert(step, outer, inner):
    me = lax.axis_index("expert")
    o, i = me // inner, me % inner
    return o * inner + partner(i, step, inner)


def select_kernel(outer, inner, capacity, base, gated, *refs):
    infos, rows = refs[:outer], refs[outer : 2 * outer]
    outs, (flat, table) = refs[2 * outer : 2 * outer + inner], refs[2 * outer + inner :]
    experts = outer * inner
    tokens = rows[0].shape[0]
    total = outer * tokens
    for k in range(outer):
        flat[pl.ds(k * tokens, tokens), :] = rows[k][...]
        table[:, pl.ds(k * tokens, tokens)] = infos[k][...].T
    shift = lax.broadcasted_iota(jnp.int32, (1, total), 1) // tokens * capacity
    slots = outer * capacity
    place = lax.broadcasted_iota(jnp.int32, (slots, total), 0)
    for j in range(inner):
        expert = my_expert(j, outer, inner)
        rank = table[pl.ds(base + experts + expert, 1), :].astype(jnp.int32)
        slot = jnp.where(rank >= 0, rank + shift, -1)
        hit = (slot == place).astype(F32)
        picked = dot(hit.astype(BF16), flat[...])
        if gated:
            gate = table[pl.ds(base + expert, 1), :]
            picked = jnp.sum(hit * gate, axis=1, keepdims=True) * picked
        outs[j][...] = picked.astype(BF16)


def select(infos, rows, inner, capacity, base, gated):
    outer = len(rows)
    tokens, width = rows[0].shape
    lanes = infos[0].shape[1]
    return call(
        functools.partial(select_kernel, outer, inner, capacity, base, gated),
        [shape(outer * capacity, width)] * inner,
        (*infos, *rows),
        scratch=(
            pltpu.VMEM((outer * tokens, width), BF16),
            pltpu.VMEM((lanes, outer * tokens), F32),
        ),
    )


def chunks(size, want):
    step = want if size % want == 0 else size
    return [pl.ds(start, step) for start in range(0, size, step)]


def forward_kernel(inner, *refs):
    rows, (w_gate, w_up, w_down) = refs[:inner], refs[inner : inner + 3]
    outs, (flat, hidden) = refs[inner + 3 : 2 * inner + 3], refs[2 * inner + 3 :]
    count = rows[0].shape[0]
    for j in range(inner):
        flat[pl.ds(j * count, count), :] = rows[j][...]
    for part in chunks(w_gate.shape[1], 256):
        gate = dot(flat[...], w_gate[:, part])
        upward = dot(flat[...], w_up[:, part])
        hidden[:, part] = (gate * jax.nn.sigmoid(gate) * upward).astype(BF16)
    for part in chunks(w_down.shape[1], 256):
        result = dot(hidden[...], w_down[:, part]).astype(BF16)
        for j in range(inner):
            outs[j][:, part] = result[j * count : (j + 1) * count]


def expert_forward(rows, w_gate, w_up, w_down):
    inner = len(rows)
    count, width = rows[0].shape
    hidden = w_gate.shape[1]
    return call(
        functools.partial(forward_kernel, inner),
        [shape(count, width)] * inner,
        (*rows, w_gate, w_up, w_down),
        scratch=(
            pltpu.VMEM((inner * count, width), BF16),
            pltpu.VMEM((inner * count, hidden), BF16),
        ),
        cost=pl.CostEstimate(
            flops=6 * inner * count * width * hidden,
            bytes_accessed=6 * width * hidden + 4 * inner * count * width,
            transcendentals=inner * count * hidden,
        ),
    )


def backward_kernel(inner, *refs):
    rows, grads = refs[:inner], refs[inner : 2 * inner]
    w_gate, w_up, w_down = refs[2 * inner : 2 * inner + 3]
    outs, (flat, flat_grad, d_gate, d_up) = refs[2 * inner + 3 : 3 * inner + 3], refs[3 * inner + 3 :]
    count = rows[0].shape[0]
    for j in range(inner):
        flat[pl.ds(j * count, count), :] = rows[j][...]
        flat_grad[pl.ds(j * count, count), :] = grads[j][...]
    for part in chunks(w_gate.shape[1], 256):
        gate = dot(flat[...], w_gate[:, part])
        upward = dot(flat[...], w_up[:, part])
        d_hidden = dot_nt(flat_grad[...], w_down[part, :])
        sigma = jax.nn.sigmoid(gate)
        d_gate[:, part] = (d_hidden * upward * sigma * (1.0 + gate * (1.0 - sigma))).astype(BF16)
        d_up[:, part] = (d_hidden * gate * sigma).astype(BF16)
    for part in chunks(w_gate.shape[0], 256):
        result = dot_nt(d_gate[...], w_gate[part, :]) + dot_nt(d_up[...], w_up[part, :])
        result = result.astype(BF16)
        for j in range(inner):
            outs[j][:, part] = result[j * count : (j + 1) * count]


def expert_backward(rows, grads, w_gate, w_up, w_down):
    inner = len(rows)
    count, width = rows[0].shape
    hidden = w_gate.shape[1]
    return call(
        functools.partial(backward_kernel, inner),
        [shape(count, width)] * inner,
        (*rows, *grads, w_gate, w_up, w_down),
        scratch=[pltpu.VMEM((inner * count, width), BF16)] * 2
        + [pltpu.VMEM((inner * count, hidden), BF16)] * 2,
        cost=pl.CostEstimate(
            flops=10 * inner * count * width * hidden,
            bytes_accessed=6 * width * hidden + 6 * inner * count * width,
            transcendentals=inner * count * hidden,
        ),
    )


def combine_kernel(outer, inner, capacity, base, gated, *refs):
    infos, results = refs[:outer], refs[outer : outer + inner]
    outs, (flat,) = refs[outer + inner : 2 * outer + inner], refs[2 * outer + inner :]
    experts = outer * inner
    tokens, lanes = infos[0].shape
    total = outer * tokens
    slots = outer * capacity
    for k in range(outer):
        flat[pl.ds(k * tokens, tokens), :] = infos[k][...]
    lane = lax.broadcasted_iota(jnp.int32, (total, lanes), 1)
    shift = lax.broadcasted_iota(jnp.int32, (total, 1), 0) // tokens * capacity
    place = lax.broadcasted_iota(jnp.int32, (total, slots), 1)
    summed = None
    for j in range(inner):
        expert = my_expert(j, outer, inner)
        column = jnp.where(lane == base + experts + expert, flat[...], 0.0)
        rank = jnp.sum(column, axis=1, keepdims=True).astype(jnp.int32)
        slot = jnp.where(rank >= 0, rank + shift, -1)
        hit = (slot == place).astype(F32).astype(BF16)
        spread = dot(hit, results[j][...])
        if gated:
            column = jnp.where(lane == base + expert, flat[...], 0.0)
            spread = jnp.sum(column, axis=1, keepdims=True) * spread
        summed = spread if summed is None else summed + spread
    for k in range(outer):
        outs[k][...] = summed[k * tokens : (k + 1) * tokens].astype(BF16)


def combine(infos, results, capacity, base, gated):
    outer, inner = len(infos), len(results)
    tokens, lanes = infos[0].shape
    return call(
        functools.partial(combine_kernel, outer, inner, capacity, base, gated),
        [shape(tokens, results[0].shape[1])] * outer,
        (*infos, *results),
        scratch=(pltpu.VMEM((outer * tokens, lanes), F32),),
    )


def output_kernel(stream, *refs):
    out = refs[-1]
    total = stream[...].astype(F32)
    parts = refs[0][...].astype(F32)
    for part in refs[1:-1]:
        parts = parts + part[...].astype(F32)
    out[0] = (total + parts).astype(BF16)


def gradient_kernel(source, grad, gain, *refs):
    out = refs[-1]
    stream = source[...].astype(F32)
    scale = norm_scale(stream)
    parts = refs[0][...].astype(F32)
    for part in refs[1:-1]:
        parts = parts + part[...].astype(F32)
    summed = gain[...] * parts
    inner = jnp.mean(summed * stream, axis=-1, keepdims=True)
    out[0] = (
        grad[...].astype(F32) + scale * summed - stream * (scale * scale * scale * inner)
    ).astype(BF16)


def on_device(
    fwd_input,
    fwd_routes,
    fwd_gates,
    bwd_input,
    bwd_grad,
    bwd_routes,
    bwd_gates,
    norm_gain,
    w_gate,
    w_up,
    w_down,
):
    experts = lax.axis_size("expert")
    inner = inner_size(experts)
    outer = experts // inner
    tokens, width = fwd_input.shape[1:]
    capacity = min(tokens, tokens * fwd_routes.shape[2] // experts)
    fx, bx, grad = fwd_input[0], bwd_input[0], bwd_grad[0]
    weights = (w_gate[0, 0], w_up[0, 0], w_down[0, 0])

    def gathered(block):
        return [block] + [over_outer(block, k, outer, inner) for k in range(1, outer)]

    def exchanged(blocks, back=False):
        return [blocks[0]] + [
            over_inner(blocks[j], j, outer, inner, back) for j in range(1, inner)
        ]

    def returned(blocks, distance):
        return [
            home_and_along(blocks[k], k, outer, inner, distance) for k in range(outer)
        ]

    all_grad = gathered(grad)
    info, f_normed, b_normed = prepare(
        experts, fwd_routes[0], fwd_gates[0], bwd_routes[0], bwd_gates[0], fx, bx, norm_gain
    )
    infos = gathered(info)
    all_b = gathered(b_normed)
    all_f = gathered(f_normed)
    fx_next = along(fx, 1)
    bx_next, grad_next, gain_next = along(bx, -1), along(grad, -1), along(norm_gain, -1)

    b_base = 2 * experts
    grads = exchanged(select(infos, all_grad, inner, capacity, b_base, True))
    b_rows = exchanged(select(infos, all_b, inner, capacity, b_base, False))
    f_rows = exchanged(select(infos, all_f, inner, capacity, 0, False))
    b_back = exchanged(expert_backward(b_rows, grads, *weights), True)
    f_back = exchanged(expert_forward(f_rows, *weights), True)
    b_parts = returned(combine(infos, b_back, capacity, b_base, False), -1)
    f_parts = returned(combine(infos, f_back, capacity, 0, True), 1)
    out = shape(1, tokens, width)
    backward_next = call(gradient_kernel, out, (bx_next, grad_next, gain_next, *b_parts))
    forward_next = call(output_kernel, out, (fx_next, *f_parts))
    return (forward_next, backward_next)


def solution(mesh):
    placed = (
        P("segment", "expert", None),
        P("segment", "expert", None),
        P("segment", "expert", None),
        P("segment", "expert", None),
        P("segment", "expert", None),
        P("segment", "expert", None),
        P("segment", "expert", None),
        P("segment", None),
        P("segment", "expert", None, None),
        P("segment", "expert", None, None),
        P("segment", "expert", None, None),
    )
    return jax.shard_map(
        on_device,
        mesh=mesh,
        in_specs=placed,
        out_specs=(P("segment", "expert", None), P("segment", "expert", None)),
        check_vma=False,
    )
```

time: 198 us -> 123 us (0.62)
  the two profiles are of different devices: /device:TPU:0 before, /device:TPU:13 now
where the time goes in v1:
time: 123 us; the launch traced here: 122 us
  waiting for transfers between devices  59.4 us (48%)
  starting transfers between devices  41 us (33%)
  Pallas kernels  12.8 us (10%)
  local copies, waits for them, and re-layouts  8.45 us (7%)
    ppermute x15, waiting for transfers between devices, over_inner(): return lax.ppermute(block, 'expert', route)  22.5 us
    ppermute x12, waiting for transfers between devices, over_outer(): return lax.ppermute(block, 'expert', route)  20.5 us
    ppermute x8, waiting for transfers between devices, home_and_along(): return lax.ppermute(block, ('segment', 'expert'), route)  16.1 us
    ppermute x15, starting transfers between devices, over_inner(): return lax.ppermute(block, 'expert', route)  14.8 us
    pallas_call x10, Pallas kernels, call(): pl.pallas_call(kernel, out_shape=out_shape, in_specs=[pl.BlockSpec(memory...  12.8 us
    ppermute x12, starting transfers between devices, over_outer(): return lax.ppermute(block, 'expert', route)  11.6 us
    unnamed x24, local copies, waits for them, and re-layouts  8.45 us
    ppermute x8, starting transfers between devices, home_and_along(): return lax.ppermute(block, ('segment', 'expert'), route)  7.62 us
  transfers between devices with their start and end apart: 39, of which 13 were waited for; matrix products, arithmetic and copies ran while one was open for 0% of the time, Pallas kernels for 9%

profile of v1, /device:TPU:13, one launch (start us, length us, event | category | flops | bytes accessed | tf_op | source)
XLA Modules:
  0.0 122.5 jit_solution(17318673509239602583)
XLA Ops:
  7.1 2.3 %collective-permute-start.21 = (bf16[64,1024]{1,0:T(8,128)(2,1)S(1)}, bf16[64,1024]{1,0:T(8,128)(2,1)S(1)}, u32[]{:S(2)}, u32[]{:S(2)}) collective-permute-start(bf16[64,1024]{1,0:T(8,128)(2,1)S(1)} %get-tuple-element.47.refs_4_), channel_id=1, source_target_pairs={{0,8},{1,9},{2,10},{3,11},{4,12},{5,13},{6,14},{7,15},{8,0},{9,1},... | collective-permute-start | bytes 393224 | tf_op jit(solution)/shard_map/ppermute | solution.py:34
  9.4 1.3 %collective-permute-start.1 = (f32[64,128]{1,0:T(8,128)S(1)}, f32[64,128]{1,0:T(8,128)S(1)}, u32[]{:S(2)}, u32[]{:S(2)}) collective-permute-start(f32[64,128]{1,0:T(8,128)S(1)} %get-tuple-element.33.refs_0_), channel_id=1, source_target_pairs={{0,4},{1,5},{2,6},{3,7},{4,0},{5,1},{6,2},{7,3},{8,12},{9,13},{10,... | collective-permute-start | bytes 98312 | tf_op jit(solution)/shard_map/ppermute | solution.py:34
  12.0 3.0 %collective-permute-done.1.refs_1_ = f32[64,128]{1,0:T(8,128)S(1)} collective-permute-done((f32[64,128]{1,0:T(8,128)S(1)}, f32[64,128]{1,0:T(8,128)S(1)}, u32[]{:S(2)}, u32[]{:S(2)}) %collective-permute-start.1) | collective-permute-done | bytes 32800 | tf_op jit(solution)/shard_map/ppermute | solution.py:34
  19.5 2.1 %collective-permute-start.26 = (bf16[64,1024]{1,0:T(8,128)(2,1)}, bf16[64,1024]{1,0:T(8,128)(2,1)S(1)}, u32[]{:S(2)}, u32[]{:S(2)}) collective-permute-start(bf16[64,1024]{1,0:T(8,128)(2,1)} %bitcast.10), channel_id=1, source_target_pairs={{0,4},{1,5},{2,6},{3,7},{4,0},{5,1},{6,2},{7,3},{8,12},{9,13},{10,... | collective-permute-start | bytes 393224 | tf_op jit(solution)/shard_map/ppermute | solution.py:34
  21.7 5.2 %collective-permute-done.22.refs_7_ = bf16[64,1024]{1,0:T(8,128)(2,1)S(1)} collective-permute-done((bf16[64,1024]{1,0:T(8,128)(2,1)S(1)}, bf16[64,1024]{1,0:T(8,128)(2,1)S(1)}, u32[]{:S(2)}, u32[]{:S(2)}) %collective-permute-start.22) | collective-permute-done | bytes 131104 | tf_op jit(solution)/shard_map/ppermute | solution.py:34
  28.8 6.6 %collective-permute-done.6.refs_7_ = bf16[64,1024]{1,0:T(8,128)(2,1)S(1)} collective-permute-done((bf16[64,1024]{1,0:T(8,128)(2,1)S(1)}, bf16[64,1024]{1,0:T(8,128)(2,1)S(1)}, u32[]{:S(2)}, u32[]{:S(2)}) %collective-permute-start.6) | collective-permute-done | bytes 131104 | tf_op jit(solution)/shard_map/ppermute | solution.py:34
  37.3 1.5 %collective-permute-start.8 = (bf16[128,1024]{1,0:T(8,128)(2,1)S(1)}, bf16[128,1024]{1,0:T(8,128)(2,1)S(1)}, u32[]{:S(2)}, u32[]{:S(2)}) collective-permute-start(bf16[128,1024]{1,0:T(8,128)(2,1)S(1)} %get-tuple-element.37), channel_id=1, source_target_pairs={{0,2},{1,3},{2,0},{3,1},{4,6},{5,7},{6,4},{7,5},{8,10},{9,11},{10,... | collective-permute-start | bytes 786440 | tf_op jit(solution)/shard_map/ppermute | solution.py:43
  41.2 4.3 %collective-permute-done.28.refs_7_ = bf16[64,1024]{1,0:T(8,128)(2,1)S(1)} collective-permute-done((bf16[64,1024]{1,0:T(8,128)(2,1)S(1)}, bf16[64,1024]{1,0:T(8,128)(2,1)S(1)}, u32[]{:S(2)}, u32[]{:S(2)}) %collective-permute-start.28) | collective-permute-done | bytes 131104 | tf_op jit(solution)/shard_map/ppermute | solution.py:34
  45.4 1.5 %collective-permute-start.24 = (bf16[128,1024]{1,0:T(8,128)(2,1)S(1)}, bf16[128,1024]{1,0:T(8,128)(2,1)S(1)}, u32[]{:S(2)}, u32[]{:S(2)}) collective-permute-start(bf16[128,1024]{1,0:T(8,128)(2,1)S(1)} %get-tuple-element.50), channel_id=1, source_target_pairs={{0,2},{1,3},{2,0},{3,1},{4,6},{5,7},{6,4},{7,5},{8,10},{9,11},{10,... | collective-permute-start | bytes 786440 | tf_op jit(solution)/shard_map/ppermute | solution.py:43
  48.8 1.5 %collective-permute-start.30 = (bf16[128,1024]{1,0:T(8,128)(2,1)S(1)}, bf16[128,1024]{1,0:T(8,128)(2,1)S(1)}, u32[]{:S(2)}, u32[]{:S(2)}) collective-permute-start(bf16[128,1024]{1,0:T(8,128)(2,1)S(1)} %get-tuple-element.54), channel_id=1, source_target_pairs={{0,2},{1,3},{2,0},{3,1},{4,6},{5,7},{6,4},{7,5},{8,10},{9,11},{10,... | collective-permute-start | bytes 786440 | tf_op jit(solution)/shard_map/ppermute | solution.py:43
  50.4 1.4 %copy-done.8 = bf16[1,1,1024,768]{3,2,1,0:T(8,128)(2,1)S(1)} copy-done((bf16[1,1,1024,768]{3,2,1,0:T(8,128)(2,1)S(1)}, bf16[1,1,1024,768]{3,2,1,0:T(8,128)(2,1)}, u32[]{:S(2)}) %copy-start.8) | copy-done | bytes 1572888
  51.8 1.4 %copy-done.9 = bf16[1,1,768,1024]{3,2,1,0:T(8,128)(2,1)S(1)} copy-done((bf16[1,1,768,1024]{3,2,1,0:T(8,128)(2,1)S(1)}, bf16[1,1,768,1024]{3,2,1,0:T(8,128)(2,1)}, u32[]{:S(2)}) %copy-start.9) | copy-done | bytes 1572888
  53.2 2.6 %shard_map.124 = (bf16[128,1024]{1,0:T(8,128)(2,1)S(1)}, bf16[128,1024]{1,0:T(8,128)(2,1)S(1)}, bf16[128,1024]{1,0:T(8,128)(2,1)S(1)}, bf16[128,1024]{1,0:T(8,128)(2,1)S(1)}) custom-call(bf16[128,1024]{1,0:T(8,128)(2,1)S(1)} %get-tuple-element.35.refs_0_, bf16[128,1024]{1,0:T(8,128)(2,1)S(1)} %collective-permute-done.7.refs_1_, ...), custom_call_target="tpu_custom_call" | custom-call | flops 2415919104 | bytes 6815744 | tf_op jit(solution)/shard_map/pallas_call | solution.py:81
  55.8 9.6 %collective-permute-done.24.refs_2_ = bf16[128,1024]{1,0:T(8,128)(2,1)S(1)} collective-permute-done((bf16[128,1024]{1,0:T(8,128)(2,1)S(1)}, bf16[128,1024]{1,0:T(8,128)(2,1)S(1)}, u32[]{:S(2)}, u32[]{:S(2)}) %collective-permute-start.24) | collective-permute-done | bytes 262176 | tf_op jit(solution)/shard_map/ppermute | solution.py:43
  66.6 1.5 %collective-permute-start.12 = (bf16[128,1024]{1,0:T(8,128)(2,1)S(1)}, bf16[128,1024]{1,0:T(8,128)(2,1)S(1)}, u32[]{:S(2)}, u32[]{:S(2)}) collective-permute-start(bf16[128,1024]{1,0:T(8,128)(2,1)S(1)} %get-tuple-element.42), channel_id=1, source_target_pairs={{0,3},{1,2},{2,1},{3,0},{4,7},{5,6},{6,5},{7,4},{8,11},{9,10},{10,... | collective-permute-start | bytes 786440 | tf_op jit(solution)/shard_map/ppermute | solution.py:43
  68.1 8.7 %collective-permute-done.30.refs_6_ = bf16[128,1024]{1,0:T(8,128)(2,1)S(1)} collective-permute-done((bf16[128,1024]{1,0:T(8,128)(2,1)S(1)}, bf16[128,1024]{1,0:T(8,128)(2,1)S(1)}, u32[]{:S(2)}, u32[]{:S(2)}) %collective-permute-start.30) | collective-permute-done | bytes 262176 | tf_op jit(solution)/shard_map/ppermute | solution.py:43
  76.8 4.4 %shard_map.129 = (bf16[128,1024]{1,0:T(8,128)(2,1)S(1)}, bf16[128,1024]{1,0:T(8,128)(2,1)S(1)}, bf16[128,1024]{1,0:T(8,128)(2,1)S(1)}, bf16[128,1024]{1,0:T(8,128)(2,1)S(1)}) custom-call(bf16[128,1024]{1,0:T(8,128)(2,1)S(1)} %get-tuple-element.48.refs_0_, bf16[128,1024]{1,0:T(8,128)(2,1)S(1)} %collective-permute-done.23.refs_1_, ...), custom_call_target="tpu_custom_call" | custom-call | flops 4026531840 | bytes 7864320 | tf_op jit(solution)/shard_map/pallas_call | solution.py:81
  82.4 1.6 %collective-permute-start.34 = (bf16[128,1024]{1,0:T(8,128)(2,1)S(1)}, bf16[128,1024]{1,0:T(8,128)(2,1)S(1)}, u32[]{:S(2)}, u32[]{:S(2)}) collective-permute-start(bf16[128,1024]{1,0:T(8,128)(2,1)S(1)} %get-tuple-element.59), channel_id=1, source_target_pairs={{0,3},{1,2},{2,1},{3,0},{4,7},{5,6},{6,5},{7,4},{8,11},{9,10},{10,... | collective-permute-start | bytes 786440 | tf_op jit(solution)/shard_map/ppermute | solution.py:43
  85.2 6.7 %collective-permute-start.18 = (bf16[64,1024]{1,0:T(8,128)(2,1)S(1)}, bf16[64,1024]{1,0:T(8,128)(2,1)S(1)}, u32[]{:S(2)}, u32[]{:S(2)}) collective-permute-start(bf16[64,1024]{1,0:T(8,128)(2,1)S(1)} %bitcast.14), channel_id=1, source_target_pairs={{0,16},{16,0},{1,17},{17,1},{2,18},{18,2},{3,19},{19,3},{4,20},{20... | collective-permute-start | bytes 393224 | tf_op jit(solution)/shard_map/ppermute | solution.py:63
  93.6 2.9 %collective-permute-done.33.refs_6_ = bf16[128,1024]{1,0:T(8,128)(2,1)S(1)} collective-permute-done((bf16[128,1024]{1,0:T(8,128)(2,1)S(1)}, bf16[128,1024]{1,0:T(8,128)(2,1)S(1)}, u32[]{:S(2)}, u32[]{:S(2)}) %collective-permute-start.33) | collective-permute-done | bytes 262176 | tf_op jit(solution)/shard_map/ppermute | solution.py:43
  97.0 2.7 %collective-permute-start.16 = (bf16[64,1024]{1,0:T(8,128)(2,1)S(1)}, bf16[64,1024]{1,0:T(8,128)(2,1)S(1)}, u32[]{:S(2)}, u32[]{:S(2)}) collective-permute-start(bf16[64,1024]{1,0:T(8,128)(2,1)S(1)} %get-tuple-element.46), channel_id=1, source_target_pairs={{0,28},{1,29},{2,30},{3,31},{4,24},{5,25},{6,26},{7,27},{8,20},{9,... | collective-permute-start | bytes 393224 | tf_op jit(solution)/shard_map/ppermute | solution.py:58
  101.1 2.6 %collective-permute-start.36 = (bf16[64,1024]{1,0:T(8,128)(2,1)S(1)}, bf16[64,1024]{1,0:T(8,128)(2,1)S(1)}, u32[]{:S(2)}, u32[]{:S(2)}) collective-permute-start(bf16[64,1024]{1,0:T(8,128)(2,1)S(1)} %get-tuple-element.61), channel_id=1, source_target_pairs={{0,20},{1,21},{2,22},{3,23},{4,16},{5,17},{6,18},{7,19},{8,28},{9,... | collective-permute-start | bytes 393224 | tf_op jit(solution)/shard_map/ppermute | solution.py:58
  104.7 12.5 %collective-permute-done.16.refs_3_ = bf16[64,1024]{1,0:T(8,128)(2,1)S(1)} collective-permute-done((bf16[64,1024]{1,0:T(8,128)(2,1)S(1)}, bf16[64,1024]{1,0:T(8,128)(2,1)S(1)}, u32[]{:S(2)}, u32[]{:S(2)}) %collective-permute-start.16) | collective-permute-done | bytes 131104 | tf_op jit(solution)/shard_map/ppermute | solution.py:58
  118.0 3.6 %collective-permute-done.38.refs_3_ = bf16[64,1024]{1,0:T(8,128)(2,1)S(1)} collective-permute-done((bf16[64,1024]{1,0:T(8,128)(2,1)S(1)}, bf16[64,1024]{1,0:T(8,128)(2,1)S(1)}, u32[]{:S(2)}, u32[]{:S(2)}) %collective-permute-start.38) | collective-permute-done | bytes 131104 | tf_op jit(solution)/shard_map/ppermute | solution.py:58
  (88 shorter events, 30.3 us)
Async XLA Ops:
  6.9 12.3 %collective-permute-start.20 = (bf16[64,1024]{1,0:T(8,128)(2,1)S(1)}, bf16[64,1024]{1,0:T(8,128)(2,1)S(1)}, u32[]{:S(2)}, u32[]{:S(2)}) collective-permute-start(bf16[64,1024]{1,0:T(8,128)(2,1)S(1)} %get-tuple-element.47.refs_4_), channel_id=1, source_target_pairs={{0,4},{1,5},{2,6},{3,7},{4,0},{5,1},{6,2},{7,3},{8,12},{9,13},{10,... | collective-permute-start | bytes 393224 | tf_op jit(solution)/shard_map/ppermute | solution.py:34
  7.1 12.5 %collective-permute-start.21 = (bf16[64,1024]{1,0:T(8,128)(2,1)S(1)}, bf16[64,1024]{1,0:T(8,128)(2,1)S(1)}, u32[]{:S(2)}, u32[]{:S(2)}) collective-permute-start(bf16[64,1024]{1,0:T(8,128)(2,1)S(1)} %get-tuple-element.47.refs_4_), channel_id=1, source_target_pairs={{0,8},{1,9},{2,10},{3,11},{4,12},{5,13},{6,14},{7,15},{8,0},{9,1},... | collective-permute-start | bytes 393224 | tf_op jit(solution)/shard_map/ppermute | solution.py:34
  15.0 11.8 %collective-permute-start.22 = (bf16[64,1024]{1,0:T(8,128)(2,1)S(1)}, bf16[64,1024]{1,0:T(8,128)(2,1)S(1)}, u32[]{:S(2)}, u32[]{:S(2)}) collective-permute-start(bf16[64,1024]{1,0:T(8,128)(2,1)S(1)} %get-tuple-element.47.refs_4_), channel_id=1, source_target_pairs={{0,12},{1,13},{2,14},{3,15},{4,8},{5,9},{6,10},{7,11},{8,4},{9,5},... | collective-permute-start | bytes 393224 | tf_op jit(solution)/shard_map/ppermute | solution.py:34
  19.2 16.2 %collective-permute-start.6 = (bf16[64,1024]{1,0:T(8,128)(2,1)S(1)}, bf16[64,1024]{1,0:T(8,128)(2,1)S(1)}, u32[]{:S(2)}, u32[]{:S(2)}) collective-permute-start(bf16[64,1024]{1,0:T(8,128)(2,1)S(1)} %get-tuple-element.34.refs_4_), channel_id=1, source_target_pairs={{0,12},{1,13},{2,14},{3,15},{4,8},{5,9},{6,10},{7,11},{8,4},{9,5},... | collective-permute-start | bytes 393224 | tf_op jit(solution)/shard_map/ppermute | solution.py:34
  19.5 19.3 %collective-permute-start.26 = (bf16[64,1024]{1,0:T(8,128)(2,1)}, bf16[64,1024]{1,0:T(8,128)(2,1)S(1)}, u32[]{:S(2)}, u32[]{:S(2)}) collective-permute-start(bf16[64,1024]{1,0:T(8,128)(2,1)} %bitcast.10), channel_id=1, source_target_pairs={{0,4},{1,5},{2,6},{3,7},{4,0},{5,1},{6,2},{7,3},{8,12},{9,13},{10,... | collective-permute-start | bytes 393224 | tf_op jit(solution)/shard_map/ppermute | solution.py:34
  26.8 13.1 %collective-permute-start.27 = (bf16[64,1024]{1,0:T(8,128)(2,1)}, bf16[64,1024]{1,0:T(8,128)(2,1)S(1)}, u32[]{:S(2)}, u32[]{:S(2)}) collective-permute-start(bf16[64,1024]{1,0:T(8,128)(2,1)} %bitcast.11), channel_id=1, source_target_pairs={{0,8},{1,9},{2,10},{3,11},{4,12},{5,13},{6,14},{7,15},{8,0},{9,1},... | collective-permute-start | bytes 393224 | tf_op jit(solution)/shard_map/ppermute | solution.py:34
  27.5 20.1 %collective-permute-start.23 = (bf16[128,1024]{1,0:T(8,128)(2,1)S(1)}, bf16[128,1024]{1,0:T(8,128)(2,1)S(1)}, u32[]{:S(2)}, u32[]{:S(2)}) collective-permute-start(bf16[128,1024]{1,0:T(8,128)(2,1)S(1)} %get-tuple-element.49), channel_id=1, source_target_pairs={{0,1},{1,0},{2,3},{3,2},{4,5},{5,4},{6,7},{7,6},{8,9},{9,8},{10,11... | collective-permute-start | bytes 786440 | tf_op jit(solution)/shard_map/ppermute | solution.py:43
  36.0 11.6 %collective-permute-start.7 = (bf16[128,1024]{1,0:T(8,128)(2,1)S(1)}, bf16[128,1024]{1,0:T(8,128)(2,1)S(1)}, u32[]{:S(2)}, u32[]{:S(2)}) collective-permute-start(bf16[128,1024]{1,0:T(8,128)(2,1)S(1)} %get-tuple-element.36), channel_id=1, source_target_pairs={{0,1},{1,0},{2,3},{3,2},{4,5},{5,4},{6,7},{7,6},{8,9},{9,8},{10,11... | collective-permute-start | bytes 786440 | tf_op jit(solution)/shard_map/ppermute | solution.py:43
  45.4 20.0 %collective-permute-start.24 = (bf16[128,1024]{1,0:T(8,128)(2,1)S(1)}, bf16[128,1024]{1,0:T(8,128)(2,1)S(1)}, u32[]{:S(2)}, u32[]{:S(2)}) collective-permute-start(bf16[128,1024]{1,0:T(8,128)(2,1)S(1)} %get-tuple-element.50), channel_id=1, source_target_pairs={{0,2},{1,3},{2,0},{3,1},{4,6},{5,7},{6,4},{7,5},{8,10},{9,11},{10,... | collective-permute-start | bytes 786440 | tf_op jit(solution)/shard_map/ppermute | solution.py:43
  47.6 17.8 %collective-permute-start.25 = (bf16[128,1024]{1,0:T(8,128)(2,1)S(1)}, bf16[128,1024]{1,0:T(8,128)(2,1)S(1)}, u32[]{:S(2)}, u32[]{:S(2)}) collective-permute-start(bf16[128,1024]{1,0:T(8,128)(2,1)S(1)} %get-tuple-element.51), channel_id=1, source_target_pairs={{0,3},{1,2},{2,1},{3,0},{4,7},{5,6},{6,5},{7,4},{8,11},{9,10},{10,... | collective-permute-start | bytes 786440 | tf_op jit(solution)/shard_map/ppermute | solution.py:43
  47.7 18.9 %collective-permute-start.29 = (bf16[128,1024]{1,0:T(8,128)(2,1)S(1)}, bf16[128,1024]{1,0:T(8,128)(2,1)S(1)}, u32[]{:S(2)}, u32[]{:S(2)}) collective-permute-start(bf16[128,1024]{1,0:T(8,128)(2,1)S(1)} %get-tuple-element.53), channel_id=1, source_target_pairs={{0,1},{1,0},{2,3},{3,2},{4,5},{5,4},{6,7},{7,6},{8,9},{9,8},{10,11... | collective-permute-start | bytes 786440 | tf_op jit(solution)/shard_map/ppermute | solution.py:43
  48.8 28.0 %collective-permute-start.30 = (bf16[128,1024]{1,0:T(8,128)(2,1)S(1)}, bf16[128,1024]{1,0:T(8,128)(2,1)S(1)}, u32[]{:S(2)}, u32[]{:S(2)}) collective-permute-start(bf16[128,1024]{1,0:T(8,128)(2,1)S(1)} %get-tuple-element.54), channel_id=1, source_target_pairs={{0,2},{1,3},{2,0},{3,1},{4,6},{5,7},{6,4},{7,5},{8,10},{9,11},{10,... | collective-permute-start | bytes 786440 | tf_op jit(solution)/shard_map/ppermute | solution.py:43
  50.3 26.5 %collective-permute-start.31 = (bf16[128,1024]{1,0:T(8,128)(2,1)S(1)}, bf16[128,1024]{1,0:T(8,128)(2,1)S(1)}, u32[]{:S(2)}, u32[]{:S(2)}) collective-permute-start(bf16[128,1024]{1,0:T(8,128)(2,1)S(1)} %get-tuple-element.55), channel_id=1, source_target_pairs={{0,3},{1,2},{2,1},{3,0},{4,7},{5,6},{6,5},{7,4},{8,11},{9,10},{10,... | collective-permute-start | bytes 786440 | tf_op jit(solution)/shard_map/ppermute | solution.py:43
  65.4 16.9 %collective-permute-start.10 = (bf16[128,1024]{1,0:T(8,128)(2,1)S(1)}, bf16[128,1024]{1,0:T(8,128)(2,1)S(1)}, u32[]{:S(2)}, u32[]{:S(2)}) collective-permute-start(bf16[128,1024]{1,0:T(8,128)(2,1)S(1)} %get-tuple-element.40), channel_id=1, source_target_pairs={{0,1},{1,0},{2,3},{3,2},{4,5},{5,4},{6,7},{7,6},{8,9},{9,8},{10,11... | collective-permute-start | bytes 786440 | tf_op jit(solution)/shard_map/ppermute | solution.py:43
  65.4 19.8 %collective-permute-start.11 = (bf16[128,1024]{1,0:T(8,128)(2,1)S(1)}, bf16[128,1024]{1,0:T(8,128)(2,1)S(1)}, u32[]{:S(2)}, u32[]{:S(2)}) collective-permute-start(bf16[128,1024]{1,0:T(8,128)(2,1)S(1)} %get-tuple-element.41), channel_id=1, source_target_pairs={{0,2},{1,3},{2,0},{3,1},{4,6},{5,7},{6,4},{7,5},{8,10},{9,11},{10,... | collective-permute-start | bytes 786440 | tf_op jit(solution)/shard_map/ppermute | solution.py:43
  66.6 25.3 %collective-permute-start.12 = (bf16[128,1024]{1,0:T(8,128)(2,1)S(1)}, bf16[128,1024]{1,0:T(8,128)(2,1)S(1)}, u32[]{:S(2)}, u32[]{:S(2)}) collective-permute-start(bf16[128,1024]{1,0:T(8,128)(2,1)S(1)} %get-tuple-element.42), channel_id=1, source_target_pairs={{0,3},{1,2},{2,1},{3,0},{4,7},{5,6},{6,5},{7,4},{8,11},{9,10},{10,... | collective-permute-start | bytes 786440 | tf_op jit(solution)/shard_map/ppermute | solution.py:43
  81.2 12.3 %collective-permute-start.32 = (bf16[128,1024]{1,0:T(8,128)(2,1)S(1)}, bf16[128,1024]{1,0:T(8,128)(2,1)S(1)}, u32[]{:S(2)}, u32[]{:S(2)}) collective-permute-start(bf16[128,1024]{1,0:T(8,128)(2,1)S(1)} %get-tuple-element.57), channel_id=1, source_target_pairs={{0,1},{1,0},{2,3},{3,2},{4,5},{5,4},{6,7},{7,6},{8,9},{9,8},{10,11... | collective-permute-start | bytes 786440 | tf_op jit(solution)/shard_map/ppermute | solution.py:43
  81.3 15.1 %collective-permute-start.33 = (bf16[128,1024]{1,0:T(8,128)(2,1)S(1)}, bf16[128,1024]{1,0:T(8,128)(2,1)S(1)}, u32[]{:S(2)}, u32[]{:S(2)}) collective-permute-start(bf16[128,1024]{1,0:T(8,128)(2,1)S(1)} %get-tuple-element.58), channel_id=1, source_target_pairs={{0,2},{1,3},{2,0},{3,1},{4,6},{5,7},{6,4},{7,5},{8,10},{9,11},{10,... | collective-permute-start | bytes 786440 | tf_op jit(solution)/shard_map/ppermute | solution.py:43
  82.4 14.6 %collective-permute-start.34 = (bf16[128,1024]{1,0:T(8,128)(2,1)S(1)}, bf16[128,1024]{1,0:T(8,128)(2,1)S(1)}, u32[]{:S(2)}, u32[]{:S(2)}) collective-permute-start(bf16[128,1024]{1,0:T(8,128)(2,1)S(1)} %get-tuple-element.59), channel_id=1, source_target_pairs={{0,3},{1,2},{2,1},{3,0},{4,7},{5,6},{6,5},{7,4},{8,11},{9,10},{10,... | collective-permute-start | bytes 786440 | tf_op jit(solution)/shard_map/ppermute | solution.py:43
  97.0 20.2 %collective-permute-start.16 = (bf16[64,1024]{1,0:T(8,128)(2,1)S(1)}, bf16[64,1024]{1,0:T(8,128)(2,1)S(1)}, u32[]{:S(2)}, u32[]{:S(2)}) collective-permute-start(bf16[64,1024]{1,0:T(8,128)(2,1)S(1)} %get-tuple-element.46), channel_id=1, source_target_pairs={{0,28},{1,29},{2,30},{3,31},{4,24},{5,25},{6,26},{7,27},{8,20},{9,... | collective-permute-start | bytes 393224 | tf_op jit(solution)/shard_map/ppermute | solution.py:58
  100.5 17.5 %collective-permute-start.17 = (bf16[64,1024]{1,0:T(8,128)(2,1)S(1)}, bf16[64,1024]{1,0:T(8,128)(2,1)S(1)}, u32[]{:S(2)}, u32[]{:S(2)}) collective-permute-start(bf16[64,1024]{1,0:T(8,128)(2,1)S(1)} %bitcast.18), channel_id=1, source_target_pairs={{0,16},{16,0},{1,17},{17,1},{2,18},{18,2},{3,19},{19,3},{4,20},{20... | collective-permute-start | bytes 393224 | tf_op jit(solution)/shard_map/ppermute | solution.py:63
  100.6 17.4 %collective-permute-start.35 = (bf16[64,1024]{1,0:T(8,128)(2,1)S(1)}, bf16[64,1024]{1,0:T(8,128)(2,1)S(1)}, u32[]{:S(2)}, u32[]{:S(2)}) collective-permute-start(bf16[64,1024]{1,0:T(8,128)(2,1)S(1)} %get-tuple-element.60), channel_id=1, source_target_pairs={{0,16},{1,17},{2,18},{3,19},{4,20},{5,21},{6,22},{7,23},{8,24},{9,... | collective-permute-start | bytes 393224 | tf_op jit(solution)/shard_map/ppermute | solution.py:58
  101.1 16.9 %collective-permute-start.36 = (bf16[64,1024]{1,0:T(8,128)(2,1)S(1)}, bf16[64,1024]{1,0:T(8,128)(2,1)S(1)}, u32[]{:S(2)}, u32[]{:S(2)}) collective-permute-start(bf16[64,1024]{1,0:T(8,128)(2,1)S(1)} %get-tuple-element.61), channel_id=1, source_target_pairs={{0,20},{1,21},{2,22},{3,23},{4,16},{5,17},{6,18},{7,19},{8,28},{9,... | collective-permute-start | bytes 393224 | tf_op jit(solution)/shard_map/ppermute | solution.py:58
  103.7 14.3 %collective-permute-start.37 = (bf16[64,1024]{1,0:T(8,128)(2,1)S(1)}, bf16[64,1024]{1,0:T(8,128)(2,1)S(1)}, u32[]{:S(2)}, u32[]{:S(2)}) collective-permute-start(bf16[64,1024]{1,0:T(8,128)(2,1)S(1)} %get-tuple-element.62), channel_id=1, source_target_pairs={{0,24},{1,25},{2,26},{3,27},{4,28},{5,29},{6,30},{7,31},{8,16},{9,... | collective-permute-start | bytes 393224 | tf_op jit(solution)/shard_map/ppermute | solution.py:58
  (25 other events, 251.5 us)

commit v2 on v1

v2 whole, which is shorter than its diff:
```python
import functools

import jax
import jax.numpy as jnp
from jax import lax
from jax.experimental import pallas as pl
from jax.experimental.pallas import tpu as pltpu
from jax.sharding import PartitionSpec as P

EPSILON = 1e-06
BF16 = jnp.bfloat16
F32 = jnp.float32


def inner_size(experts):
    inner = 1
    while inner * inner * 4 <= experts and experts % (inner * 2) == 0:
        inner *= 2
    return inner


def partner(place, step, size, back=False):
    if size & (size - 1) == 0:
        return place ^ step
    return (place + (size - step if back else step)) % size


def over_outer(block, step, outer, inner):
    route = [
        (o * inner + i, partner(o, step, outer) * inner + i)
        for o in range(outer)
        for i in range(inner)
    ]
    return lax.ppermute(block, "expert", route)


def over_inner(block, step, outer, inner, back=False):
    route = [
        (o * inner + i, o * inner + partner(i, step, inner, back))
        for o in range(outer)
        for i in range(inner)
    ]
    return lax.ppermute(block, "expert", route)


def home_and_along(block, step, outer, inner, distance):
    segments = lax.axis_size("segment")
    experts = outer * inner
    route = [
        (
            s * experts + o * inner + i,
            (s + distance) % segments * experts + partner(o, step, outer, True) * inner + i,
        )
        for s in range(segments)
        for o in range(outer)
        for i in range(inner)
    ]
    return lax.ppermute(block, ("segment", "expert"), route)


def after(values, *others):
    return lax.optimization_barrier((values, others))[0]


def norm_scale(stream):
    return lax.rsqrt(jnp.mean(stream * stream, axis=-1, keepdims=True) + EPSILON)


def dot(left, right):
    return jnp.dot(left, right, preferred_element_type=F32)


def dot_nt(left, right):
    return lax.dot_general(left, right, (((1,), (1,)), ((), ())), preferred_element_type=F32)


def call(kernel, out_shape, args, far=(), scratch=(), cost=None, limit=16 * 2**20):
    near = pl.BlockSpec(memory_space=pltpu.VMEM)
    return pl.pallas_call(
        kernel,
        out_shape=out_shape,
        in_specs=[near] * len(args) + [pl.BlockSpec(memory_space=pltpu.HBM)] * len(far),
        out_specs=jax.tree.map(lambda _: near, out_shape),
        scratch_shapes=[
            *scratch,
            *(pltpu.VMEM(v.shape, v.dtype) for v in far),
            *([pltpu.SemaphoreType.DMA((len(far),))] if far else []),
        ],
        compiler_params=pltpu.CompilerParams(vmem_limit_bytes=limit),
        cost_estimate=cost or pl.CostEstimate(flops=2**31, bytes_accessed=2**22, transcendentals=0),
    )(*args, *far)


def fetches(sources, targets, semaphores):
    copies = [
        pltpu.make_async_copy(source, target, semaphores.at[i])
        for i, (source, target) in enumerate(zip(sources, targets))
    ]
    for copy in copies:
        copy.start()
    return copies


def shape(*dims, dtype=BF16):
    return jax.ShapeDtypeStruct(dims, dtype)


def my_expert(step, outer, inner):
    me = lax.axis_index("expert")
    o, i = me // inner, me % inner
    return o * inner + partner(i, step, inner)


def normed_rows(rows, gain):
    stream = rows.astype(F32)
    return (stream * norm_scale(stream) * gain).astype(BF16)


def fill_table(experts, table, lists):
    tokens = table.shape[1]
    row = lax.broadcasted_iota(jnp.int32, (experts, tokens), 0)
    before = lax.broadcasted_iota(jnp.int32, (tokens, tokens), 0) < lax.broadcasted_iota(
        jnp.int32, (tokens, tokens), 1
    )
    before = before.astype(F32).astype(BF16)
    for side, (routes, values) in enumerate((lists[:2], lists[2:])):
        rest = jnp.zeros((experts, tokens), F32)
        chosen = jnp.zeros((experts, tokens), jnp.bool_)
        for k in range(routes.shape[0]):
            here = row == routes[k : k + 1, :]
            rest = jnp.where(here, values[k : k + 1, :], rest)
            chosen = chosen | here
        base = 4 * experts * side
        for term in range(3):
            rounded = rest.astype(BF16).astype(F32)
            table[pl.ds(base + term * experts, experts), :] = rounded
            rest = rest - rounded
        rank = dot(chosen.astype(F32).astype(BF16), before)
        table[pl.ds(base + 3 * experts, experts), :] = jnp.where(chosen, rank, -1.0)


def picked(table, side, expert, experts, blocks, capacity):
    total = table.shape[1]
    shift = lax.broadcasted_iota(jnp.int32, (1, total), 1) // (total // blocks) * capacity
    place = lax.broadcasted_iota(jnp.int32, (blocks * capacity, total), 0)
    rank = table[pl.ds((4 * side + 3) * experts + expert, 1), :].astype(jnp.int32)
    return (jnp.where(rank >= 0, rank + shift, -1) == place).astype(F32)


def gate_of(table, side, expert, experts):
    terms = [table[pl.ds((4 * side + term) * experts + expert, 1), :] for term in range(3)]
    return terms[0] + terms[1] + terms[2]


def prepare_kernel(outer, inner, capacity, *refs):
    far, (f_pack, b_pack, home), own = refs[:8], refs[8:11], refs[11 : 11 + inner]
    table, *near, semaphores = refs[11 + inner :]
    experts = outer * inner
    copies = fetches(far, near, semaphores)
    lists, (fx, bx, grad, gain) = near[:4], near[4:]
    tokens, width = fx.shape
    for copy in copies:
        copy.wait()
    fill_table(experts, table, lists)
    f_pack[:, pl.ds(width, table.shape[0])] = table[...].T.astype(BF16)
    f_pack[:, pl.ds(0, width)] = normed_rows(fx[...], gain[...])
    b_pack[pl.ds(0, tokens), :] = normed_rows(bx[...], gain[...])
    b_pack[pl.ds(tokens, tokens), :] = grad[...]
    home[pl.ds(0, tokens), :] = bx[...]
    home[pl.ds(tokens, tokens), :] = grad[...]
    for j in range(inner):
        expert = my_expert(j, outer, inner)
        f_hit = picked(table, 0, expert, experts, 1, capacity).astype(BF16)
        b_hit = picked(table, 1, expert, experts, 1, capacity)
        gate = jnp.sum(b_hit * gate_of(table, 1, expert, experts), axis=1, keepdims=True)
        b_hit = b_hit.astype(BF16)
        own[j][pl.ds(0, capacity), :] = dot(f_hit, f_pack[:, pl.ds(0, width)]).astype(BF16)
        own[j][pl.ds(capacity, capacity), :] = dot(b_hit, b_pack[pl.ds(0, tokens), :]).astype(BF16)
        own[j][pl.ds(2 * capacity, capacity), :] = (gate * dot(b_hit, grad[...])).astype(BF16)


def prepare(outer, inner, capacity, *args):
    tokens, width = args[4].shape
    lanes = 8 * outer * inner
    return call(
        functools.partial(prepare_kernel, outer, inner, capacity),
        [shape(tokens, width + lanes), shape(2 * tokens, width), shape(2 * tokens, width)]
        + [shape(3 * capacity, width)] * inner,
        (),
        args,
        scratch=(pltpu.VMEM((lanes, tokens), F32),),
        limit=60 * 2**20,
    )


def select_kernel(outer, inner, capacity, side, blocks, *refs):
    experts = outer * inner
    packs, rows = refs[:blocks], refs[blocks : 2 * blocks]
    outs, (flat, table) = refs[2 * blocks : 2 * blocks + inner], refs[2 * blocks + inner :]
    tokens, width = packs[0].shape[0], flat.shape[1]
    total = blocks * tokens
    for k in range(blocks):
        table[:, pl.ds(k * tokens, tokens)] = packs[k][:, pl.ds(width, 8 * experts)].astype(F32).T
        for part in range(side + 1):
            flat[pl.ds(part * total + k * tokens, tokens), :] = rows[k][
                pl.ds(part * tokens, tokens), pl.ds(0, width)
            ]
    slots = blocks * capacity
    for j in range(inner):
        expert = my_expert(j, outer, inner)
        hit = picked(table, side, expert, experts, blocks, capacity)
        outs[j][pl.ds(0, slots), :] = dot(hit.astype(BF16), flat[pl.ds(0, total), :]).astype(BF16)
        if side == 1:
            gate = jnp.sum(hit * gate_of(table, 1, expert, experts), axis=1, keepdims=True)
            grads = dot(hit.astype(BF16), flat[pl.ds(total, total), :])
            outs[j][pl.ds(slots, slots), :] = (gate * grads).astype(BF16)


def select(packs, rows, width, outer, inner, capacity, side):
    blocks = len(rows)
    tokens = packs[0].shape[0]
    return call(
        functools.partial(select_kernel, outer, inner, capacity, side, blocks),
        [shape(blocks * capacity * (side + 1), width)] * inner,
        (*packs, *rows),
        scratch=(
            pltpu.VMEM((blocks * tokens * (side + 1), width), BF16),
            pltpu.VMEM((8 * outer * inner, blocks * tokens), F32),
        ),
    )


def chunks(size, want):
    step = want if size % want == 0 else size
    return [pl.ds(start, step) for start in range(0, size, step)]


def load_rows(flat, own, others, groups, capacity, part, parts):
    rest = others[0].shape[0] // parts
    first = 0 if parts == 1 else part + 1
    at = 0
    for j, k in [(j, k) for group in groups for j in range(len(own)) for k in group]:
        if k == 0:
            rows = own[j][pl.ds(first * capacity, capacity), :]
        else:
            rows = others[j][pl.ds(part * rest + (k - 1) * capacity, capacity), :]
        flat[pl.ds(at, capacity), :] = rows
        at += capacity


def forward_kernel(inner, blocks, capacity, *refs):
    own, others, (w_gate, w_up, w_down) = (
        refs[:inner],
        refs[inner : 2 * inner],
        refs[2 * inner : 2 * inner + 3],
    )
    outs, (flat, hidden) = refs[2 * inner + 3 : 3 * inner + 3], refs[3 * inner + 3 :]
    load_rows(flat, own, others, (blocks,), capacity, 0, 1)
    for part in chunks(w_gate.shape[1], 256):
        gate = dot(flat[...], w_gate[:, part])
        upward = dot(flat[...], w_up[:, part])
        hidden[:, part] = (gate * jax.nn.sigmoid(gate) * upward).astype(BF16)
    count = outs[0].shape[0]
    for part in chunks(w_down.shape[1], 256):
        result = dot(hidden[...], w_down[:, part]).astype(BF16)
        for j in range(inner):
            outs[j][:, part] = result[j * count : (j + 1) * count]


def expert_forward(own, others, weights, blocks, capacity):
    inner = len(own)
    count = len(blocks) * capacity
    width, hidden = weights[0].shape
    return call(
        functools.partial(forward_kernel, inner, blocks, capacity),
        [shape(count, width)] * inner,
        (*own, *others, *weights),
        scratch=(
            pltpu.VMEM((inner * count, width), BF16),
            pltpu.VMEM((inner * count, hidden), BF16),
        ),
        cost=pl.CostEstimate(
            flops=6 * inner * count * width * hidden,
            bytes_accessed=6 * width * hidden + 4 * inner * count * width,
            transcendentals=inner * count * hidden,
        ),
    )


def backward_kernel(inner, groups, capacity, *refs):
    own, others, (w_gate, w_up, w_down) = (
        refs[:inner],
        refs[inner : 2 * inner],
        refs[2 * inner : 2 * inner + 3],
    )
    outs, (flat, flat_grad, d_gate, d_up) = refs[2 * inner + 3 : -4], refs[-4:]
    load_rows(flat, own, others, groups, capacity, 0, 2)
    load_rows(flat_grad, own, others, groups, capacity, 1, 2)
    for part in chunks(w_gate.shape[1], 256):
        gate = dot(flat[...], w_gate[:, part])
        upward = dot(flat[...], w_up[:, part])
        d_hidden = dot_nt(flat_grad[...], w_down[part, :])
        sigma = jax.nn.sigmoid(gate)
        d_gate[:, part] = (d_hidden * upward * sigma * (1.0 + gate * (1.0 - sigma))).astype(BF16)
        d_up[:, part] = (d_hidden * gate * sigma).astype(BF16)
    for part in chunks(w_gate.shape[0], 256):
        result = dot_nt(d_gate[...], w_gate[part, :]) + dot_nt(d_up[...], w_up[part, :])
        result = result.astype(BF16)
        at = 0
        for out in outs:
            out[:, part] = result[at : at + out.shape[0]]
            at += out.shape[0]


def expert_backward(own, others, weights, groups, capacity):
    inner = len(own)
    count = sum(len(group) for group in groups) * capacity
    width, hidden = weights[0].shape
    outs = call(
        functools.partial(backward_kernel, inner, groups, capacity),
        [shape(len(group) * capacity, width) for group in groups for _ in range(inner)],
        (*own, *others, *weights),
        scratch=[pltpu.VMEM((inner * count, width), BF16)] * 2
        + [pltpu.VMEM((inner * count, hidden), BF16)] * 2,
        cost=pl.CostEstimate(
            flops=10 * inner * count * width * hidden,
            bytes_accessed=6 * width * hidden + 6 * inner * count * width,
            transcendentals=inner * count * hidden,
        ),
    )
    return outs[:inner], outs[inner:]


def combine_kernel(blocks, experts, inner, capacity, side, *refs):
    packs, results = refs[:blocks], refs[blocks : blocks + inner]
    gain, home = refs[blocks + inner : blocks + inner + 2]
    outs, flat = refs[blocks + inner + 2 : -1], refs[-1]
    tokens, lanes = packs[0].shape[0], flat.shape[1]
    width = packs[0].shape[1] - lanes
    total = blocks * tokens
    slots = blocks * capacity
    for k in range(blocks):
        flat[pl.ds(k * tokens, tokens), :] = packs[k][:, pl.ds(width, lanes)].astype(F32)
    lane = lax.broadcasted_iota(jnp.int32, (total, lanes), 1)
    shift = lax.broadcasted_iota(jnp.int32, (total, 1), 0) // tokens * capacity
    place = lax.broadcasted_iota(jnp.int32, (total, slots), 1)
    summed = None
    for j in range(inner):
        first = 4 * experts * side + my_expert(j, experts // inner, inner)
        column = jnp.where(lane == first + 3 * experts, flat[...], 0.0)
        rank = jnp.sum(column, axis=1, keepdims=True).astype(jnp.int32)
        slot = jnp.where(rank >= 0, rank + shift, -1)
        hit = (slot == place).astype(F32).astype(BF16)
        spread = dot(hit, results[j][...])
        if side == 0:
            terms = (lane == first) | (lane == first + experts) | (lane == first + 2 * experts)
            column = jnp.where(terms, flat[...], 0.0)
            spread = jnp.sum(column, axis=1, keepdims=True) * spread
        summed = spread if summed is None else summed + spread
    if side == 1:
        summed = gain[...] * summed
    for k in range(blocks):
        part = summed[k * tokens : (k + 1) * tokens]
        if outs[k].dtype == F32:
            outs[k][...] = home[...].astype(F32) + part
        else:
            outs[k][pl.ds(0, tokens), :] = part.astype(BF16)
            if outs[k].shape[0] > tokens:
                outs[k][pl.ds(tokens, 2 * tokens), :] = home[...]


def combine(packs, results, gain, home, steps, inner, capacity, side):
    packs = [packs[k] for k in steps]
    blocks = len(packs)
    tokens, width = packs[0].shape[0], results[0].shape[1]
    lanes = packs[0].shape[1] - width
    local = shape(3 * tokens, width) if side == 1 else shape(tokens, width, dtype=F32)
    return call(
        functools.partial(combine_kernel, blocks, lanes // 8, inner, capacity, side),
        [shape(tokens, width) if k else local for k in steps],
        (*packs, *results, gain, home),
        scratch=(pltpu.VMEM((blocks * tokens, lanes), F32),),
    )


def output_kernel(*refs):
    total = refs[-2][...]
    for part in refs[:-2]:
        total = total + part[...].astype(F32)
    refs[-1][0] = total.astype(BF16)


def gradient_kernel(*refs):
    local, out = refs[-2:]
    tokens = out.shape[1]
    summed, stream, grad = (
        local[pl.ds(i * tokens, tokens), :].astype(F32) for i in range(3)
    )
    scale = norm_scale(stream)
    for part in refs[:-2]:
        summed = summed + part[...].astype(F32)
    inner = jnp.mean(summed * stream, axis=-1, keepdims=True)
    out[0] = (grad + scale * summed - stream * (scale * scale * scale * inner)).astype(BF16)


def on_device(
    fwd_input,
    fwd_routes,
    fwd_gates,
    bwd_input,
    bwd_grad,
    bwd_routes,
    bwd_gates,
    norm_gain,
    w_gate,
    w_up,
    w_down,
):
    experts = lax.axis_size("expert")
    inner = inner_size(experts)
    outer = experts // inner
    tokens, width = fwd_input.shape[1:]
    capacity = min(tokens, tokens * fwd_routes.shape[2] // experts)
    fx, bx, grad = fwd_input[0], bwd_input[0], bwd_grad[0]
    weights = (w_gate[0, 0], w_up[0, 0], w_down[0, 0])

    def spread(block):
        return [over_outer(block, k, outer, inner) for k in range(1, outer)]

    def exchanged(blocks, back=False):
        return [blocks[0]] + [
            over_inner(blocks[j], j, outer, inner, back) for j in range(1, inner)
        ]

    def returned(blocks, steps, distance):
        return [
            home_and_along(block, k, outer, inner, distance) for k, block in zip(steps, blocks)
        ]

    lists = [v[0].T for v in (fwd_routes, fwd_gates, bwd_routes, bwd_gates)]
    f_pack, b_pack, home, *own = prepare(
        outer, inner, capacity, *lists, fx, bx, grad, norm_gain
    )
    f_away = spread(f_pack)
    own = exchanged(own)
    b_away = spread(after(b_pack, f_away[0]))

    sizes = (width, outer, inner, capacity)
    f_rows = exchanged(select(f_away, f_away, *sizes, 0))
    every = (*range(1, outer), 0)
    f_back = exchanged(expert_forward(own, f_rows, weights, every, capacity), True)
    b_away, f_back = after((b_away, f_back))
    b_picked = select(f_away, b_away, *sizes, 1)
    b_rows = exchanged(b_picked)
    packs = [f_pack] + f_away
    f_sums = combine(packs, after(f_back, b_picked[0]), norm_gain, fx, every, inner, capacity, 0)
    f_parts = returned(f_sums, every, 1)
    b_rows = after(b_rows, f_parts)
    half = outer // 2
    groups = ((half,), (*range(1, half), *range(half + 1, outer), 0))
    first, last = expert_backward(own, b_rows, weights, groups, capacity)
    b_back = exchanged(first, True)
    out = shape(1, tokens, width)
    forward_next = call(output_kernel, out, f_parts)
    b_back = after(b_back, forward_next)
    b_sums = combine(packs, b_back, norm_gain, home, groups[0], inner, capacity, 1)
    b_parts = returned(b_sums, groups[0], -1)
    b_last = after(exchanged(after(last, b_sums[0]), True), b_parts[0])
    b_sums = combine(packs, b_last, norm_gain, home, groups[1], inner, capacity, 1)
    b_parts += returned(b_sums, groups[1], -1)
    backward_next = call(gradient_kernel, out, b_parts)
    return (forward_next, backward_next)


def solution(mesh):
    placed = (
        P("segment", "expert", None),
        P("segment", "expert", None),
        P("segment", "expert", None),
        P("segment", "expert", None),
        P("segment", "expert", None),
        P("segment", "expert", None),
        P("segment", "expert", None),
        P("segment", None),
        P("segment", "expert", None, None),
        P("segment", "expert", None, None),
        P("segment", "expert", None, None),
    )
    return jax.shard_map(
        on_device,
        mesh=mesh,
        in_specs=placed,
        out_specs=(P("segment", "expert", None), P("segment", "expert", None)),
        check_vma=False,
    )
```

time: 123 us -> 105 us (0.85)
  the two profiles are of different devices: /device:TPU:13 before, /device:TPU:0 now
where the time goes in v2:
time: 105 us; the launch traced here: 104 us
  starting transfers between devices  49.9 us (48%)
  waiting for transfers between devices  39.1 us (37%)
  Pallas kernels  14.3 us (14%)
    ppermute x18, starting transfers between devices, over_inner(): return lax.ppermute(block, 'expert', route)  23.6 us
    ppermute x8, waiting for transfers between devices, home_and_along(): return lax.ppermute(block, ('segment', 'expert'), route)  18.7 us
    ppermute x6, waiting for transfers between devices, over_outer(): return lax.ppermute(block, 'expert', route)  14.6 us
    pallas_call x10, Pallas kernels, call(): pl.pallas_call(kernel, out_shape=out_shape, in_specs=[near] * len(args) +...  14.3 us
    ppermute x8, starting transfers between devices, home_and_along(): return lax.ppermute(block, ('segment', 'expert'), route)  13.7 us
    ppermute x6, starting transfers between devices, over_outer(): return lax.ppermute(block, 'expert', route)  12.6 us
    ppermute x18, waiting for transfers between devices, over_inner(): return lax.ppermute(block, 'expert', route)  5.85 us
  transfers between devices with their start and end apart: 32, of which 13 were waited for; matrix products, arithmetic and copies ran while one was open for 0% of the time, Pallas kernels for 4%

profile of v2, /device:TPU:0, one launch (start us, length us, event | category | flops | bytes accessed | tf_op | source)
XLA Modules:
  0.0 104.4 jit_solution(6468343764098467084)
XLA Ops:
  0.6 2.7 %shard_map.122 = (bf16[64,1152]{1,0:T(8,128)(2,1)}, bf16[128,1024]{1,0:T(8,128)(2,1)}, bf16[128,1024]{1,0:T(8,128)(2,1)}, bf16[96,1024]{1,0:T(8,128)(2,1)}, bf16...) custom-call(s32[8,64]{1,0:T(8,128)} %bitcast.28, f32[8,64]{1,0:T(8,128)} %bitcast.29, ...), custom_call_target="tpu_custom_call" | custom-call | flops 2147483648 | bytes 4194304 | tf_op jit(solution)/shard_map/pallas_call | solution.py:79
  3.3 5.1 %collective-permute-start.2 = (bf16[64,1152]{1,0:T(8,128)(2,1)}, bf16[64,1152]{1,0:T(8,128)(2,1)S(1)}, u32[]{:S(2)}, u32[]{:S(2)}) collective-permute-start(bf16[64,1152]{1,0:T(8,128)(2,1)} %get-tuple-element.64.refs_3_.refs_2_), channel_id=1, source_target_pairs={{0,12},{1,13},{2,14},{3,15},{4,8},{5,9},{6,10},{7,11},{8,4},{9,5},... | collective-permute-start | bytes 442376 | tf_op jit(solution)/shard_map/ppermute | solution.py:34
  9.0 1.6 %collective-permute-start.6 = (bf16[96,1024]{1,0:T(8,128)(2,1)}, bf16[96,1024]{1,0:T(8,128)(2,1)S(1)}, u32[]{:S(2)}, u32[]{:S(2)}) collective-permute-start(bf16[96,1024]{1,0:T(8,128)(2,1)} %get-tuple-element.68), channel_id=1, source_target_pairs={{0,1},{1,0},{2,3},{3,2},{4,5},{5,4},{6,7},{7,6},{8,9},{9,8},{10,11... | collective-permute-start | bytes 589832 | tf_op jit(solution)/shard_map/ppermute | solution.py:43
  13.4 2.7 %collective-permute-start.8 = (bf16[96,1024]{1,0:T(8,128)(2,1)}, bf16[96,1024]{1,0:T(8,128)(2,1)S(1)}, u32[]{:S(2)}, u32[]{:S(2)}) collective-permute-start(bf16[96,1024]{1,0:T(8,128)(2,1)} %get-tuple-element.70), channel_id=1, source_target_pairs={{0,3},{1,2},{2,1},{3,0},{4,7},{5,6},{6,5},{7,4},{8,11},{9,10},{10,... | collective-permute-start | bytes 589832 | tf_op jit(solution)/shard_map/ppermute | solution.py:43
  16.1 5.0 %collective-permute-done.1.refs_1_.refs_4_.refs_0_ = bf16[64,1152]{1,0:T(8,128)(2,1)S(1)} collective-permute-done((bf16[64,1152]{1,0:T(8,128)(2,1)}, bf16[64,1152]{1,0:T(8,128)(2,1)S(1)}, u32[]{:S(2)}, u32[]{:S(2)}) %collective-permute-start.1) | collective-permute-done | bytes 147488 | tf_op jit(solution)/shard_map/ppermute | solution.py:34
  21.6 1.6 %collective-permute-start.9 = (bf16[96,1024]{1,0:T(8,128)(2,1)S(1)}, bf16[96,1024]{1,0:T(8,128)(2,1)S(1)}, u32[]{:S(2)}, u32[]{:S(2)}) collective-permute-start(bf16[96,1024]{1,0:T(8,128)(2,1)S(1)} %get-tuple-element.72), channel_id=1, source_target_pairs={{0,1},{1,0},{2,3},{3,2},{4,5},{5,4},{6,7},{7,6},{8,9},{9,8},{10,11... | collective-permute-start | bytes 589832 | tf_op jit(solution)/shard_map/ppermute | solution.py:43
  25.2 2.5 %collective-permute-start.5 = (bf16[128,1024]{1,0:T(8,128)(2,1)S(1)}, bf16[128,1024]{1,0:T(8,128)(2,1)S(1)}, u32[]{:S(2)}, u32[]{:S(2)}) collective-permute-start(bf16[128,1024]{1,0:T(8,128)(2,1)S(1)} %copy-done.8), channel_id=1, source_target_pairs={{0,12},{1,13},{2,14},{3,15},{4,8},{5,9},{6,10},{7,11},{8,4},{9,5},... | collective-permute-start | bytes 786440 | tf_op jit(solution)/shard_map/ppermute | solution.py:34
  27.7 2.1 %collective-permute-start.4 = (bf16[128,1024]{1,0:T(8,128)(2,1)S(1)}, bf16[128,1024]{1,0:T(8,128)(2,1)S(1)}, u32[]{:S(2)}, u32[]{:S(2)}) collective-permute-start(bf16[128,1024]{1,0:T(8,128)(2,1)S(1)} %copy-done.8), channel_id=1, source_target_pairs={{0,8},{1,9},{2,10},{3,11},{4,12},{5,13},{6,14},{7,15},{8,0},{9,1},... | collective-permute-start | bytes 786440 | tf_op jit(solution)/shard_map/ppermute | solution.py:34
  29.8 2.2 %collective-permute-start.3 = (bf16[128,1024]{1,0:T(8,128)(2,1)S(1)}, bf16[128,1024]{1,0:T(8,128)(2,1)S(1)}, u32[]{:S(2)}, u32[]{:S(2)}) collective-permute-start(bf16[128,1024]{1,0:T(8,128)(2,1)S(1)} %copy-done.8), channel_id=1, source_target_pairs={{0,4},{1,5},{2,6},{3,7},{4,0},{5,1},{6,2},{7,3},{8,12},{9,13},{10,... | collective-permute-start | bytes 786440 | tf_op jit(solution)/shard_map/ppermute | solution.py:34
  33.1 2.6 %shard_map.124 = (bf16[128,1024]{1,0:T(8,128)(2,1)S(1)}, bf16[128,1024]{1,0:T(8,128)(2,1)S(1)}, bf16[128,1024]{1,0:T(8,128)(2,1)S(1)}, bf16[128,1024]{1,0:T(8,128)(2,1)S(1)}) custom-call(bf16[96,1024]{1,0:T(8,128)(2,1)S(1)} %copy-done.6, bf16[96,1024]{1,0:T(8,128)(2,1)S(1)} %collective-permute-done.6.refs_1_, ...), custom_call_target="tpu_custom_call" | custom-call | flops 2415919104 | bytes 6815744 | tf_op jit(solution)/shard_map/pallas_call | solution.py:79
  39.3 8.4 %collective-permute-done.4.refs_4_ = bf16[128,1024]{1,0:T(8,128)(2,1)S(1)} collective-permute-done((bf16[128,1024]{1,0:T(8,128)(2,1)S(1)}, bf16[128,1024]{1,0:T(8,128)(2,1)S(1)}, u32[]{:S(2)}, u32[]{:S(2)}) %collective-permute-start.4) | collective-permute-done | bytes 262176 | tf_op jit(solution)/shard_map/ppermute | solution.py:34
  54.2 1.5 %collective-permute-start.16 = (bf16[64,1024]{1,0:T(8,128)(2,1)S(1)}, bf16[64,1024]{1,0:T(8,128)(2,1)S(1)}, u32[]{:S(2)}, u32[]{:S(2)}) collective-permute-start(bf16[64,1024]{1,0:T(8,128)(2,1)S(1)} %get-tuple-element.92), channel_id=1, source_target_pairs={{0,24},{1,25},{2,26},{3,27},{4,28},{5,29},{6,30},{7,31},{8,16},{9,... | collective-permute-start | bytes 393224 | tf_op jit(solution)/shard_map/ppermute | solution.py:58
  55.7 3.3 %collective-permute-start.18 = (f32[64,1024]{1,0:T(8,128)S(1)}, f32[64,1024]{1,0:T(8,128)S(1)}, u32[]{:S(2)}, u32[]{:S(2)}) collective-permute-start(f32[64,1024]{1,0:T(8,128)S(1)} %get-tuple-element.94), channel_id=1, source_target_pairs={{0,16},{1,17},{2,18},{3,19},{4,20},{5,21},{6,22},{7,23},{8,24},{9,... | collective-permute-start | bytes 786440 | tf_op jit(solution)/shard_map/ppermute | solution.py:58
  59.0 1.9 %collective-permute-done.16.refs_1_ = bf16[64,1024]{1,0:T(8,128)(2,1)S(1)} collective-permute-done((bf16[64,1024]{1,0:T(8,128)(2,1)S(1)}, bf16[64,1024]{1,0:T(8,128)(2,1)S(1)}, u32[]{:S(2)}, u32[]{:S(2)}) %collective-permute-start.16) | collective-permute-done | bytes 131104 | tf_op jit(solution)/shard_map/ppermute | solution.py:58
  60.9 5.2 %collective-permute-start.17 = (bf16[64,1024]{1,0:T(8,128)(2,1)S(1)}, bf16[64,1024]{1,0:T(8,128)(2,1)S(1)}, u32[]{:S(2)}, u32[]{:S(2)}) collective-permute-start(bf16[64,1024]{1,0:T(8,128)(2,1)S(1)} %get-tuple-element.93), channel_id=1, source_target_pairs={{0,28},{1,29},{2,30},{3,31},{4,24},{5,25},{6,26},{7,27},{8,20},{9,... | collective-permute-start | bytes 393224 | tf_op jit(solution)/shard_map/ppermute | solution.py:58
  66.2 2.8 %collective-permute-done.17.refs_2_ = bf16[64,1024]{1,0:T(8,128)(2,1)S(1)} collective-permute-done((bf16[64,1024]{1,0:T(8,128)(2,1)S(1)}, bf16[64,1024]{1,0:T(8,128)(2,1)S(1)}, u32[]{:S(2)}, u32[]{:S(2)}) %collective-permute-start.17) | collective-permute-done | bytes 131104 | tf_op jit(solution)/shard_map/ppermute | solution.py:58
  69.0 4.4 %shard_map.128 = (bf16[32,1024]{1,0:T(8,128)(2,1)S(1)}, bf16[32,1024]{1,0:T(8,128)(2,1)S(1)}, bf16[32,1024]{1,0:T(8,128)(2,1)S(1)}, bf16[32,1024]{1,0:T(8,128)(2...) custom-call(bf16[96,1024]{1,0:T(8,128)(2,1)S(1)} %copy-done.6, ...), custom_call_target="tpu_custom_call" | custom-call | flops 4026531840 | bytes 7864320 | tf_op jit(solution)/shard_map/pallas_call | solution.py:79
  73.4 1.5 %collective-permute-start.22 = (bf16[32,1024]{1,0:T(8,128)(2,1)S(1)}, bf16[32,1024]{1,0:T(8,128)(2,1)S(1)}, u32[]{:S(2)}, u32[]{:S(2)}) collective-permute-start(bf16[32,1024]{1,0:T(8,128)(2,1)S(1)} %get-tuple-element.103), channel_id=1, source_target_pairs={{0,1},{1,0},{2,3},{3,2},{4,5},{5,4},{6,7},{7,6},{8,9},{9,8},{10,11... | collective-permute-start | bytes 196616 | tf_op jit(solution)/shard_map/ppermute | solution.py:43
  79.2 1.9 %collective-permute-done.24.refs_4_ = bf16[32,1024]{1,0:T(8,128)(2,1)S(1)} collective-permute-done((bf16[32,1024]{1,0:T(8,128)(2,1)S(1)}, bf16[32,1024]{1,0:T(8,128)(2,1)S(1)}, u32[]{:S(2)}, u32[]{:S(2)}) %collective-permute-start.24) | collective-permute-done | bytes 65568 | tf_op jit(solution)/shard_map/ppermute | solution.py:43
  83.4 1.6 %collective-permute-start.28 = (bf16[96,1024]{1,0:T(8,128)(2,1)S(1)}, bf16[96,1024]{1,0:T(8,128)(2,1)S(1)}, u32[]{:S(2)}, u32[]{:S(2)}) collective-permute-start(bf16[96,1024]{1,0:T(8,128)(2,1)S(1)} %get-tuple-element.118), channel_id=1, source_target_pairs={{0,3},{1,2},{2,1},{3,0},{4,7},{5,6},{6,5},{7,4},{8,11},{9,10},{10,... | collective-permute-start | bytes 589832 | tf_op jit(solution)/shard_map/ppermute | solution.py:43
  86.3 7.6 %collective-permute-done.25.refs_0_ = bf16[64,1024]{1,0:T(8,128)(2,1)S(1)} collective-permute-done((bf16[64,1024]{1,0:T(8,128)(2,1)S(1)}, bf16[64,1024]{1,0:T(8,128)(2,1)S(1)}, u32[]{:S(2)}, u32[]{:S(2)}) %collective-permute-start.25) | collective-permute-done | bytes 131104 | tf_op jit(solution)/shard_map/ppermute | solution.py:58
  95.6 1.6 %collective-permute-start.30 = (bf16[64,1024]{1,0:T(8,128)(2,1)S(1)}, bf16[64,1024]{1,0:T(8,128)(2,1)S(1)}, u32[]{:S(2)}, u32[]{:S(2)}) collective-permute-start(bf16[64,1024]{1,0:T(8,128)(2,1)S(1)} %get-tuple-element.124), channel_id=1, source_target_pairs={{0,28},{1,29},{2,30},{3,31},{4,24},{5,25},{6,26},{7,27},{8,20},{9,... | collective-permute-start | bytes 393224 | tf_op jit(solution)/shard_map/ppermute | solution.py:58
  97.1 3.1 %collective-permute-done.29.refs_1_ = bf16[64,1024]{1,0:T(8,128)(2,1)S(1)} collective-permute-done((bf16[64,1024]{1,0:T(8,128)(2,1)S(1)}, bf16[64,1024]{1,0:T(8,128)(2,1)S(1)}, u32[]{:S(2)}, u32[]{:S(2)}) %collective-permute-start.29) | collective-permute-done | bytes 131104 | tf_op jit(solution)/shard_map/ppermute | solution.py:58
  100.2 3.3 %collective-permute-done.30.refs_2_ = bf16[64,1024]{1,0:T(8,128)(2,1)S(1)} collective-permute-done((bf16[64,1024]{1,0:T(8,128)(2,1)S(1)}, bf16[64,1024]{1,0:T(8,128)(2,1)S(1)}, u32[]{:S(2)}, u32[]{:S(2)}) %collective-permute-start.30) | collective-permute-done | bytes 131104 | tf_op jit(solution)/shard_map/ppermute | solution.py:58
  (68 shorter events, 27.4 us)
Async XLA Ops:
  3.3 10.1 %collective-permute-start.2 = (bf16[64,1152]{1,0:T(8,128)(2,1)}, bf16[64,1152]{1,0:T(8,128)(2,1)S(1)}, u32[]{:S(2)}, u32[]{:S(2)}) collective-permute-start(bf16[64,1152]{1,0:T(8,128)(2,1)} %get-tuple-element.64.refs_3_.refs_2_), channel_id=1, source_target_pairs={{0,12},{1,13},{2,14},{3,15},{4,8},{5,9},{6,10},{7,11},{8,4},{9,5},... | collective-permute-start | bytes 442376 | tf_op jit(solution)/shard_map/ppermute | solution.py:34
  8.4 12.7 %collective-permute-start.1 = (bf16[64,1152]{1,0:T(8,128)(2,1)}, bf16[64,1152]{1,0:T(8,128)(2,1)S(1)}, u32[]{:S(2)}, u32[]{:S(2)}) collective-permute-start(bf16[64,1152]{1,0:T(8,128)(2,1)} %get-tuple-element.64.refs_3_.refs_2_), channel_id=1, source_target_pairs={{0,8},{1,9},{2,10},{3,11},{4,12},{5,13},{6,14},{7,15},{8,0},{9,1},... | collective-permute-start | bytes 442376 | tf_op jit(solution)/shard_map/ppermute | solution.py:34
  8.4 12.7 %collective-permute-start = (bf16[64,1152]{1,0:T(8,128)(2,1)}, bf16[64,1152]{1,0:T(8,128)(2,1)S(1)}, u32[]{:S(2)}, u32[]{:S(2)}) collective-permute-start(bf16[64,1152]{1,0:T(8,128)(2,1)} %get-tuple-element.64.refs_3_.refs_2_), channel_id=1, source_target_pairs={{0,4},{1,5},{2,6},{3,7},{4,0},{5,1},{6,2},{7,3},{8,12},{9,13},{10,... | collective-permute-start | bytes 442376 | tf_op jit(solution)/shard_map/ppermute | solution.py:34
  9.0 15.7 %collective-permute-start.6 = (bf16[96,1024]{1,0:T(8,128)(2,1)}, bf16[96,1024]{1,0:T(8,128)(2,1)S(1)}, u32[]{:S(2)}, u32[]{:S(2)}) collective-permute-start(bf16[96,1024]{1,0:T(8,128)(2,1)} %get-tuple-element.68), channel_id=1, source_target_pairs={{0,1},{1,0},{2,3},{3,2},{4,5},{5,4},{6,7},{7,6},{8,9},{9,8},{10,11... | collective-permute-start | bytes 589832 | tf_op jit(solution)/shard_map/ppermute | solution.py:43
  10.7 14.5 %collective-permute-start.7 = (bf16[96,1024]{1,0:T(8,128)(2,1)}, bf16[96,1024]{1,0:T(8,128)(2,1)S(1)}, u32[]{:S(2)}, u32[]{:S(2)}) collective-permute-start(bf16[96,1024]{1,0:T(8,128)(2,1)} %get-tuple-element.69), channel_id=1, source_target_pairs={{0,2},{1,3},{2,0},{3,1},{4,6},{5,7},{6,4},{7,5},{8,10},{9,11},{10,... | collective-permute-start | bytes 589832 | tf_op jit(solution)/shard_map/ppermute | solution.py:43
  13.4 14.3 %collective-permute-start.8 = (bf16[96,1024]{1,0:T(8,128)(2,1)}, bf16[96,1024]{1,0:T(8,128)(2,1)S(1)}, u32[]{:S(2)}, u32[]{:S(2)}) collective-permute-start(bf16[96,1024]{1,0:T(8,128)(2,1)} %get-tuple-element.70), channel_id=1, source_target_pairs={{0,3},{1,2},{2,1},{3,0},{4,7},{5,6},{6,5},{7,4},{8,11},{9,10},{10,... | collective-permute-start | bytes 589832 | tf_op jit(solution)/shard_map/ppermute | solution.py:43
  21.6 8.2 %collective-permute-start.9 = (bf16[96,1024]{1,0:T(8,128)(2,1)S(1)}, bf16[96,1024]{1,0:T(8,128)(2,1)S(1)}, u32[]{:S(2)}, u32[]{:S(2)}) collective-permute-start(bf16[96,1024]{1,0:T(8,128)(2,1)S(1)} %get-tuple-element.72), channel_id=1, source_target_pairs={{0,1},{1,0},{2,3},{3,2},{4,5},{5,4},{6,7},{7,6},{8,9},{9,8},{10,11... | collective-permute-start | bytes 589832 | tf_op jit(solution)/shard_map/ppermute | solution.py:43
  23.2 9.9 %collective-permute-start.10 = (bf16[96,1024]{1,0:T(8,128)(2,1)S(1)}, bf16[96,1024]{1,0:T(8,128)(2,1)S(1)}, u32[]{:S(2)}, u32[]{:S(2)}) collective-permute-start(bf16[96,1024]{1,0:T(8,128)(2,1)S(1)} %get-tuple-element.73), channel_id=1, source_target_pairs={{0,2},{1,3},{2,0},{3,1},{4,6},{5,7},{6,4},{7,5},{8,10},{9,11},{10,... | collective-permute-start | bytes 589832 | tf_op jit(solution)/shard_map/ppermute | solution.py:43
  24.7 8.4 %collective-permute-start.11 = (bf16[96,1024]{1,0:T(8,128)(2,1)S(1)}, bf16[96,1024]{1,0:T(8,128)(2,1)S(1)}, u32[]{:S(2)}, u32[]{:S(2)}) collective-permute-start(bf16[96,1024]{1,0:T(8,128)(2,1)S(1)} %get-tuple-element.74), channel_id=1, source_target_pairs={{0,3},{1,2},{2,1},{3,0},{4,7},{5,6},{6,5},{7,4},{8,11},{9,10},{10,... | collective-permute-start | bytes 589832 | tf_op jit(solution)/shard_map/ppermute | solution.py:43
  25.2 12.6 %collective-permute-start.5 = (bf16[128,1024]{1,0:T(8,128)(2,1)S(1)}, bf16[128,1024]{1,0:T(8,128)(2,1)S(1)}, u32[]{:S(2)}, u32[]{:S(2)}) collective-permute-start(bf16[128,1024]{1,0:T(8,128)(2,1)S(1)} %copy-done.8), channel_id=1, source_target_pairs={{0,12},{1,13},{2,14},{3,15},{4,8},{5,9},{6,10},{7,11},{8,4},{9,5},... | collective-permute-start | bytes 786440 | tf_op jit(solution)/shard_map/ppermute | solution.py:34
  27.7 20.0 %collective-permute-start.4 = (bf16[128,1024]{1,0:T(8,128)(2,1)S(1)}, bf16[128,1024]{1,0:T(8,128)(2,1)S(1)}, u32[]{:S(2)}, u32[]{:S(2)}) collective-permute-start(bf16[128,1024]{1,0:T(8,128)(2,1)S(1)} %copy-done.8), channel_id=1, source_target_pairs={{0,8},{1,9},{2,10},{3,11},{4,12},{5,13},{6,14},{7,15},{8,0},{9,1},... | collective-permute-start | bytes 786440 | tf_op jit(solution)/shard_map/ppermute | solution.py:34
  29.8 17.9 %collective-permute-start.3 = (bf16[128,1024]{1,0:T(8,128)(2,1)S(1)}, bf16[128,1024]{1,0:T(8,128)(2,1)S(1)}, u32[]{:S(2)}, u32[]{:S(2)}) collective-permute-start(bf16[128,1024]{1,0:T(8,128)(2,1)S(1)} %copy-done.8), channel_id=1, source_target_pairs={{0,4},{1,5},{2,6},{3,7},{4,0},{5,1},{6,2},{7,3},{8,12},{9,13},{10,... | collective-permute-start | bytes 786440 | tf_op jit(solution)/shard_map/ppermute | solution.py:34
  35.7 12.0 %collective-permute-start.12 = (bf16[128,1024]{1,0:T(8,128)(2,1)S(1)}, bf16[128,1024]{1,0:T(8,128)(2,1)S(1)}, u32[]{:S(2)}, u32[]{:S(2)}) collective-permute-start(bf16[128,1024]{1,0:T(8,128)(2,1)S(1)} %get-tuple-element.76), channel_id=1, source_target_pairs={{0,1},{1,0},{2,3},{3,2},{4,5},{5,4},{6,7},{7,6},{8,9},{9,8},{10,11... | collective-permute-start | bytes 786440 | tf_op jit(solution)/shard_map/ppermute | solution.py:43
  37.0 11.8 %collective-permute-start.13 = (bf16[128,1024]{1,0:T(8,128)(2,1)S(1)}, bf16[128,1024]{1,0:T(8,128)(2,1)S(1)}, u32[]{:S(2)}, u32[]{:S(2)}) collective-permute-start(bf16[128,1024]{1,0:T(8,128)(2,1)S(1)} %get-tuple-element.77), channel_id=1, source_target_pairs={{0,2},{1,3},{2,0},{3,1},{4,6},{5,7},{6,4},{7,5},{8,10},{9,11},{10,... | collective-permute-start | bytes 786440 | tf_op jit(solution)/shard_map/ppermute | solution.py:43
  37.8 10.9 %collective-permute-start.14 = (bf16[128,1024]{1,0:T(8,128)(2,1)S(1)}, bf16[128,1024]{1,0:T(8,128)(2,1)S(1)}, u32[]{:S(2)}, u32[]{:S(2)}) collective-permute-start(bf16[128,1024]{1,0:T(8,128)(2,1)S(1)} %get-tuple-element.78), channel_id=1, source_target_pairs={{0,3},{1,2},{2,1},{3,0},{4,7},{5,6},{6,5},{7,4},{8,11},{9,10},{10,... | collective-permute-start | bytes 786440 | tf_op jit(solution)/shard_map/ppermute | solution.py:43
  50.7 18.3 %collective-permute-start.19 = (bf16[192,1024]{1,0:T(8,128)(2,1)S(1)}, bf16[192,1024]{1,0:T(8,128)(2,1)S(1)}, u32[]{:S(2)}, u32[]{:S(2)}) collective-permute-start(bf16[192,1024]{1,0:T(8,128)(2,1)S(1)} %get-tuple-element.95), channel_id=1, source_target_pairs={{0,1},{1,0},{2,3},{3,2},{4,5},{5,4},{6,7},{7,6},{8,9},{9,8},{10,11... | collective-permute-start | bytes 1179656 | tf_op jit(solution)/shard_map/ppermute | solution.py:43
  51.4 17.6 %collective-permute-start.20 = (bf16[192,1024]{1,0:T(8,128)(2,1)S(1)}, bf16[192,1024]{1,0:T(8,128)(2,1)S(1)}, u32[]{:S(2)}, u32[]{:S(2)}) collective-permute-start(bf16[192,1024]{1,0:T(8,128)(2,1)S(1)} %get-tuple-element.96), channel_id=1, source_target_pairs={{0,2},{1,3},{2,0},{3,1},{4,6},{5,7},{6,4},{7,5},{8,10},{9,11},{10,... | collective-permute-start | bytes 1179656 | tf_op jit(solution)/shard_map/ppermute | solution.py:43
  52.9 16.1 %collective-permute-start.21 = (bf16[192,1024]{1,0:T(8,128)(2,1)S(1)}, bf16[192,1024]{1,0:T(8,128)(2,1)S(1)}, u32[]{:S(2)}, u32[]{:S(2)}) collective-permute-start(bf16[192,1024]{1,0:T(8,128)(2,1)S(1)} %get-tuple-element.97), channel_id=1, source_target_pairs={{0,3},{1,2},{2,1},{3,0},{4,7},{5,6},{6,5},{7,4},{8,11},{9,10},{10,... | collective-permute-start | bytes 1179656 | tf_op jit(solution)/shard_map/ppermute | solution.py:43
  55.7 13.2 %collective-permute-start.18 = (f32[64,1024]{1,0:T(8,128)S(1)}, f32[64,1024]{1,0:T(8,128)S(1)}, u32[]{:S(2)}, u32[]{:S(2)}) collective-permute-start(f32[64,1024]{1,0:T(8,128)S(1)} %get-tuple-element.94), channel_id=1, source_target_pairs={{0,16},{1,17},{2,18},{3,19},{4,20},{5,21},{6,22},{7,23},{8,24},{9,... | collective-permute-start | bytes 786440 | tf_op jit(solution)/shard_map/ppermute | solution.py:58
  81.4 12.5 %collective-permute-start.26 = (bf16[96,1024]{1,0:T(8,128)(2,1)S(1)}, bf16[96,1024]{1,0:T(8,128)(2,1)S(1)}, u32[]{:S(2)}, u32[]{:S(2)}) collective-permute-start(bf16[96,1024]{1,0:T(8,128)(2,1)S(1)} %get-tuple-element.116), channel_id=1, source_target_pairs={{0,1},{1,0},{2,3},{3,2},{4,5},{5,4},{6,7},{7,6},{8,9},{9,8},{10,11... | collective-permute-start | bytes 589832 | tf_op jit(solution)/shard_map/ppermute | solution.py:43
  82.6 11.7 %collective-permute-start.27 = (bf16[96,1024]{1,0:T(8,128)(2,1)S(1)}, bf16[96,1024]{1,0:T(8,128)(2,1)S(1)}, u32[]{:S(2)}, u32[]{:S(2)}) collective-permute-start(bf16[96,1024]{1,0:T(8,128)(2,1)S(1)} %get-tuple-element.117), channel_id=1, source_target_pairs={{0,2},{1,3},{2,0},{3,1},{4,6},{5,7},{6,4},{7,5},{8,10},{9,11},{10,... | collective-permute-start | bytes 589832 | tf_op jit(solution)/shard_map/ppermute | solution.py:43
  83.4 10.8 %collective-permute-start.28 = (bf16[96,1024]{1,0:T(8,128)(2,1)S(1)}, bf16[96,1024]{1,0:T(8,128)(2,1)S(1)}, u32[]{:S(2)}, u32[]{:S(2)}) collective-permute-start(bf16[96,1024]{1,0:T(8,128)(2,1)S(1)} %get-tuple-element.118), channel_id=1, source_target_pairs={{0,3},{1,2},{2,1},{3,0},{4,7},{5,6},{6,5},{7,4},{8,11},{9,10},{10,... | collective-permute-start | bytes 589832 | tf_op jit(solution)/shard_map/ppermute | solution.py:43
  85.0 8.9 %collective-permute-start.25 = (bf16[64,1024]{1,0:T(8,128)(2,1)S(1)}, bf16[64,1024]{1,0:T(8,128)(2,1)S(1)}, u32[]{:S(2)}, u32[]{:S(2)}) collective-permute-start(bf16[64,1024]{1,0:T(8,128)(2,1)S(1)} %shard_map.129), channel_id=1, source_target_pairs={{0,24},{1,25},{2,26},{3,27},{4,28},{5,29},{6,30},{7,31},{8,16},{9,... | collective-permute-start | bytes 393224 | tf_op jit(solution)/shard_map/ppermute | solution.py:58
  94.9 8.6 %collective-permute-start.31 = (bf16[192,1024]{1,0:T(8,128)(2,1)S(1)}, bf16[192,1024]{1,0:T(8,128)(2,1)S(1)}, u32[]{:S(2)}, u32[]{:S(2)}) collective-permute-start(bf16[192,1024]{1,0:T(8,128)(2,1)S(1)} %get-tuple-element.125), channel_id=1, source_target_pairs={{0,16},{1,17},{2,18},{3,19},{4,20},{5,21},{6,22},{7,23},{8,24},{9,... | collective-permute-start | bytes 1179656 | tf_op jit(solution)/shard_map/ppermute | solution.py:58
  (17 other events, 146.0 us)

commit v3 on v2

--- a/solution.py
+++ b/solution.py
@@ -8,6 +8,16 @@
 from jax.sharding import PartitionSpec as P
 
 EPSILON = 1e-06
+COST = {
+    "prepare": 2,
+    "local": 2,
+    "select": 2,
+    "f_expert": 2.25,
+    "b_expert": 0.5,
+    "combine": 2,
+    "output": 2,
+    "gradient": 2,
+}
 BF16 = jnp.bfloat16
 F32 = jnp.float32
 
@@ -74,7 +84,7 @@
     return lax.dot_general(left, right, (((1,), (1,)), ((), ())), preferred_element_type=F32)
 
 
-def call(kernel, out_shape, args, far=(), scratch=(), cost=None, limit=16 * 2**20):
+def call(kernel, out_shape, args, cost, far=(), scratch=(), limit=16 * 2**20):
     near = pl.BlockSpec(memory_space=pltpu.VMEM)
     return pl.pallas_call(
         kernel,
@@ -87,7 +97,9 @@
             *([pltpu.SemaphoreType.DMA((len(far),))] if far else []),
         ],
         compiler_params=pltpu.CompilerParams(vmem_limit_bytes=limit),
-        cost_estimate=cost or pl.CostEstimate(flops=2**31, bytes_accessed=2**22, transcendentals=0),
+        cost_estimate=pl.CostEstimate(
+            flops=int(cost * 2**30), bytes_accessed=2**16, transcendentals=0
+        ),
     )(*args, *far)
 
 
@@ -152,18 +164,44 @@
     return terms[0] + terms[1] + terms[2]
 
 
-def prepare_kernel(outer, inner, capacity, *refs):
-    far, (f_pack, b_pack, home), own = refs[:8], refs[8:11], refs[11 : 11 + inner]
-    table, *near, semaphores = refs[11 + inner :]
+def prepare_kernel(experts, *refs):
+    far, (f_pack,) = refs[:6], refs[6:7]
+    table, *near, semaphores = refs[7:]
+    copies = fetches(far, near, semaphores)
+    lists, (fx, gain) = near[:4], near[4:]
+    width = fx.shape[1]
+    for copy in copies:
+        copy.wait()
+    f_pack[:, pl.ds(0, width)] = normed_rows(fx[...], gain[...])
+    fill_table(experts, table, lists)
+    f_pack[:, pl.ds(width, table.shape[0])] = table[...].T.astype(BF16)
+
+
+def prepare(experts, *args):
+    tokens, width = args[4].shape
+    lanes = 8 * experts
+    return call(
+        functools.partial(prepare_kernel, experts),
+        [shape(tokens, width + lanes)],
+        (),
+        COST["prepare"],
+        args,
+        scratch=(pltpu.VMEM((lanes, tokens), F32),),
+        limit=60 * 2**20,
+    )[0]
+
+
+def local_kernel(outer, inner, capacity, *refs):
+    f_pack, far = refs[0], refs[1:4]
+    (b_pack, home), own = refs[4:6], refs[6 : 6 + inner]
+    table, *near, semaphores = refs[6 + inner :]
     experts = outer * inner
     copies = fetches(far, near, semaphores)
-    lists, (fx, bx, grad, gain) = near[:4], near[4:]
-    tokens, width = fx.shape
+    bx, grad, gain = near
+    tokens, width = bx.shape
+    table[...] = f_pack[:, pl.ds(width, table.shape[0])].astype(F32).T
     for copy in copies:
         copy.wait()
-    fill_table(experts, table, lists)
-    f_pack[:, pl.ds(width, table.shape[0])] = table[...].T.astype(BF16)
-    f_pack[:, pl.ds(0, width)] = normed_rows(fx[...], gain[...])
     b_pack[pl.ds(0, tokens), :] = normed_rows(bx[...], gain[...])
     b_pack[pl.ds(tokens, tokens), :] = grad[...]
     home[pl.ds(0, tokens), :] = bx[...]
@@ -179,14 +217,15 @@
         own[j][pl.ds(2 * capacity, capacity), :] = (gate * dot(b_hit, grad[...])).astype(BF16)
 
 
-def prepare(outer, inner, capacity, *args):
-    tokens, width = args[4].shape
-    lanes = 8 * outer * inner
+def local(f_pack, outer, inner, capacity, *args):
+    tokens, width = args[0].shape
+    lanes = f_pack.shape[1] - width
     return call(
-        functools.partial(prepare_kernel, outer, inner, capacity),
-        [shape(tokens, width + lanes), shape(2 * tokens, width), shape(2 * tokens, width)]
+        functools.partial(local_kernel, outer, inner, capacity),
+        [shape(2 * tokens, width), shape(2 * tokens, width)]
         + [shape(3 * capacity, width)] * inner,
-        (),
+        (f_pack,),
+        COST["local"],
         args,
         scratch=(pltpu.VMEM((lanes, tokens), F32),),
         limit=60 * 2**20,
@@ -223,6 +262,7 @@
         functools.partial(select_kernel, outer, inner, capacity, side, blocks),
         [shape(blocks * capacity * (side + 1), width)] * inner,
         (*packs, *rows),
+        COST["select"],
         scratch=(
             pltpu.VMEM((blocks * tokens * (side + 1), width), BF16),
             pltpu.VMEM((8 * outer * inner, blocks * tokens), F32),
@@ -235,67 +275,47 @@
     return [pl.ds(start, step) for start in range(0, size, step)]
 
 
-def load_rows(flat, own, others, groups, capacity, part, parts):
+def places(inner, groups):
+    return [(j, k) for group in groups for j in range(inner) for k in group]
+
+
+def load_rows(flat, own, others, inner, groups, steps, capacity, part, parts):
     rest = others[0].shape[0] // parts
     first = 0 if parts == 1 else part + 1
-    at = 0
-    for j, k in [(j, k) for group in groups for j in range(len(own)) for k in group]:
+    for at, (j, k) in enumerate(places(inner, groups)):
         if k == 0:
             rows = own[j][pl.ds(first * capacity, capacity), :]
         else:
-            rows = others[j][pl.ds(part * rest + (k - 1) * capacity, capacity), :]
-        flat[pl.ds(at, capacity), :] = rows
-        at += capacity
-
-
-def forward_kernel(inner, blocks, capacity, *refs):
-    own, others, (w_gate, w_up, w_down) = (
-        refs[:inner],
-        refs[inner : 2 * inner],
-        refs[2 * inner : 2 * inner + 3],
-    )
-    outs, (flat, hidden) = refs[2 * inner + 3 : 3 * inner + 3], refs[3 * inner + 3 :]
-    load_rows(flat, own, others, (blocks,), capacity, 0, 1)
+            rows = others[j][pl.ds(part * rest + steps.index(k) * capacity, capacity), :]
+        flat[pl.ds(at * capacity, capacity), :] = rows
+
+
+def store_rows(outs, result, part):
+    at = 0
+    for out in outs:
+        out[:, part] = result[at : at + out.shape[0]]
+        at += out.shape[0]
+
+
+def forward_kernel(inner, groups, steps, capacity, *refs):
+    own, others = refs[:inner], refs[inner : 2 * inner]
+    w_gate, w_up, w_down = refs[2 * inner : 2 * inner + 3]
+    outs, (flat, hidden) = refs[2 * inner + 3 : -2], refs[-2:]
+    load_rows(flat, own, others, inner, groups, steps, capacity, 0, 1)
     for part in chunks(w_gate.shape[1], 256):
         gate = dot(flat[...], w_gate[:, part])
         upward = dot(flat[...], w_up[:, part])
         hidden[:, part] = (gate * jax.nn.sigmoid(gate) * upward).astype(BF16)
-    count = outs[0].shape[0]
     for part in chunks(w_down.shape[1], 256):
-        result = dot(hidden[...], w_down[:, part]).astype(BF16)
-        for j in range(inner):
-            outs[j][:, part] = result[j * count : (j + 1) * count]
-
-
-def expert_forward(own, others, weights, blocks, capacity):
-    inner = len(own)
-    count = len(blocks) * capacity
-    width, hidden = weights[0].shape
-    return call(
-        functools.partial(forward_kernel, inner, blocks, capacity),
-        [shape(count, width)] * inner,
-        (*own, *others, *weights),
-        scratch=(
-            pltpu.VMEM((inner * count, width), BF16),
-            pltpu.VMEM((inner * count, hidden), BF16),
-        ),
-        cost=pl.CostEstimate(
-            flops=6 * inner * count * width * hidden,
-            bytes_accessed=6 * width * hidden + 4 * inner * count * width,
-            transcendentals=inner * count * hidden,
-        ),
-    )
-
-
-def backward_kernel(inner, groups, capacity, *refs):
-    own, others, (w_gate, w_up, w_down) = (
-        refs[:inner],
-        refs[inner : 2 * inner],
-        refs[2 * inner : 2 * inner + 3],
-    )
+        store_rows(outs, dot(hidden[...], w_down[:, part]).astype(BF16), part)
+
+
+def backward_kernel(inner, groups, steps, capacity, *refs):
+    own, others = refs[:inner], refs[inner : 2 * inner]
+    w_gate, w_up, w_down = refs[2 * inner : 2 * inner + 3]
     outs, (flat, flat_grad, d_gate, d_up) = refs[2 * inner + 3 : -4], refs[-4:]
-    load_rows(flat, own, others, groups, capacity, 0, 2)
-    load_rows(flat_grad, own, others, groups, capacity, 1, 2)
+    load_rows(flat, own, others, inner, groups, steps, capacity, 0, 2)
+    load_rows(flat_grad, own, others, inner, groups, steps, capacity, 1, 2)
     for part in chunks(w_gate.shape[1], 256):
         gate = dot(flat[...], w_gate[:, part])
         upward = dot(flat[...], w_up[:, part])
@@ -305,30 +325,22 @@
         d_up[:, part] = (d_hidden * gate * sigma).astype(BF16)
     for part in chunks(w_gate.shape[0], 256):
         result = dot_nt(d_gate[...], w_gate[part, :]) + dot_nt(d_up[...], w_up[part, :])
-        result = result.astype(BF16)
-        at = 0
-        for out in outs:
-            out[:, part] = result[at : at + out.shape[0]]
-            at += out.shape[0]
-
-
-def expert_backward(own, others, weights, groups, capacity):
+        store_rows(outs, result.astype(BF16), part)
+
+
+def expert(kernel, own, others, weights, groups, steps, capacity, inputs, products, cost):
     inner = len(own)
-    count = sum(len(group) for group in groups) * capacity
+    count = len(places(inner, groups)) * capacity
     width, hidden = weights[0].shape
     outs = call(
-        functools.partial(backward_kernel, inner, groups, capacity),
+        functools.partial(kernel, inner, groups, steps, capacity),
         [shape(len(group) * capacity, width) for group in groups for _ in range(inner)],
         (*own, *others, *weights),
-        scratch=[pltpu.VMEM((inner * count, width), BF16)] * 2
-        + [pltpu.VMEM((inner * count, hidden), BF16)] * 2,
-        cost=pl.CostEstimate(
-            flops=10 * inner * count * width * hidden,
-            bytes_accessed=6 * width * hidden + 6 * inner * count * width,
-            transcendentals=inner * count * hidden,
-        ),
-    )
-    return outs[:inner], outs[inner:]
+        scratch=[pltpu.VMEM((count, width), BF16)] * inputs
+        + [pltpu.VMEM((count, hidden), BF16)] * inputs,
+        cost=cost,
+    )
+    return [outs[i * inner : (i + 1) * inner] for i in range(len(groups))]
 
 
 def combine_kernel(blocks, experts, inner, capacity, side, *refs):
@@ -364,9 +376,7 @@
         if outs[k].dtype == F32:
             outs[k][...] = home[...].astype(F32) + part
         else:
-            outs[k][pl.ds(0, tokens), :] = part.astype(BF16)
-            if outs[k].shape[0] > tokens:
-                outs[k][pl.ds(tokens, 2 * tokens), :] = home[...]
+            outs[k][...] = part.astype(BF16)
 
 
 def combine(packs, results, gain, home, steps, inner, capacity, side):
@@ -374,11 +384,12 @@
     blocks = len(packs)
     tokens, width = packs[0].shape[0], results[0].shape[1]
     lanes = packs[0].shape[1] - width
-    local = shape(3 * tokens, width) if side == 1 else shape(tokens, width, dtype=F32)
+    local = shape(tokens, width, dtype=BF16 if side else F32)
     return call(
         functools.partial(combine_kernel, blocks, lanes // 8, inner, capacity, side),
         [shape(tokens, width) if k else local for k in steps],
         (*packs, *results, gain, home),
+        COST["combine"],
         scratch=(pltpu.VMEM((blocks * tokens, lanes), F32),),
     )
 
@@ -391,13 +402,12 @@
 
 
 def gradient_kernel(*refs):
-    local, out = refs[-2:]
+    home, out = refs[-2:]
     tokens = out.shape[1]
-    summed, stream, grad = (
-        local[pl.ds(i * tokens, tokens), :].astype(F32) for i in range(3)
-    )
+    stream, grad = (home[pl.ds(i * tokens, tokens), :].astype(F32) for i in range(2))
     scale = norm_scale(stream)
-    for part in refs[:-2]:
+    summed = refs[0][...].astype(F32)
+    for part in refs[1:-2]:
         summed = summed + part[...].astype(F32)
     inner = jnp.mean(summed * stream, axis=-1, keepdims=True)
     out[0] = (grad + scale * summed - stream * (scale * scale * scale * inner)).astype(BF16)
@@ -424,13 +434,14 @@
     fx, bx, grad = fwd_input[0], bwd_input[0], bwd_grad[0]
     weights = (w_gate[0, 0], w_up[0, 0], w_down[0, 0])
 
+    steps = tuple(range(1, outer))
+
     def spread(block):
-        return [over_outer(block, k, outer, inner) for k in range(1, outer)]
+        return [over_outer(block, k, outer, inner) for k in steps]
 
     def exchanged(blocks, back=False):
-        return [blocks[0]] + [
-            over_inner(blocks[j], j, outer, inner, back) for j in range(1, inner)
-        ]
+        sent = {j: over_inner(blocks[j], j, outer, inner, back) for j in reversed(range(1, inner))}
+        return [blocks[0], *(sent[j] for j in range(1, inner))]
 
     def returned(blocks, steps, distance):
         return [
@@ -438,37 +449,65 @@
         ]
 
     lists = [v[0].T for v in (fwd_routes, fwd_gates, bwd_routes, bwd_gates)]
-    f_pack, b_pack, home, *own = prepare(
-        outer, inner, capacity, *lists, fx, bx, grad, norm_gain
-    )
+    f_pack = prepare(experts, *lists, fx, norm_gain)
+    b_pack, home, *own = local(f_pack, outer, inner, capacity, bx, grad, norm_gain)
     f_away = spread(f_pack)
     own = exchanged(own)
-    b_away = spread(after(b_pack, f_away[0]))
-
+    every = (*range(outer // 2, outer), *range(1, outer // 2), 0)
     sizes = (width, outer, inner, capacity)
-    f_rows = exchanged(select(f_away, f_away, *sizes, 0))
-    every = (*range(1, outer), 0)
-    f_back = exchanged(expert_forward(own, f_rows, weights, every, capacity), True)
-    b_away, f_back = after((b_away, f_back))
-    b_picked = select(f_away, b_away, *sizes, 1)
-    b_rows = exchanged(b_picked)
-    packs = [f_pack] + f_away
-    f_sums = combine(packs, after(f_back, b_picked[0]), norm_gain, fx, every, inner, capacity, 0)
-    f_parts = returned(f_sums, every, 1)
-    b_rows = after(b_rows, f_parts)
     half = outer // 2
-    groups = ((half,), (*range(1, half), *range(half + 1, outer), 0))
-    first, last = expert_backward(own, b_rows, weights, groups, capacity)
-    b_back = exchanged(first, True)
+    lower, upper = tuple(range(1, half)), tuple(range(half, outer))
+    near = (*lower, 0)
+    packs = {0: f_pack, **dict(zip(steps, f_away))}
+    b_away = dict(zip(steps, spread(after(b_pack, f_away[0]))))
+    f_picked = select(f_away, f_away, *sizes, 0)
+    f_rows = exchanged(f_picked)
+    f_result = expert(
+        forward_kernel, own, f_rows, weights, (every,), steps, capacity, 1, 3, COST["f_expert"]
+    )[0]
+    f_back = exchanged(f_result, True)
+
+    def b_selected(steps, before):
+        chosen = after(([packs[k] for k in steps], [b_away[k] for k in steps]), before)
+        return select(*chosen, *sizes, 1)
+
+    def b_expert(rows, steps, given):
+        return expert(
+            backward_kernel,
+            own,
+            rows,
+            weights,
+            (steps,),
+            given,
+            capacity,
+            2,
+            5,
+            COST["b_expert"],
+        )[0]
+
+    def combined(results, steps, home, side):
+        return combine(packs, results, norm_gain, home, steps, inner, capacity, side)
+
+    b_low = b_selected(lower, f_result[0])
+    b_low_rows = exchanged(b_low)
+    b_up = b_selected(upper, (b_low[0], f_back))
+    b_up_rows = exchanged(b_up)
+    f_sums = combined(after(f_back, b_up[0]), every, fx, 0)
+    f_parts = returned(f_sums[: len(upper)], upper, 1)
+    low_result = b_expert(after(b_low_rows, f_sums[0]), near, lower)
+    f_near, home = after((f_sums[len(upper) :], home), low_result[0])
+    f_parts += returned(f_near, near, 1)
+    home_next = home_and_along(home, 0, outer, inner, -1)
+    up_result = b_expert(after(b_up_rows, (low_result[0], f_parts[0])), upper, upper)
     out = shape(1, tokens, width)
-    forward_next = call(output_kernel, out, f_parts)
-    b_back = after(b_back, forward_next)
-    b_sums = combine(packs, b_back, norm_gain, home, groups[0], inner, capacity, 1)
-    b_parts = returned(b_sums, groups[0], -1)
-    b_last = after(exchanged(after(last, b_sums[0]), True), b_parts[0])
-    b_sums = combine(packs, b_last, norm_gain, home, groups[1], inner, capacity, 1)
-    b_parts += returned(b_sums, groups[1], -1)
-    backward_next = call(gradient_kernel, out, b_parts)
+    forward_next = call(output_kernel, out, f_parts, COST["output"])
+    up_back = exchanged(up_result, True)
+    low_back = exchanged(after(low_result, up_back[1]), True)
+    up_sums = combined(after(up_back, (home_next, forward_next)), upper, fx, 1)
+    b_parts = returned(up_sums, upper, -1)
+    low_sums = combined(after(low_back, up_sums[0]), near, fx, 1)
+    b_parts += returned(low_sums, near, -1)
+    backward_next = call(gradient_kernel, out, [*b_parts, home_next], COST["gradient"])
     return (forward_next, backward_next)
 
 

time: 105 us -> 95 us (0.905)
  starting transfers between devices: 49.9 us -> 41.2 us
  waiting for transfers between devices: 39.1 us -> 35.2 us
  Pallas kernels: 14.3 us -> 17.4 us
    ppermute x8 -> x9, waiting for transfers between devices: 18.7 us -> 8.46 us  [home_and_along(): return lax.ppermute(block, ('segment', 'expert'), route)]
    ppermute x8 -> x9, starting transfers between devices: 13.7 us -> 4.62 us  [home_and_along(): return lax.ppermute(block, ('segment', 'expert'), route)]
    ppermute x18 -> x21, waiting for transfers between devices: 5.85 us -> 12 us  [over_inner(): return lax.ppermute(block, 'expert', route)]
    ppermute x18 -> x21, starting transfers between devices: 23.6 us -> 27.8 us  [over_inner(): return lax.ppermute(block, 'expert', route)]
    ppermute x6, starting transfers between devices: 12.6 us -> 8.84 us  [over_outer(): return lax.ppermute(block, 'expert', route)]
    pallas_call x10 -> x13, Pallas kernels: 14.3 us -> 17.4 us  [call(): pl.pallas_call(kernel, out_shape=out_shape, in_specs=[near] * len(args) +...]
  transfers between devices with their start and end apart: 32 -> 36, of which waited for: 13 -> 13; matrix products, arithmetic and copies ran while one was open for 0% -> 0% of each run, Pallas kernels for 4% -> 16%
where the time goes in v3:
time: 95 us; the launch traced here: 94.8 us
  starting transfers between devices  41.2 us (43%)
  waiting for transfers between devices  35.2 us (37%)
  Pallas kernels  17.4 us (18%)
    ppermute x21, starting transfers between devices, over_inner(): return lax.ppermute(block, 'expert', route)  27.8 us
    pallas_call x13, Pallas kernels, call(): pl.pallas_call(kernel, out_shape=out_shape, in_specs=[near] * len(args) +...  17.4 us
    ppermute x6, waiting for transfers between devices, over_outer(): return lax.ppermute(block, 'expert', route)  14.7 us
    ppermute x21, waiting for transfers between devices, over_inner(): return lax.ppermute(block, 'expert', route)  12 us
    ppermute x6, starting transfers between devices, over_outer(): return lax.ppermute(block, 'expert', route)  8.84 us
    ppermute x9, waiting for transfers between devices, home_and_along(): return lax.ppermute(block, ('segment', 'expert'), route)  8.46 us
    ppermute x9, starting transfers between devices, home_and_along(): return lax.ppermute(block, ('segment', 'expert'), route)  4.62 us
  transfers between devices with their start and end apart: 36, of which 13 were waited for; matrix products, arithmetic and copies ran while one was open for 0% of the time, Pallas kernels for 16%

profile of v3, /device:TPU:0, one launch (start us, length us, event | category | flops | bytes accessed | tf_op | source)
XLA Modules:
  0.0 94.8 jit_solution(201592115570692957)
XLA Ops:
  0.6 1.9 %shard_map.122.refs_0_.refs_3_.refs_1_ = bf16[64,1152]{1,0:T(8,128)(2,1)} custom-call(s32[8,64]{1,0:T(8,128)} %bitcast.33, f32[8,64]{1,0:T(8,128)} %bitcast.34, s32[8,64]{1,0:T(8,128)} %bitcast.35, f32[8,64]{1,0:T(8,128)} %bitcast.36, bf16[64,1024]{1,0:T(8,128)(2,1)} %bitcast.27, f32[1,1024]{1,0:T(1,128)} %refs_6_.3), custom_call_target="tpu_custom_call" | custom-call | flops 2147483648 | bytes 65536 | tf_op jit(solution)/shard_map/pallas_call | solution.py:89
  2.5 3.1 %collective-permute-start.2 = (bf16[64,1152]{1,0:T(8,128)(2,1)}, bf16[64,1152]{1,0:T(8,128)(2,1)S(1)}, u32[]{:S(2)}, u32[]{:S(2)}) collective-permute-start(bf16[64,1152]{1,0:T(8,128)(2,1)} %shard_map.122.refs_0_.refs_3_.refs_1_), channel_id=1, source_target_pairs={{0,4},{1,5},{2,6},{3,7},{4,0},{5,1},{6,2},{7,3},{8,12},{9,13},{10,... | collective-permute-start | bytes 442376 | tf_op jit(solution)/shard_map/ppermute | solution.py:44
  5.6 2.5 %collective-permute-start.1 = (bf16[64,1152]{1,0:T(8,128)(2,1)}, bf16[64,1152]{1,0:T(8,128)(2,1)S(1)}, u32[]{:S(2)}, u32[]{:S(2)}) collective-permute-start(bf16[64,1152]{1,0:T(8,128)(2,1)} %shard_map.122.refs_0_.refs_3_.refs_1_), channel_id=1, source_target_pairs={{0,12},{1,13},{2,14},{3,15},{4,8},{5,9},{6,10},{7,11},{8,4},{9,5},... | collective-permute-start | bytes 442376 | tf_op jit(solution)/shard_map/ppermute | solution.py:44
  8.2 3.4 %shard_map.123 = (bf16[128,1024]{1,0:T(8,128)(2,1)}, bf16[128,1024]{1,0:T(8,128)(2,1)}, bf16[96,1024]{1,0:T(8,128)(2,1)}, bf16[96,1024]{1,0:T(8,128)(2,1)}, bf16...) custom-call(bf16[64,1152]{1,0:T(8,128)(2,1)} %shard_map.122.refs_0_.refs_3_.refs_1_, bf16[64,1024]{1,0:T(8,128)(2,1)} %bitcast.31, ...), custom_call_target="tpu_custom_call" | custom-call | flops 2147483648 | bytes 65536 | tf_op jit(solution)/shard_map/pallas_call | solution.py:89
  11.6 1.6 %collective-permute-start.3 = (bf16[96,1024]{1,0:T(8,128)(2,1)}, bf16[96,1024]{1,0:T(8,128)(2,1)S(1)}, u32[]{:S(2)}, u32[]{:S(2)}) collective-permute-start(bf16[96,1024]{1,0:T(8,128)(2,1)} %get-tuple-element.75), channel_id=1, source_target_pairs={{0,1},{1,0},{2,3},{3,2},{4,5},{5,4},{6,7},{7,6},{8,9},{9,8},{10,11... | collective-permute-start | bytes 589832 | tf_op jit(solution)/shard_map/ppermute | solution.py:53
  13.1 1.5 %collective-permute-start.4 = (bf16[96,1024]{1,0:T(8,128)(2,1)}, bf16[96,1024]{1,0:T(8,128)(2,1)S(1)}, u32[]{:S(2)}, u32[]{:S(2)}) collective-permute-start(bf16[96,1024]{1,0:T(8,128)(2,1)} %get-tuple-element.76), channel_id=1, source_target_pairs={{0,2},{1,3},{2,0},{3,1},{4,6},{5,7},{6,4},{7,5},{8,10},{9,11},{10,... | collective-permute-start | bytes 589832 | tf_op jit(solution)/shard_map/ppermute | solution.py:53
  16.3 5.2 %collective-permute-done.refs_1_.refs_4_.refs_0_ = bf16[64,1152]{1,0:T(8,128)(2,1)S(1)} collective-permute-done((bf16[64,1152]{1,0:T(8,128)(2,1)}, bf16[64,1152]{1,0:T(8,128)(2,1)S(1)}, u32[]{:S(2)}, u32[]{:S(2)}) %collective-permute-start) | collective-permute-done | bytes 147488 | tf_op jit(solution)/shard_map/ppermute | solution.py:44
  22.0 1.6 %collective-permute-start.6 = (bf16[96,1024]{1,0:T(8,128)(2,1)S(1)}, bf16[96,1024]{1,0:T(8,128)(2,1)S(1)}, u32[]{:S(2)}, u32[]{:S(2)}) collective-permute-start(bf16[96,1024]{1,0:T(8,128)(2,1)S(1)} %get-tuple-element.79), channel_id=1, source_target_pairs={{0,1},{1,0},{2,3},{3,2},{4,5},{5,4},{6,7},{7,6},{8,9},{9,8},{10,11... | collective-permute-start | bytes 589832 | tf_op jit(solution)/shard_map/ppermute | solution.py:53
  23.6 1.5 %collective-permute-start.7 = (bf16[96,1024]{1,0:T(8,128)(2,1)S(1)}, bf16[96,1024]{1,0:T(8,128)(2,1)S(1)}, u32[]{:S(2)}, u32[]{:S(2)}) collective-permute-start(bf16[96,1024]{1,0:T(8,128)(2,1)S(1)} %get-tuple-element.80), channel_id=1, source_target_pairs={{0,2},{1,3},{2,0},{3,1},{4,6},{5,7},{6,4},{7,5},{8,10},{9,11},{10,... | collective-permute-start | bytes 589832 | tf_op jit(solution)/shard_map/ppermute | solution.py:53
  25.6 2.7 %collective-permute-start.13 = (bf16[128,1024]{1,0:T(8,128)(2,1)S(1)}, bf16[128,1024]{1,0:T(8,128)(2,1)S(1)}, u32[]{:S(2)}, u32[]{:S(2)}) collective-permute-start(bf16[128,1024]{1,0:T(8,128)(2,1)S(1)} %copy-done.8), channel_id=1, source_target_pairs={{0,12},{1,13},{2,14},{3,15},{4,8},{5,9},{6,10},{7,11},{8,4},{9,5},... | collective-permute-start | bytes 786440 | tf_op jit(solution)/shard_map/ppermute | solution.py:44
  30.2 3.2 %collective-permute-done.7.refs_6_ = bf16[96,1024]{1,0:T(8,128)(2,1)S(1)} collective-permute-done((bf16[96,1024]{1,0:T(8,128)(2,1)S(1)}, bf16[96,1024]{1,0:T(8,128)(2,1)S(1)}, u32[]{:S(2)}, u32[]{:S(2)}) %collective-permute-start.7) | collective-permute-done | bytes 196640 | tf_op jit(solution)/shard_map/ppermute | solution.py:53
  33.4 2.6 %shard_map.125 = (bf16[128,1024]{1,0:T(8,128)(2,1)S(1)}, bf16[128,1024]{1,0:T(8,128)(2,1)S(1)}, bf16[128,1024]{1,0:T(8,128)(2,1)S(1)}, bf16[128,1024]{1,0:T(8,128)(2,1)S(1)}) custom-call(bf16[96,1024]{1,0:T(8,128)(2,1)S(1)} %copy-done.3, bf16[96,1024]{1,0:T(8,128)(2,1)S(1)} %collective-permute-done.3.refs_1_, ...), custom_call_target="tpu_custom_call" | custom-call | flops 2415919104 | bytes 65536 | tf_op jit(solution)/shard_map/pallas_call | solution.py:89
  38.1 1.5 %collective-permute-start.11 = (bf16[128,1024]{1,0:T(8,128)(2,1)S(1)}, bf16[128,1024]{1,0:T(8,128)(2,1)S(1)}, u32[]{:S(2)}, u32[]{:S(2)}) collective-permute-start(bf16[128,1024]{1,0:T(8,128)(2,1)S(1)} %get-tuple-element.85), channel_id=1, source_target_pairs={{0,3},{1,2},{2,1},{3,0},{4,7},{5,6},{6,5},{7,4},{8,11},{9,10},{10,... | collective-permute-start | bytes 786440 | tf_op jit(solution)/shard_map/ppermute | solution.py:53
  42.6 7.4 %collective-permute-done.12.refs_2_ = bf16[128,1024]{1,0:T(8,128)(2,1)S(1)} collective-permute-done((bf16[128,1024]{1,0:T(8,128)(2,1)S(1)}, bf16[128,1024]{1,0:T(8,128)(2,1)S(1)}, u32[]{:S(2)}, u32[]{:S(2)}) %collective-permute-start.12) | collective-permute-done | bytes 262176 | tf_op jit(solution)/shard_map/ppermute | solution.py:44
  54.2 1.5 %collective-permute-start.23 = (bf16[128,1024]{1,0:T(8,128)(2,1)S(1)}, bf16[128,1024]{1,0:T(8,128)(2,1)S(1)}, u32[]{:S(2)}, u32[]{:S(2)}) collective-permute-start(bf16[128,1024]{1,0:T(8,128)(2,1)S(1)} %get-tuple-element.116), channel_id=1, source_target_pairs={{0,2},{1,3},{2,0},{3,1},{4,6},{5,7},{6,4},{7,5},{8,10},{9,11},{10,... | collective-permute-start | bytes 786440 | tf_op jit(solution)/shard_map/ppermute | solution.py:53
  56.7 3.4 %collective-permute-start.24 = (bf16[128,1024]{1,0:T(8,128)(2,1)S(1)}, bf16[128,1024]{1,0:T(8,128)(2,1)S(1)}, u32[]{:S(2)}, u32[]{:S(2)}) collective-permute-start(bf16[128,1024]{1,0:T(8,128)(2,1)S(1)} %get-tuple-element.117), channel_id=1, source_target_pairs={{0,3},{1,2},{2,1},{3,0},{4,7},{5,6},{6,5},{7,4},{8,11},{9,10},{10,... | collective-permute-start | bytes 786440 | tf_op jit(solution)/shard_map/ppermute | solution.py:53
  60.1 2.3 %shard_map.129 = (bf16[64,1024]{1,0:T(8,128)(2,1)S(1)}, bf16[64,1024]{1,0:T(8,128)(2,1)S(1)}, bf16[64,1024]{1,0:T(8,128)(2,1)S(1)}, bf16[64,1024]{1,0:T(8,128)(2,1)S(1)}) custom-call(bf16[96,1024]{1,0:T(8,128)(2,1)S(1)} %copy-done.3, bf16[96,1024]{1,0:T(8,128)(2,1)S(1)} %collective-permute-done.3.refs_1_, ...), custom_call_target="tpu_custom_call" | custom-call | flops 536870912 | bytes 65536 | tf_op jit(solution)/shard_map/pallas_call | solution.py:89
  65.1 2.2 %collective-permute-done.23.refs_6_ = bf16[128,1024]{1,0:T(8,128)(2,1)S(1)} collective-permute-done((bf16[128,1024]{1,0:T(8,128)(2,1)S(1)}, bf16[128,1024]{1,0:T(8,128)(2,1)S(1)}, u32[]{:S(2)}, u32[]{:S(2)}) %collective-permute-start.23) | collective-permute-done | bytes 262176 | tf_op jit(solution)/shard_map/ppermute | solution.py:53
  67.4 2.3 %shard_map.131 = (bf16[64,1024]{1,0:T(8,128)(2,1)S(1)}, bf16[64,1024]{1,0:T(8,128)(2,1)S(1)}, bf16[64,1024]{1,0:T(8,128)(2,1)S(1)}, bf16[64,1024]{1,0:T(8,128)(2,1)S(1)}) custom-call(bf16[96,1024]{1,0:T(8,128)(2,1)S(1)} %copy-done.3, bf16[96,1024]{1,0:T(8,128)(2,1)S(1)} %collective-permute-done.3.refs_1_, ...), custom_call_target="tpu_custom_call" | custom-call | flops 536870912 | bytes 65536 | tf_op jit(solution)/shard_map/pallas_call | solution.py:89
  69.7 1.6 %collective-permute-start.25 = (bf16[64,1024]{1,0:T(8,128)(2,1)S(1)}, bf16[64,1024]{1,0:T(8,128)(2,1)S(1)}, u32[]{:S(2)}, u32[]{:S(2)}) collective-permute-start(bf16[64,1024]{1,0:T(8,128)(2,1)S(1)} %get-tuple-element.123), channel_id=1, source_target_pairs={{0,1},{1,0},{2,3},{3,2},{4,5},{5,4},{6,7},{7,6},{8,9},{9,8},{10,11... | collective-permute-start | bytes 393224 | tf_op jit(solution)/shard_map/ppermute | solution.py:53
  74.0 2.1 %collective-permute-done.25.refs_3_ = bf16[64,1024]{1,0:T(8,128)(2,1)S(1)} collective-permute-done((bf16[64,1024]{1,0:T(8,128)(2,1)S(1)}, bf16[64,1024]{1,0:T(8,128)(2,1)S(1)}, u32[]{:S(2)}, u32[]{:S(2)}) %collective-permute-start.25) | collective-permute-done | bytes 131104 | tf_op jit(solution)/shard_map/ppermute | solution.py:53
  80.3 1.6 %collective-permute-start.30 = (bf16[64,1024]{1,0:T(8,128)(2,1)S(1)}, bf16[64,1024]{1,0:T(8,128)(2,1)S(1)}, u32[]{:S(2)}, u32[]{:S(2)}) collective-permute-start(bf16[64,1024]{1,0:T(8,128)(2,1)S(1)} %get-tuple-element.132), channel_id=1, source_target_pairs={{0,28},{1,29},{2,30},{3,31},{4,24},{5,25},{6,26},{7,27},{8,20},{9,... | collective-permute-start | bytes 393224 | tf_op jit(solution)/shard_map/ppermute | solution.py:68
  82.6 2.7 %collective-permute-done.32.refs_4_ = bf16[64,1024]{1,0:T(8,128)(2,1)S(1)} collective-permute-done((bf16[64,1024]{1,0:T(8,128)(2,1)S(1)}, bf16[64,1024]{1,0:T(8,128)(2,1)S(1)}, u32[]{:S(2)}, u32[]{:S(2)}) %collective-permute-start.32) | collective-permute-done | bytes 131104 | tf_op jit(solution)/shard_map/ppermute | solution.py:53
  88.1 5.9 %collective-permute-done.29.refs_0_ = bf16[64,1024]{1,0:T(8,128)(2,1)S(1)} collective-permute-done((bf16[64,1024]{1,0:T(8,128)(2,1)S(1)}, bf16[64,1024]{1,0:T(8,128)(2,1)S(1)}, u32[]{:S(2)}, u32[]{:S(2)}) %collective-permute-start.29) | collective-permute-done | bytes 131104 | tf_op jit(solution)/shard_map/ppermute | solution.py:68
  (79 shorter events, 28.7 us)
Async XLA Ops:
  2.5 12.2 %collective-permute-start.2 = (bf16[64,1152]{1,0:T(8,128)(2,1)}, bf16[64,1152]{1,0:T(8,128)(2,1)S(1)}, u32[]{:S(2)}, u32[]{:S(2)}) collective-permute-start(bf16[64,1152]{1,0:T(8,128)(2,1)} %shard_map.122.refs_0_.refs_3_.refs_1_), channel_id=1, source_target_pairs={{0,4},{1,5},{2,6},{3,7},{4,0},{5,1},{6,2},{7,3},{8,12},{9,13},{10,... | collective-permute-start | bytes 442376 | tf_op jit(solution)/shard_map/ppermute | solution.py:44
  5.6 10.7 %collective-permute-start.1 = (bf16[64,1152]{1,0:T(8,128)(2,1)}, bf16[64,1152]{1,0:T(8,128)(2,1)S(1)}, u32[]{:S(2)}, u32[]{:S(2)}) collective-permute-start(bf16[64,1152]{1,0:T(8,128)(2,1)} %shard_map.122.refs_0_.refs_3_.refs_1_), channel_id=1, source_target_pairs={{0,12},{1,13},{2,14},{3,15},{4,8},{5,9},{6,10},{7,11},{8,4},{9,5},... | collective-permute-start | bytes 442376 | tf_op jit(solution)/shard_map/ppermute | solution.py:44
  8.1 13.4 %collective-permute-start = (bf16[64,1152]{1,0:T(8,128)(2,1)}, bf16[64,1152]{1,0:T(8,128)(2,1)S(1)}, u32[]{:S(2)}, u32[]{:S(2)}) collective-permute-start(bf16[64,1152]{1,0:T(8,128)(2,1)} %shard_map.122.refs_0_.refs_3_.refs_1_), channel_id=1, source_target_pairs={{0,8},{1,9},{2,10},{3,11},{4,12},{5,13},{6,14},{7,15},{8,0},{9,1},... | collective-permute-start | bytes 442376 | tf_op jit(solution)/shard_map/ppermute | solution.py:44
  11.6 13.5 %collective-permute-start.3 = (bf16[96,1024]{1,0:T(8,128)(2,1)}, bf16[96,1024]{1,0:T(8,128)(2,1)S(1)}, u32[]{:S(2)}, u32[]{:S(2)}) collective-permute-start(bf16[96,1024]{1,0:T(8,128)(2,1)} %get-tuple-element.75), channel_id=1, source_target_pairs={{0,1},{1,0},{2,3},{3,2},{4,5},{5,4},{6,7},{7,6},{8,9},{9,8},{10,11... | collective-permute-start | bytes 589832 | tf_op jit(solution)/shard_map/ppermute | solution.py:53
  13.1 12.4 %collective-permute-start.4 = (bf16[96,1024]{1,0:T(8,128)(2,1)}, bf16[96,1024]{1,0:T(8,128)(2,1)S(1)}, u32[]{:S(2)}, u32[]{:S(2)}) collective-permute-start(bf16[96,1024]{1,0:T(8,128)(2,1)} %get-tuple-element.76), channel_id=1, source_target_pairs={{0,2},{1,3},{2,0},{3,1},{4,6},{5,7},{6,4},{7,5},{8,10},{9,11},{10,... | collective-permute-start | bytes 589832 | tf_op jit(solution)/shard_map/ppermute | solution.py:53
  14.7 10.9 %collective-permute-start.5 = (bf16[96,1024]{1,0:T(8,128)(2,1)}, bf16[96,1024]{1,0:T(8,128)(2,1)S(1)}, u32[]{:S(2)}, u32[]{:S(2)}) collective-permute-start(bf16[96,1024]{1,0:T(8,128)(2,1)} %get-tuple-element.77), channel_id=1, source_target_pairs={{0,3},{1,2},{2,1},{3,0},{4,7},{5,6},{6,5},{7,4},{8,11},{9,10},{10,... | collective-permute-start | bytes 589832 | tf_op jit(solution)/shard_map/ppermute | solution.py:53
  23.6 9.8 %collective-permute-start.7 = (bf16[96,1024]{1,0:T(8,128)(2,1)S(1)}, bf16[96,1024]{1,0:T(8,128)(2,1)S(1)}, u32[]{:S(2)}, u32[]{:S(2)}) collective-permute-start(bf16[96,1024]{1,0:T(8,128)(2,1)S(1)} %get-tuple-element.80), channel_id=1, source_target_pairs={{0,2},{1,3},{2,0},{3,1},{4,6},{5,7},{6,4},{7,5},{8,10},{9,11},{10,... | collective-permute-start | bytes 589832 | tf_op jit(solution)/shard_map/ppermute | solution.py:53
  25.1 8.3 %collective-permute-start.8 = (bf16[96,1024]{1,0:T(8,128)(2,1)S(1)}, bf16[96,1024]{1,0:T(8,128)(2,1)S(1)}, u32[]{:S(2)}, u32[]{:S(2)}) collective-permute-start(bf16[96,1024]{1,0:T(8,128)(2,1)S(1)} %get-tuple-element.81), channel_id=1, source_target_pairs={{0,3},{1,2},{2,1},{3,0},{4,7},{5,6},{6,5},{7,4},{8,11},{9,10},{10,... | collective-permute-start | bytes 589832 | tf_op jit(solution)/shard_map/ppermute | solution.py:53
  25.6 12.5 %collective-permute-start.14 = (bf16[128,1024]{1,0:T(8,128)(2,1)S(1)}, bf16[128,1024]{1,0:T(8,128)(2,1)S(1)}, u32[]{:S(2)}, u32[]{:S(2)}) collective-permute-start(bf16[128,1024]{1,0:T(8,128)(2,1)S(1)} %copy-done.8), channel_id=1, source_target_pairs={{0,4},{1,5},{2,6},{3,7},{4,0},{5,1},{6,2},{7,3},{8,12},{9,13},{10,... | collective-permute-start | bytes 786440 | tf_op jit(solution)/shard_map/ppermute | solution.py:44
  25.6 15.5 %collective-permute-start.13 = (bf16[128,1024]{1,0:T(8,128)(2,1)S(1)}, bf16[128,1024]{1,0:T(8,128)(2,1)S(1)}, u32[]{:S(2)}, u32[]{:S(2)}) collective-permute-start(bf16[128,1024]{1,0:T(8,128)(2,1)S(1)} %copy-done.8), channel_id=1, source_target_pairs={{0,12},{1,13},{2,14},{3,15},{4,8},{5,9},{6,10},{7,11},{8,4},{9,5},... | collective-permute-start | bytes 786440 | tf_op jit(solution)/shard_map/ppermute | solution.py:44
  29.7 20.3 %collective-permute-start.12 = (bf16[128,1024]{1,0:T(8,128)(2,1)S(1)}, bf16[128,1024]{1,0:T(8,128)(2,1)S(1)}, u32[]{:S(2)}, u32[]{:S(2)}) collective-permute-start(bf16[128,1024]{1,0:T(8,128)(2,1)S(1)} %copy-done.8), channel_id=1, source_target_pairs={{0,8},{1,9},{2,10},{3,11},{4,12},{5,13},{6,14},{7,15},{8,0},{9,1},... | collective-permute-start | bytes 786440 | tf_op jit(solution)/shard_map/ppermute | solution.py:44
  36.1 15.5 %collective-permute-start.9 = (bf16[128,1024]{1,0:T(8,128)(2,1)S(1)}, bf16[128,1024]{1,0:T(8,128)(2,1)S(1)}, u32[]{:S(2)}, u32[]{:S(2)}) collective-permute-start(bf16[128,1024]{1,0:T(8,128)(2,1)S(1)} %get-tuple-element.83), channel_id=1, source_target_pairs={{0,1},{1,0},{2,3},{3,2},{4,5},{5,4},{6,7},{7,6},{8,9},{9,8},{10,11... | collective-permute-start | bytes 786440 | tf_op jit(solution)/shard_map/ppermute | solution.py:53
  37.3 15.7 %collective-permute-start.10 = (bf16[128,1024]{1,0:T(8,128)(2,1)S(1)}, bf16[128,1024]{1,0:T(8,128)(2,1)S(1)}, u32[]{:S(2)}, u32[]{:S(2)}) collective-permute-start(bf16[128,1024]{1,0:T(8,128)(2,1)S(1)} %get-tuple-element.84), channel_id=1, source_target_pairs={{0,2},{1,3},{2,0},{3,1},{4,6},{5,7},{6,4},{7,5},{8,10},{9,11},{10,... | collective-permute-start | bytes 786440 | tf_op jit(solution)/shard_map/ppermute | solution.py:53
  38.1 14.9 %collective-permute-start.11 = (bf16[128,1024]{1,0:T(8,128)(2,1)S(1)}, bf16[128,1024]{1,0:T(8,128)(2,1)S(1)}, u32[]{:S(2)}, u32[]{:S(2)}) collective-permute-start(bf16[128,1024]{1,0:T(8,128)(2,1)S(1)} %get-tuple-element.85), channel_id=1, source_target_pairs={{0,3},{1,2},{2,1},{3,0},{4,7},{5,6},{6,5},{7,4},{8,11},{9,10},{10,... | collective-permute-start | bytes 786440 | tf_op jit(solution)/shard_map/ppermute | solution.py:53
  41.1 15.4 %collective-permute-start.17 = (bf16[64,1024]{1,0:T(8,128)(2,1)S(1)}, bf16[64,1024]{1,0:T(8,128)(2,1)S(1)}, u32[]{:S(2)}, u32[]{:S(2)}) collective-permute-start(bf16[64,1024]{1,0:T(8,128)(2,1)S(1)} %get-tuple-element.105), channel_id=1, source_target_pairs={{0,1},{1,0},{2,3},{3,2},{4,5},{5,4},{6,7},{7,6},{8,9},{9,8},{10,11... | collective-permute-start | bytes 393224 | tf_op jit(solution)/shard_map/ppermute | solution.py:53
  51.5 8.6 %collective-permute-start.19 = (bf16[64,1024]{1,0:T(8,128)(2,1)S(1)}, bf16[64,1024]{1,0:T(8,128)(2,1)S(1)}, u32[]{:S(2)}, u32[]{:S(2)}) collective-permute-start(bf16[64,1024]{1,0:T(8,128)(2,1)S(1)} %get-tuple-element.107), channel_id=1, source_target_pairs={{0,3},{1,2},{2,1},{3,0},{4,7},{5,6},{6,5},{7,4},{8,11},{9,10},{10,... | collective-permute-start | bytes 393224 | tf_op jit(solution)/shard_map/ppermute | solution.py:53
  53.6 10.3 %collective-permute-start.22 = (bf16[128,1024]{1,0:T(8,128)(2,1)S(1)}, bf16[128,1024]{1,0:T(8,128)(2,1)S(1)}, u32[]{:S(2)}, u32[]{:S(2)}) collective-permute-start(bf16[128,1024]{1,0:T(8,128)(2,1)S(1)} %get-tuple-element.115), channel_id=1, source_target_pairs={{0,1},{1,0},{2,3},{3,2},{4,5},{5,4},{6,7},{7,6},{8,9},{9,8},{10,11... | collective-permute-start | bytes 786440 | tf_op jit(solution)/shard_map/ppermute | solution.py:53
  54.2 13.2 %collective-permute-start.23 = (bf16[128,1024]{1,0:T(8,128)(2,1)S(1)}, bf16[128,1024]{1,0:T(8,128)(2,1)S(1)}, u32[]{:S(2)}, u32[]{:S(2)}) collective-permute-start(bf16[128,1024]{1,0:T(8,128)(2,1)S(1)} %get-tuple-element.116), channel_id=1, source_target_pairs={{0,2},{1,3},{2,0},{3,1},{4,6},{5,7},{6,4},{7,5},{8,10},{9,11},{10,... | collective-permute-start | bytes 786440 | tf_op jit(solution)/shard_map/ppermute | solution.py:53
  56.7 10.7 %collective-permute-start.24 = (bf16[128,1024]{1,0:T(8,128)(2,1)S(1)}, bf16[128,1024]{1,0:T(8,128)(2,1)S(1)}, u32[]{:S(2)}, u32[]{:S(2)}) collective-permute-start(bf16[128,1024]{1,0:T(8,128)(2,1)S(1)} %get-tuple-element.117), channel_id=1, source_target_pairs={{0,3},{1,2},{2,1},{3,0},{4,7},{5,6},{6,5},{7,4},{8,11},{9,10},{10,... | collective-permute-start | bytes 786440 | tf_op jit(solution)/shard_map/ppermute | solution.py:53
  62.4 10.8 %collective-permute-start.21 = (f32[64,1024]{1,0:T(8,128)S(1)}, f32[64,1024]{1,0:T(8,128)S(1)}, u32[]{:S(2)}, u32[]{:S(2)}) collective-permute-start(f32[64,1024]{1,0:T(8,128)S(1)} %get-tuple-element.114), channel_id=1, source_target_pairs={{0,16},{1,17},{2,18},{3,19},{4,20},{5,21},{6,22},{7,23},{8,24},{9,... | collective-permute-start | bytes 786440 | tf_op jit(solution)/shard_map/ppermute | solution.py:68
  63.9 8.7 %collective-permute-start.16 = (bf16[64,1024]{1,0:T(8,128)(2,1)S(1)}, bf16[64,1024]{1,0:T(8,128)(2,1)S(1)}, u32[]{:S(2)}, u32[]{:S(2)}) collective-permute-start(bf16[64,1024]{1,0:T(8,128)(2,1)S(1)} %get-tuple-element.101), channel_id=1, source_target_pairs={{0,28},{1,29},{2,30},{3,31},{4,24},{5,25},{6,26},{7,27},{8,20},{9,... | collective-permute-start | bytes 393224 | tf_op jit(solution)/shard_map/ppermute | solution.py:68
  67.4 11.5 %collective-permute-start.28 = (bf16[128,1024]{1,0:T(8,128)(2,1)S(1)}, bf16[128,1024]{1,0:T(8,128)(2,1)S(1)}, u32[]{:S(2)}, u32[]{:S(2)}) collective-permute-start(bf16[128,1024]{1,0:T(8,128)(2,1)S(1)} %copy-done.7), channel_id=1, source_target_pairs={{0,16},{1,17},{2,18},{3,19},{4,20},{5,21},{6,22},{7,23},{8,24},{9,... | collective-permute-start | bytes 786440 | tf_op jit(solution)/shard_map/ppermute | solution.py:68
  71.3 8.6 %collective-permute-start.26 = (bf16[64,1024]{1,0:T(8,128)(2,1)S(1)}, bf16[64,1024]{1,0:T(8,128)(2,1)S(1)}, u32[]{:S(2)}, u32[]{:S(2)}) collective-permute-start(bf16[64,1024]{1,0:T(8,128)(2,1)S(1)} %get-tuple-element.124), channel_id=1, source_target_pairs={{0,2},{1,3},{2,0},{3,1},{4,6},{5,7},{6,4},{7,5},{8,10},{9,11},{10,... | collective-permute-start | bytes 393224 | tf_op jit(solution)/shard_map/ppermute | solution.py:53
  81.9 12.0 %collective-permute-start.29 = (bf16[64,1024]{1,0:T(8,128)(2,1)S(1)}, bf16[64,1024]{1,0:T(8,128)(2,1)S(1)}, u32[]{:S(2)}, u32[]{:S(2)}) collective-permute-start(bf16[64,1024]{1,0:T(8,128)(2,1)S(1)} %get-tuple-element.131), channel_id=1, source_target_pairs={{0,24},{1,25},{2,26},{3,27},{4,28},{5,29},{6,30},{7,31},{8,16},{9,... | collective-permute-start | bytes 393224 | tf_op jit(solution)/shard_map/ppermute | solution.py:68
  (21 other events, 192.0 us)

commit v4 on v3

--- a/solution.py
+++ b/solution.py
@@ -164,6 +164,17 @@
     return terms[0] + terms[1] + terms[2]
 
 
+def all_picked(table, side, outer, inner, blocks, capacity):
+    hits, gates = [], []
+    for j in range(inner):
+        expert = my_expert(j, outer, inner)
+        hit = picked(table, side, expert, outer * inner, blocks, capacity)
+        gate = gate_of(table, side, expert, outer * inner)
+        hits.append(hit)
+        gates.append(jnp.sum(hit * gate, axis=1, keepdims=True))
+    return jnp.concatenate(hits).astype(BF16), jnp.concatenate(gates)
+
+
 def prepare_kernel(experts, *refs):
     far, (f_pack,) = refs[:6], refs[6:7]
     table, *near, semaphores = refs[7:]
@@ -206,15 +217,14 @@
     b_pack[pl.ds(tokens, tokens), :] = grad[...]
     home[pl.ds(0, tokens), :] = bx[...]
     home[pl.ds(tokens, tokens), :] = grad[...]
-    for j in range(inner):
-        expert = my_expert(j, outer, inner)
-        f_hit = picked(table, 0, expert, experts, 1, capacity).astype(BF16)
-        b_hit = picked(table, 1, expert, experts, 1, capacity)
-        gate = jnp.sum(b_hit * gate_of(table, 1, expert, experts), axis=1, keepdims=True)
-        b_hit = b_hit.astype(BF16)
-        own[j][pl.ds(0, capacity), :] = dot(f_hit, f_pack[:, pl.ds(0, width)]).astype(BF16)
-        own[j][pl.ds(capacity, capacity), :] = dot(b_hit, b_pack[pl.ds(0, tokens), :]).astype(BF16)
-        own[j][pl.ds(2 * capacity, capacity), :] = (gate * dot(b_hit, grad[...])).astype(BF16)
+    f_hits, _ = all_picked(table, 0, outer, inner, 1, capacity)
+    b_hits, gates = all_picked(table, 1, outer, inner, 1, capacity)
+    f_rows = dot(f_hits, f_pack[:, pl.ds(0, width)]).astype(BF16)
+    b_rows = dot(b_hits, b_pack[pl.ds(0, tokens), :]).astype(BF16)
+    grads = (gates * dot(b_hits, grad[...])).astype(BF16)
+    for part, rows in enumerate((f_rows, b_rows, grads)):
+        for j in range(inner):
+            own[j][pl.ds(part * capacity, capacity), :] = rows[j * capacity : (j + 1) * capacity]
 
 
 def local(f_pack, outer, inner, capacity, *args):
@@ -228,7 +238,7 @@
         COST["local"],
         args,
         scratch=(pltpu.VMEM((lanes, tokens), F32),),
-        limit=60 * 2**20,
+        limit=16 * 2**20,
     )
 
 
@@ -245,14 +255,13 @@
                 pl.ds(part * tokens, tokens), pl.ds(0, width)
             ]
     slots = blocks * capacity
-    for j in range(inner):
-        expert = my_expert(j, outer, inner)
-        hit = picked(table, side, expert, experts, blocks, capacity)
-        outs[j][pl.ds(0, slots), :] = dot(hit.astype(BF16), flat[pl.ds(0, total), :]).astype(BF16)
-        if side == 1:
-            gate = jnp.sum(hit * gate_of(table, 1, expert, experts), axis=1, keepdims=True)
-            grads = dot(hit.astype(BF16), flat[pl.ds(total, total), :])
-            outs[j][pl.ds(slots, slots), :] = (gate * grads).astype(BF16)
+    hits, gates = all_picked(table, side, outer, inner, blocks, capacity)
+    found = [dot(hits, flat[pl.ds(0, total), :]).astype(BF16)]
+    if side == 1:
+        found.append((gates * dot(hits, flat[pl.ds(total, total), :])).astype(BF16))
+    for part, rows_found in enumerate(found):
+        for j in range(inner):
+            outs[j][pl.ds(part * slots, slots), :] = rows_found[j * slots : (j + 1) * slots]
 
 
 def select(packs, rows, width, outer, inner, capacity, side):
@@ -356,21 +365,24 @@
     lane = lax.broadcasted_iota(jnp.int32, (total, lanes), 1)
     shift = lax.broadcasted_iota(jnp.int32, (total, 1), 0) // tokens * capacity
     place = lax.broadcasted_iota(jnp.int32, (total, slots), 1)
-    summed = None
+    hits, summed = [], None
     for j in range(inner):
         first = 4 * experts * side + my_expert(j, experts // inner, inner)
         column = jnp.where(lane == first + 3 * experts, flat[...], 0.0)
         rank = jnp.sum(column, axis=1, keepdims=True).astype(jnp.int32)
         slot = jnp.where(rank >= 0, rank + shift, -1)
         hit = (slot == place).astype(F32).astype(BF16)
+        if side == 1:
+            hits.append(hit)
+            continue
         spread = dot(hit, results[j][...])
-        if side == 0:
-            terms = (lane == first) | (lane == first + experts) | (lane == first + 2 * experts)
-            column = jnp.where(terms, flat[...], 0.0)
-            spread = jnp.sum(column, axis=1, keepdims=True) * spread
+        terms = (lane == first) | (lane == first + experts) | (lane == first + 2 * experts)
+        column = jnp.where(terms, flat[...], 0.0)
+        spread = jnp.sum(column, axis=1, keepdims=True) * spread
         summed = spread if summed is None else summed + spread
     if side == 1:
-        summed = gain[...] * summed
+        rows = jnp.concatenate([result[...] for result in results])
+        summed = gain[...] * dot(jnp.concatenate(hits, axis=1), rows)
     for k in range(blocks):
         part = summed[k * tokens : (k + 1) * tokens]
         if outs[k].dtype == F32:
@@ -488,9 +500,9 @@
     def combined(results, steps, home, side):
         return combine(packs, results, norm_gain, home, steps, inner, capacity, side)
 
-    b_low = b_selected(lower, f_result[0])
+    b_low = b_selected(lower, f_picked[0])
     b_low_rows = exchanged(b_low)
-    b_up = b_selected(upper, (b_low[0], f_back))
+    b_up = b_selected(upper, (b_low[0], f_back[:-1]))
     b_up_rows = exchanged(b_up)
     f_sums = combined(after(f_back, b_up[0]), every, fx, 0)
     f_parts = returned(f_sums[: len(upper)], upper, 1)

time: 95 us -> 95 us (level)
  Pallas kernels: 17.4 us -> 14.9 us
  waiting for transfers between devices: 35.2 us -> 37.4 us
    pallas_call x13, Pallas kernels: 17.4 us -> 14.9 us  [call(): pl.pallas_call(kernel, out_shape=out_shape, in_specs=[near] * len(args) +...]
    ppermute x6, waiting for transfers between devices: 14.7 us -> 16.3 us  [over_outer(): return lax.ppermute(block, 'expert', route)]
  transfers between devices with their start and end apart: 36 -> 36, of which waited for: 13 -> 15; matrix products, arithmetic and copies ran while one was open for 0% -> 0% of each run, Pallas kernels for 16% -> 13%
where the time goes in v4:
time: 95 us; the launch traced here: 94.8 us
  starting transfers between devices  40.8 us (43%)
  waiting for transfers between devices  37.4 us (39%)
  Pallas kernels  14.9 us (16%)
  local copies, waits for them, and re-layouts  0.96 us (1%)
    ppermute x21, starting transfers between devices, over_inner(): return lax.ppermute(block, 'expert', route)  27.8 us
    ppermute x6, waiting for transfers between devices, over_outer(): return lax.ppermute(block, 'expert', route)  16.3 us
    pallas_call x13, Pallas kernels, call(): pl.pallas_call(kernel, out_shape=out_shape, in_specs=[near] * len(args) +...  14.9 us
    ppermute x21, waiting for transfers between devices, over_inner(): return lax.ppermute(block, 'expert', route)  12.7 us
    ppermute x9, waiting for transfers between devices, home_and_along(): return lax.ppermute(block, ('segment', 'expert'), route)  8.41 us
    ppermute x6, starting transfers between devices, over_outer(): return lax.ppermute(block, 'expert', route)  8.36 us
    ppermute x9, starting transfers between devices, home_and_along(): return lax.ppermute(block, ('segment', 'expert'), route)  4.61 us
  transfers between devices with their start and end apart: 36, of which 15 were waited for; matrix products, arithmetic and copies ran while one was open for 0% of the time, Pallas kernels for 13%

profile of v4, /device:TPU:0, one launch (start us, length us, event | category | flops | bytes accessed | tf_op | source)
XLA Modules:
  0.0 94.8 jit_solution(18232386063752842296)
XLA Ops:
  0.7 1.9 %shard_map.122.refs_0_.refs_3_.refs_1_ = bf16[64,1152]{1,0:T(8,128)(2,1)} custom-call(s32[8,64]{1,0:T(8,128)} %bitcast.33, f32[8,64]{1,0:T(8,128)} %bitcast.34, s32[8,64]{1,0:T(8,128)} %bitcast.35, f32[8,64]{1,0:T(8,128)} %bitcast.36, bf16[64,1024]{1,0:T(8,128)(2,1)} %bitcast.29, f32[1,1024]{1,0:T(1,128)} %refs_6_.3), custom_call_target="tpu_custom_call" | custom-call | flops 2147483648 | bytes 65536 | tf_op jit(solution)/shard_map/pallas_call | solution.py:89
  2.6 3.1 %collective-permute-start.2 = (bf16[64,1152]{1,0:T(8,128)(2,1)}, bf16[64,1152]{1,0:T(8,128)(2,1)S(1)}, u32[]{:S(2)}, u32[]{:S(2)}) collective-permute-start(bf16[64,1152]{1,0:T(8,128)(2,1)} %shard_map.122.refs_0_.refs_3_.refs_1_), channel_id=1, source_target_pairs={{0,4},{1,5},{2,6},{3,7},{4,0},{5,1},{6,2},{7,3},{8,12},{9,13},{10,... | collective-permute-start | bytes 442376 | tf_op jit(solution)/shard_map/ppermute | solution.py:44
  5.7 2.5 %collective-permute-start.1 = (bf16[64,1152]{1,0:T(8,128)(2,1)}, bf16[64,1152]{1,0:T(8,128)(2,1)S(1)}, u32[]{:S(2)}, u32[]{:S(2)}) collective-permute-start(bf16[64,1152]{1,0:T(8,128)(2,1)} %shard_map.122.refs_0_.refs_3_.refs_1_), channel_id=1, source_target_pairs={{0,12},{1,13},{2,14},{3,15},{4,8},{5,9},{6,10},{7,11},{8,4},{9,5},... | collective-permute-start | bytes 442376 | tf_op jit(solution)/shard_map/ppermute | solution.py:44
  10.1 1.6 %collective-permute-start.3 = (bf16[96,1024]{1,0:T(8,128)(2,1)S(1)}, bf16[96,1024]{1,0:T(8,128)(2,1)S(1)}, u32[]{:S(2)}, u32[]{:S(2)}) collective-permute-start(bf16[96,1024]{1,0:T(8,128)(2,1)S(1)} %get-tuple-element.75), channel_id=1, source_target_pairs={{0,1},{1,0},{2,3},{3,2},{4,5},{5,4},{6,7},{7,6},{8,9},{9,8},{10,11... | collective-permute-start | bytes 589832 | tf_op jit(solution)/shard_map/ppermute | solution.py:53
  13.8 2.6 %collective-permute-done.1.refs_2_.refs_5_.refs_1_ = bf16[64,1152]{1,0:T(8,128)(2,1)S(1)} collective-permute-done((bf16[64,1152]{1,0:T(8,128)(2,1)}, bf16[64,1152]{1,0:T(8,128)(2,1)S(1)}, u32[]{:S(2)}, u32[]{:S(2)}) %collective-permute-start.1) | collective-permute-done | bytes 147488 | tf_op jit(solution)/shard_map/ppermute | solution.py:44
  16.4 5.2 %collective-permute-done.refs_1_.refs_4_.refs_0_ = bf16[64,1152]{1,0:T(8,128)(2,1)S(1)} collective-permute-done((bf16[64,1152]{1,0:T(8,128)(2,1)}, bf16[64,1152]{1,0:T(8,128)(2,1)S(1)}, u32[]{:S(2)}, u32[]{:S(2)}) %collective-permute-start) | collective-permute-done | bytes 147488 | tf_op jit(solution)/shard_map/ppermute | solution.py:44
  22.1 1.6 %collective-permute-start.6 = (bf16[96,1024]{1,0:T(8,128)(2,1)S(1)}, bf16[96,1024]{1,0:T(8,128)(2,1)S(1)}, u32[]{:S(2)}, u32[]{:S(2)}) collective-permute-start(bf16[96,1024]{1,0:T(8,128)(2,1)S(1)} %get-tuple-element.79), channel_id=1, source_target_pairs={{0,1},{1,0},{2,3},{3,2},{4,5},{5,4},{6,7},{7,6},{8,9},{9,8},{10,11... | collective-permute-start | bytes 589832 | tf_op jit(solution)/shard_map/ppermute | solution.py:53
  23.7 1.5 %collective-permute-start.7 = (bf16[96,1024]{1,0:T(8,128)(2,1)S(1)}, bf16[96,1024]{1,0:T(8,128)(2,1)S(1)}, u32[]{:S(2)}, u32[]{:S(2)}) collective-permute-start(bf16[96,1024]{1,0:T(8,128)(2,1)S(1)} %get-tuple-element.80), channel_id=1, source_target_pairs={{0,2},{1,3},{2,0},{3,1},{4,6},{5,7},{6,4},{7,5},{8,10},{9,11},{10,... | collective-permute-start | bytes 589832 | tf_op jit(solution)/shard_map/ppermute | solution.py:53
  25.7 2.7 %collective-permute-start.13 = (bf16[128,1024]{1,0:T(8,128)(2,1)S(1)}, bf16[128,1024]{1,0:T(8,128)(2,1)S(1)}, u32[]{:S(2)}, u32[]{:S(2)}) collective-permute-start(bf16[128,1024]{1,0:T(8,128)(2,1)S(1)} %get-tuple-element.87), channel_id=1, source_target_pairs={{0,12},{1,13},{2,14},{3,15},{4,8},{5,9},{6,10},{7,11},{8,4},{9,5},... | collective-permute-start | bytes 786440 | tf_op jit(solution)/shard_map/ppermute | solution.py:44
  29.8 3.7 %collective-permute-done.7.refs_6_ = bf16[96,1024]{1,0:T(8,128)(2,1)S(1)} collective-permute-done((bf16[96,1024]{1,0:T(8,128)(2,1)S(1)}, bf16[96,1024]{1,0:T(8,128)(2,1)S(1)}, u32[]{:S(2)}, u32[]{:S(2)}) %collective-permute-start.7) | collective-permute-done | bytes 196640 | tf_op jit(solution)/shard_map/ppermute | solution.py:53
  33.5 2.6 %shard_map.125 = (bf16[128,1024]{1,0:T(8,128)(2,1)S(1)}, bf16[128,1024]{1,0:T(8,128)(2,1)S(1)}, bf16[128,1024]{1,0:T(8,128)(2,1)S(1)}, bf16[128,1024]{1,0:T(8,128)(2,1)S(1)}) custom-call(bf16[96,1024]{1,0:T(8,128)(2,1)S(1)} %get-tuple-element.74.refs_0_, bf16[96,1024]{1,0:T(8,128)(2,1)S(1)} %collective-permute-done.3.refs_1_, ...), custom_call_target="tpu_custom_call" | custom-call | flops 2415919104 | bytes 65536 | tf_op jit(solution)/shard_map/pallas_call | solution.py:89
  38.2 1.5 %collective-permute-start.11 = (bf16[128,1024]{1,0:T(8,128)(2,1)S(1)}, bf16[128,1024]{1,0:T(8,128)(2,1)S(1)}, u32[]{:S(2)}, u32[]{:S(2)}) collective-permute-start(bf16[128,1024]{1,0:T(8,128)(2,1)S(1)} %get-tuple-element.85), channel_id=1, source_target_pairs={{0,3},{1,2},{2,1},{3,0},{4,7},{5,6},{6,5},{7,4},{8,11},{9,10},{10,... | collective-permute-start | bytes 786440 | tf_op jit(solution)/shard_map/ppermute | solution.py:53
  42.7 7.4 %collective-permute-done.12.refs_2_ = bf16[128,1024]{1,0:T(8,128)(2,1)S(1)} collective-permute-done((bf16[128,1024]{1,0:T(8,128)(2,1)S(1)}, bf16[128,1024]{1,0:T(8,128)(2,1)S(1)}, u32[]{:S(2)}, u32[]{:S(2)}) %collective-permute-start.12) | collective-permute-done | bytes 262176 | tf_op jit(solution)/shard_map/ppermute | solution.py:44
  50.1 1.5 %collective-permute-start.18 = (bf16[64,1024]{1,0:T(8,128)(2,1)S(1)}, bf16[64,1024]{1,0:T(8,128)(2,1)S(1)}, u32[]{:S(2)}, u32[]{:S(2)}) collective-permute-start(bf16[64,1024]{1,0:T(8,128)(2,1)S(1)} %get-tuple-element.106), channel_id=1, source_target_pairs={{0,2},{1,3},{2,0},{3,1},{4,6},{5,7},{6,4},{7,5},{8,10},{9,11},{10,... | collective-permute-start | bytes 393224 | tf_op jit(solution)/shard_map/ppermute | solution.py:53
  54.2 1.5 %collective-permute-start.23 = (bf16[128,1024]{1,0:T(8,128)(2,1)S(1)}, bf16[128,1024]{1,0:T(8,128)(2,1)S(1)}, u32[]{:S(2)}, u32[]{:S(2)}) collective-permute-start(bf16[128,1024]{1,0:T(8,128)(2,1)S(1)} %get-tuple-element.116), channel_id=1, source_target_pairs={{0,2},{1,3},{2,0},{3,1},{4,6},{5,7},{6,4},{7,5},{8,10},{9,11},{10,... | collective-permute-start | bytes 786440 | tf_op jit(solution)/shard_map/ppermute | solution.py:53
  56.8 3.5 %collective-permute-start.24 = (bf16[128,1024]{1,0:T(8,128)(2,1)S(1)}, bf16[128,1024]{1,0:T(8,128)(2,1)S(1)}, u32[]{:S(2)}, u32[]{:S(2)}) collective-permute-start(bf16[128,1024]{1,0:T(8,128)(2,1)S(1)} %get-tuple-element.117), channel_id=1, source_target_pairs={{0,3},{1,2},{2,1},{3,0},{4,7},{5,6},{6,5},{7,4},{8,11},{9,10},{10,... | collective-permute-start | bytes 786440 | tf_op jit(solution)/shard_map/ppermute | solution.py:53
  60.2 2.3 %shard_map.129 = (bf16[64,1024]{1,0:T(8,128)(2,1)S(1)}, bf16[64,1024]{1,0:T(8,128)(2,1)S(1)}, bf16[64,1024]{1,0:T(8,128)(2,1)S(1)}, bf16[64,1024]{1,0:T(8,128)(2,1)S(1)}) custom-call(bf16[96,1024]{1,0:T(8,128)(2,1)S(1)} %get-tuple-element.74.refs_0_, bf16[96,1024]{1,0:T(8,128)(2,1)S(1)} %collective-permute-done.3.refs_1_, ...), custom_call_target="tpu_custom_call" | custom-call | flops 536870912 | bytes 65536 | tf_op jit(solution)/shard_map/pallas_call | solution.py:89
  65.3 2.2 %collective-permute-done.23.refs_6_ = bf16[128,1024]{1,0:T(8,128)(2,1)S(1)} collective-permute-done((bf16[128,1024]{1,0:T(8,128)(2,1)S(1)}, bf16[128,1024]{1,0:T(8,128)(2,1)S(1)}, u32[]{:S(2)}, u32[]{:S(2)}) %collective-permute-start.23) | collective-permute-done | bytes 262176 | tf_op jit(solution)/shard_map/ppermute | solution.py:53
  67.5 2.3 %shard_map.131 = (bf16[64,1024]{1,0:T(8,128)(2,1)S(1)}, bf16[64,1024]{1,0:T(8,128)(2,1)S(1)}, bf16[64,1024]{1,0:T(8,128)(2,1)S(1)}, bf16[64,1024]{1,0:T(8,128)(2,1)S(1)}) custom-call(bf16[96,1024]{1,0:T(8,128)(2,1)S(1)} %get-tuple-element.74.refs_0_, bf16[96,1024]{1,0:T(8,128)(2,1)S(1)} %collective-permute-done.3.refs_1_, ...), custom_call_target="tpu_custom_call" | custom-call | flops 536870912 | bytes 65536 | tf_op jit(solution)/shard_map/pallas_call | solution.py:89
  69.8 1.6 %collective-permute-start.25 = (bf16[64,1024]{1,0:T(8,128)(2,1)S(1)}, bf16[64,1024]{1,0:T(8,128)(2,1)S(1)}, u32[]{:S(2)}, u32[]{:S(2)}) collective-permute-start(bf16[64,1024]{1,0:T(8,128)(2,1)S(1)} %get-tuple-element.123), channel_id=1, source_target_pairs={{0,1},{1,0},{2,3},{3,2},{4,5},{5,4},{6,7},{7,6},{8,9},{9,8},{10,11... | collective-permute-start | bytes 393224 | tf_op jit(solution)/shard_map/ppermute | solution.py:53
  74.1 2.1 %collective-permute-done.25.refs_3_ = bf16[64,1024]{1,0:T(8,128)(2,1)S(1)} collective-permute-done((bf16[64,1024]{1,0:T(8,128)(2,1)S(1)}, bf16[64,1024]{1,0:T(8,128)(2,1)S(1)}, u32[]{:S(2)}, u32[]{:S(2)}) %collective-permute-start.25) | collective-permute-done | bytes 131104 | tf_op jit(solution)/shard_map/ppermute | solution.py:53
  80.4 1.5 %collective-permute-start.30 = (bf16[64,1024]{1,0:T(8,128)(2,1)S(1)}, bf16[64,1024]{1,0:T(8,128)(2,1)S(1)}, u32[]{:S(2)}, u32[]{:S(2)}) collective-permute-start(bf16[64,1024]{1,0:T(8,128)(2,1)S(1)} %get-tuple-element.132), channel_id=1, source_target_pairs={{0,28},{1,29},{2,30},{3,31},{4,24},{5,25},{6,26},{7,27},{8,20},{9,... | collective-permute-start | bytes 393224 | tf_op jit(solution)/shard_map/ppermute | solution.py:68
  82.6 2.9 %collective-permute-done.32.refs_4_ = bf16[64,1024]{1,0:T(8,128)(2,1)S(1)} collective-permute-done((bf16[64,1024]{1,0:T(8,128)(2,1)S(1)}, bf16[64,1024]{1,0:T(8,128)(2,1)S(1)}, u32[]{:S(2)}, u32[]{:S(2)}) %collective-permute-start.32) | collective-permute-done | bytes 131104 | tf_op jit(solution)/shard_map/ppermute | solution.py:53
  88.2 5.7 %collective-permute-done.29.refs_0_ = bf16[64,1024]{1,0:T(8,128)(2,1)S(1)} collective-permute-done((bf16[64,1024]{1,0:T(8,128)(2,1)S(1)}, bf16[64,1024]{1,0:T(8,128)(2,1)S(1)}, u32[]{:S(2)}, u32[]{:S(2)}) %collective-permute-start.29) | collective-permute-done | bytes 131104 | tf_op jit(solution)/shard_map/ppermute | solution.py:68
  (79 shorter events, 29.1 us)
Async XLA Ops:
  2.6 10.6 %collective-permute-start.2 = (bf16[64,1152]{1,0:T(8,128)(2,1)}, bf16[64,1152]{1,0:T(8,128)(2,1)S(1)}, u32[]{:S(2)}, u32[]{:S(2)}) collective-permute-start(bf16[64,1152]{1,0:T(8,128)(2,1)} %shard_map.122.refs_0_.refs_3_.refs_1_), channel_id=1, source_target_pairs={{0,4},{1,5},{2,6},{3,7},{4,0},{5,1},{6,2},{7,3},{8,12},{9,13},{10,... | collective-permute-start | bytes 442376 | tf_op jit(solution)/shard_map/ppermute | solution.py:44
  5.7 10.7 %collective-permute-start.1 = (bf16[64,1152]{1,0:T(8,128)(2,1)}, bf16[64,1152]{1,0:T(8,128)(2,1)S(1)}, u32[]{:S(2)}, u32[]{:S(2)}) collective-permute-start(bf16[64,1152]{1,0:T(8,128)(2,1)} %shard_map.122.refs_0_.refs_3_.refs_1_), channel_id=1, source_target_pairs={{0,12},{1,13},{2,14},{3,15},{4,8},{5,9},{6,10},{7,11},{8,4},{9,5},... | collective-permute-start | bytes 442376 | tf_op jit(solution)/shard_map/ppermute | solution.py:44
  8.2 13.4 %collective-permute-start = (bf16[64,1152]{1,0:T(8,128)(2,1)}, bf16[64,1152]{1,0:T(8,128)(2,1)S(1)}, u32[]{:S(2)}, u32[]{:S(2)}) collective-permute-start(bf16[64,1152]{1,0:T(8,128)(2,1)} %shard_map.122.refs_0_.refs_3_.refs_1_), channel_id=1, source_target_pairs={{0,8},{1,9},{2,10},{3,11},{4,12},{5,13},{6,14},{7,15},{8,0},{9,1},... | collective-permute-start | bytes 442376 | tf_op jit(solution)/shard_map/ppermute | solution.py:44
  10.1 15.0 %collective-permute-start.3 = (bf16[96,1024]{1,0:T(8,128)(2,1)S(1)}, bf16[96,1024]{1,0:T(8,128)(2,1)S(1)}, u32[]{:S(2)}, u32[]{:S(2)}) collective-permute-start(bf16[96,1024]{1,0:T(8,128)(2,1)S(1)} %get-tuple-element.75), channel_id=1, source_target_pairs={{0,1},{1,0},{2,3},{3,2},{4,5},{5,4},{6,7},{7,6},{8,9},{9,8},{10,11... | collective-permute-start | bytes 589832 | tf_op jit(solution)/shard_map/ppermute | solution.py:53
  11.7 14.0 %collective-permute-start.4 = (bf16[96,1024]{1,0:T(8,128)(2,1)S(1)}, bf16[96,1024]{1,0:T(8,128)(2,1)S(1)}, u32[]{:S(2)}, u32[]{:S(2)}) collective-permute-start(bf16[96,1024]{1,0:T(8,128)(2,1)S(1)} %get-tuple-element.76), channel_id=1, source_target_pairs={{0,2},{1,3},{2,0},{3,1},{4,6},{5,7},{6,4},{7,5},{8,10},{9,11},{10,... | collective-permute-start | bytes 589832 | tf_op jit(solution)/shard_map/ppermute | solution.py:53
  13.2 12.4 %collective-permute-start.5 = (bf16[96,1024]{1,0:T(8,128)(2,1)S(1)}, bf16[96,1024]{1,0:T(8,128)(2,1)S(1)}, u32[]{:S(2)}, u32[]{:S(2)}) collective-permute-start(bf16[96,1024]{1,0:T(8,128)(2,1)S(1)} %get-tuple-element.77), channel_id=1, source_target_pairs={{0,3},{1,2},{2,1},{3,0},{4,7},{5,6},{6,5},{7,4},{8,11},{9,10},{10,... | collective-permute-start | bytes 589832 | tf_op jit(solution)/shard_map/ppermute | solution.py:53
  23.7 9.8 %collective-permute-start.7 = (bf16[96,1024]{1,0:T(8,128)(2,1)S(1)}, bf16[96,1024]{1,0:T(8,128)(2,1)S(1)}, u32[]{:S(2)}, u32[]{:S(2)}) collective-permute-start(bf16[96,1024]{1,0:T(8,128)(2,1)S(1)} %get-tuple-element.80), channel_id=1, source_target_pairs={{0,2},{1,3},{2,0},{3,1},{4,6},{5,7},{6,4},{7,5},{8,10},{9,11},{10,... | collective-permute-start | bytes 589832 | tf_op jit(solution)/shard_map/ppermute | solution.py:53
  25.2 8.3 %collective-permute-start.8 = (bf16[96,1024]{1,0:T(8,128)(2,1)S(1)}, bf16[96,1024]{1,0:T(8,128)(2,1)S(1)}, u32[]{:S(2)}, u32[]{:S(2)}) collective-permute-start(bf16[96,1024]{1,0:T(8,128)(2,1)S(1)} %get-tuple-element.81), channel_id=1, source_target_pairs={{0,3},{1,2},{2,1},{3,0},{4,7},{5,6},{6,5},{7,4},{8,11},{9,10},{10,... | collective-permute-start | bytes 589832 | tf_op jit(solution)/shard_map/ppermute | solution.py:53
  25.7 12.5 %collective-permute-start.14 = (bf16[128,1024]{1,0:T(8,128)(2,1)S(1)}, bf16[128,1024]{1,0:T(8,128)(2,1)S(1)}, u32[]{:S(2)}, u32[]{:S(2)}) collective-permute-start(bf16[128,1024]{1,0:T(8,128)(2,1)S(1)} %get-tuple-element.87), channel_id=1, source_target_pairs={{0,4},{1,5},{2,6},{3,7},{4,0},{5,1},{6,2},{7,3},{8,12},{9,13},{10,... | collective-permute-start | bytes 786440 | tf_op jit(solution)/shard_map/ppermute | solution.py:44
  25.7 15.5 %collective-permute-start.13 = (bf16[128,1024]{1,0:T(8,128)(2,1)S(1)}, bf16[128,1024]{1,0:T(8,128)(2,1)S(1)}, u32[]{:S(2)}, u32[]{:S(2)}) collective-permute-start(bf16[128,1024]{1,0:T(8,128)(2,1)S(1)} %get-tuple-element.87), channel_id=1, source_target_pairs={{0,12},{1,13},{2,14},{3,15},{4,8},{5,9},{6,10},{7,11},{8,4},{9,5},... | collective-permute-start | bytes 786440 | tf_op jit(solution)/shard_map/ppermute | solution.py:44
  29.8 20.3 %collective-permute-start.12 = (bf16[128,1024]{1,0:T(8,128)(2,1)S(1)}, bf16[128,1024]{1,0:T(8,128)(2,1)S(1)}, u32[]{:S(2)}, u32[]{:S(2)}) collective-permute-start(bf16[128,1024]{1,0:T(8,128)(2,1)S(1)} %get-tuple-element.87), channel_id=1, source_target_pairs={{0,8},{1,9},{2,10},{3,11},{4,12},{5,13},{6,14},{7,15},{8,0},{9,1},... | collective-permute-start | bytes 786440 | tf_op jit(solution)/shard_map/ppermute | solution.py:44
  36.1 15.5 %collective-permute-start.9 = (bf16[128,1024]{1,0:T(8,128)(2,1)S(1)}, bf16[128,1024]{1,0:T(8,128)(2,1)S(1)}, u32[]{:S(2)}, u32[]{:S(2)}) collective-permute-start(bf16[128,1024]{1,0:T(8,128)(2,1)S(1)} %get-tuple-element.83), channel_id=1, source_target_pairs={{0,1},{1,0},{2,3},{3,2},{4,5},{5,4},{6,7},{7,6},{8,9},{9,8},{10,11... | collective-permute-start | bytes 786440 | tf_op jit(solution)/shard_map/ppermute | solution.py:53
  37.3 15.7 %collective-permute-start.10 = (bf16[128,1024]{1,0:T(8,128)(2,1)S(1)}, bf16[128,1024]{1,0:T(8,128)(2,1)S(1)}, u32[]{:S(2)}, u32[]{:S(2)}) collective-permute-start(bf16[128,1024]{1,0:T(8,128)(2,1)S(1)} %get-tuple-element.84), channel_id=1, source_target_pairs={{0,2},{1,3},{2,0},{3,1},{4,6},{5,7},{6,4},{7,5},{8,10},{9,11},{10,... | collective-permute-start | bytes 786440 | tf_op jit(solution)/shard_map/ppermute | solution.py:53
  38.2 15.5 %collective-permute-start.11 = (bf16[128,1024]{1,0:T(8,128)(2,1)S(1)}, bf16[128,1024]{1,0:T(8,128)(2,1)S(1)}, u32[]{:S(2)}, u32[]{:S(2)}) collective-permute-start(bf16[128,1024]{1,0:T(8,128)(2,1)S(1)} %get-tuple-element.85), channel_id=1, source_target_pairs={{0,3},{1,2},{2,1},{3,0},{4,7},{5,6},{6,5},{7,4},{8,11},{9,10},{10,... | collective-permute-start | bytes 786440 | tf_op jit(solution)/shard_map/ppermute | solution.py:53
  41.2 15.4 %collective-permute-start.17 = (bf16[64,1024]{1,0:T(8,128)(2,1)S(1)}, bf16[64,1024]{1,0:T(8,128)(2,1)S(1)}, u32[]{:S(2)}, u32[]{:S(2)}) collective-permute-start(bf16[64,1024]{1,0:T(8,128)(2,1)S(1)} %get-tuple-element.105), channel_id=1, source_target_pairs={{0,1},{1,0},{2,3},{3,2},{4,5},{5,4},{6,7},{7,6},{8,9},{9,8},{10,11... | collective-permute-start | bytes 393224 | tf_op jit(solution)/shard_map/ppermute | solution.py:53
  51.6 8.6 %collective-permute-start.19 = (bf16[64,1024]{1,0:T(8,128)(2,1)S(1)}, bf16[64,1024]{1,0:T(8,128)(2,1)S(1)}, u32[]{:S(2)}, u32[]{:S(2)}) collective-permute-start(bf16[64,1024]{1,0:T(8,128)(2,1)S(1)} %get-tuple-element.107), channel_id=1, source_target_pairs={{0,3},{1,2},{2,1},{3,0},{4,7},{5,6},{6,5},{7,4},{8,11},{9,10},{10,... | collective-permute-start | bytes 393224 | tf_op jit(solution)/shard_map/ppermute | solution.py:53
  53.6 10.3 %collective-permute-start.22 = (bf16[128,1024]{1,0:T(8,128)(2,1)S(1)}, bf16[128,1024]{1,0:T(8,128)(2,1)S(1)}, u32[]{:S(2)}, u32[]{:S(2)}) collective-permute-start(bf16[128,1024]{1,0:T(8,128)(2,1)S(1)} %get-tuple-element.115), channel_id=1, source_target_pairs={{0,1},{1,0},{2,3},{3,2},{4,5},{5,4},{6,7},{7,6},{8,9},{9,8},{10,11... | collective-permute-start | bytes 786440 | tf_op jit(solution)/shard_map/ppermute | solution.py:53
  54.2 13.2 %collective-permute-start.23 = (bf16[128,1024]{1,0:T(8,128)(2,1)S(1)}, bf16[128,1024]{1,0:T(8,128)(2,1)S(1)}, u32[]{:S(2)}, u32[]{:S(2)}) collective-permute-start(bf16[128,1024]{1,0:T(8,128)(2,1)S(1)} %get-tuple-element.116), channel_id=1, source_target_pairs={{0,2},{1,3},{2,0},{3,1},{4,6},{5,7},{6,4},{7,5},{8,10},{9,11},{10,... | collective-permute-start | bytes 786440 | tf_op jit(solution)/shard_map/ppermute | solution.py:53
  56.8 10.7 %collective-permute-start.24 = (bf16[128,1024]{1,0:T(8,128)(2,1)S(1)}, bf16[128,1024]{1,0:T(8,128)(2,1)S(1)}, u32[]{:S(2)}, u32[]{:S(2)}) collective-permute-start(bf16[128,1024]{1,0:T(8,128)(2,1)S(1)} %get-tuple-element.117), channel_id=1, source_target_pairs={{0,3},{1,2},{2,1},{3,0},{4,7},{5,6},{6,5},{7,4},{8,11},{9,10},{10,... | collective-permute-start | bytes 786440 | tf_op jit(solution)/shard_map/ppermute | solution.py:53
  62.5 10.8 %collective-permute-start.21 = (f32[64,1024]{1,0:T(8,128)S(1)}, f32[64,1024]{1,0:T(8,128)S(1)}, u32[]{:S(2)}, u32[]{:S(2)}) collective-permute-start(f32[64,1024]{1,0:T(8,128)S(1)} %get-tuple-element.114), channel_id=1, source_target_pairs={{0,16},{1,17},{2,18},{3,19},{4,20},{5,21},{6,22},{7,23},{8,24},{9,... | collective-permute-start | bytes 786440 | tf_op jit(solution)/shard_map/ppermute | solution.py:68
  64.0 8.7 %collective-permute-start.16 = (bf16[64,1024]{1,0:T(8,128)(2,1)S(1)}, bf16[64,1024]{1,0:T(8,128)(2,1)S(1)}, u32[]{:S(2)}, u32[]{:S(2)}) collective-permute-start(bf16[64,1024]{1,0:T(8,128)(2,1)S(1)} %get-tuple-element.101), channel_id=1, source_target_pairs={{0,28},{1,29},{2,30},{3,31},{4,24},{5,25},{6,26},{7,27},{8,20},{9,... | collective-permute-start | bytes 393224 | tf_op jit(solution)/shard_map/ppermute | solution.py:68
  67.4 11.5 %collective-permute-start.28 = (bf16[128,1024]{1,0:T(8,128)(2,1)S(1)}, bf16[128,1024]{1,0:T(8,128)(2,1)S(1)}, u32[]{:S(2)}, u32[]{:S(2)}) collective-permute-start(bf16[128,1024]{1,0:T(8,128)(2,1)S(1)} %get-tuple-element.126), channel_id=1, source_target_pairs={{0,16},{1,17},{2,18},{3,19},{4,20},{5,21},{6,22},{7,23},{8,24},{9,... | collective-permute-start | bytes 786440 | tf_op jit(solution)/shard_map/ppermute | solution.py:68
  71.3 8.6 %collective-permute-start.26 = (bf16[64,1024]{1,0:T(8,128)(2,1)S(1)}, bf16[64,1024]{1,0:T(8,128)(2,1)S(1)}, u32[]{:S(2)}, u32[]{:S(2)}) collective-permute-start(bf16[64,1024]{1,0:T(8,128)(2,1)S(1)} %get-tuple-element.124), channel_id=1, source_target_pairs={{0,2},{1,3},{2,0},{3,1},{4,6},{5,7},{6,4},{7,5},{8,10},{9,11},{10,... | collective-permute-start | bytes 393224 | tf_op jit(solution)/shard_map/ppermute | solution.py:53
  81.9 12.0 %collective-permute-start.29 = (bf16[64,1024]{1,0:T(8,128)(2,1)S(1)}, bf16[64,1024]{1,0:T(8,128)(2,1)S(1)}, u32[]{:S(2)}, u32[]{:S(2)}) collective-permute-start(bf16[64,1024]{1,0:T(8,128)(2,1)S(1)} %get-tuple-element.131), channel_id=1, source_target_pairs={{0,24},{1,25},{2,26},{3,27},{4,28},{5,29},{6,30},{7,31},{8,16},{9,... | collective-permute-start | bytes 393224 | tf_op jit(solution)/shard_map/ppermute | solution.py:68
  (21 other events, 177.5 us)

commit v5 on v4

--- a/solution.py
+++ b/solution.py
@@ -181,9 +181,11 @@
     copies = fetches(far, near, semaphores)
     lists, (fx, gain) = near[:4], near[4:]
     width = fx.shape[1]
-    for copy in copies:
+    for copy in copies[4:]:
         copy.wait()
     f_pack[:, pl.ds(0, width)] = normed_rows(fx[...], gain[...])
+    for copy in copies[:4]:
+        copy.wait()
     fill_table(experts, table, lists)
     f_pack[:, pl.ds(width, table.shape[0])] = table[...].T.astype(BF16)
 

time: 95 us -> 95.1 us (level)
  no operation moved by 1% of the time
where the time goes in v5:
time: 95.1 us; the launch traced here: 94.9 us
  starting transfers between devices  40.8 us (43%)
  waiting for transfers between devices  37.4 us (39%)
  Pallas kernels  15 us (16%)
  local copies, waits for them, and re-layouts  0.96 us (1%)
    ppermute x21, starting transfers between devices, over_inner(): return lax.ppermute(block, 'expert', route)  27.8 us
    ppermute x6, waiting for transfers between devices, over_outer(): return lax.ppermute(block, 'expert', route)  16.3 us
    pallas_call x13, Pallas kernels, call(): pl.pallas_call(kernel, out_shape=out_shape, in_specs=[near] * len(args) +...  15 us
    ppermute x21, waiting for transfers between devices, over_inner(): return lax.ppermute(block, 'expert', route)  12.6 us
    ppermute x9, waiting for transfers between devices, home_and_along(): return lax.ppermute(block, ('segment', 'expert'), route)  8.4 us
    ppermute x6, starting transfers between devices, over_outer(): return lax.ppermute(block, 'expert', route)  8.36 us
    ppermute x9, starting transfers between devices, home_and_along(): return lax.ppermute(block, ('segment', 'expert'), route)  4.64 us
  transfers between devices with their start and end apart: 36, of which 15 were waited for; matrix products, arithmetic and copies ran while one was open for 0% of the time, Pallas kernels for 13%

profile of v5, /device:TPU:0, one launch (start us, length us, event | category | flops | bytes accessed | tf_op | source)
XLA Modules:
  0.0 94.9 jit_solution(252065608265349491)
XLA Ops:
  0.7 2.1 %shard_map.122.refs_0_.refs_3_.refs_1_ = bf16[64,1152]{1,0:T(8,128)(2,1)} custom-call(s32[8,64]{1,0:T(8,128)} %bitcast.33, f32[8,64]{1,0:T(8,128)} %bitcast.34, s32[8,64]{1,0:T(8,128)} %bitcast.35, f32[8,64]{1,0:T(8,128)} %bitcast.36, bf16[64,1024]{1,0:T(8,128)(2,1)} %bitcast.29, f32[1,1024]{1,0:T(1,128)} %refs_6_.3), custom_call_target="tpu_custom_call" | custom-call | flops 2147483648 | bytes 65536 | tf_op jit(solution)/shard_map/pallas_call | solution.py:89
  2.7 3.1 %collective-permute-start.2 = (bf16[64,1152]{1,0:T(8,128)(2,1)}, bf16[64,1152]{1,0:T(8,128)(2,1)S(1)}, u32[]{:S(2)}, u32[]{:S(2)}) collective-permute-start(bf16[64,1152]{1,0:T(8,128)(2,1)} %shard_map.122.refs_0_.refs_3_.refs_1_), channel_id=1, source_target_pairs={{0,4},{1,5},{2,6},{3,7},{4,0},{5,1},{6,2},{7,3},{8,12},{9,13},{10,... | collective-permute-start | bytes 442376 | tf_op jit(solution)/shard_map/ppermute | solution.py:44
  5.8 2.5 %collective-permute-start.1 = (bf16[64,1152]{1,0:T(8,128)(2,1)}, bf16[64,1152]{1,0:T(8,128)(2,1)S(1)}, u32[]{:S(2)}, u32[]{:S(2)}) collective-permute-start(bf16[64,1152]{1,0:T(8,128)(2,1)} %shard_map.122.refs_0_.refs_3_.refs_1_), channel_id=1, source_target_pairs={{0,12},{1,13},{2,14},{3,15},{4,8},{5,9},{6,10},{7,11},{8,4},{9,5},... | collective-permute-start | bytes 442376 | tf_op jit(solution)/shard_map/ppermute | solution.py:44
  10.3 1.6 %collective-permute-start.3 = (bf16[96,1024]{1,0:T(8,128)(2,1)S(1)}, bf16[96,1024]{1,0:T(8,128)(2,1)S(1)}, u32[]{:S(2)}, u32[]{:S(2)}) collective-permute-start(bf16[96,1024]{1,0:T(8,128)(2,1)S(1)} %get-tuple-element.75), channel_id=1, source_target_pairs={{0,1},{1,0},{2,3},{3,2},{4,5},{5,4},{6,7},{7,6},{8,9},{9,8},{10,11... | collective-permute-start | bytes 589832 | tf_op jit(solution)/shard_map/ppermute | solution.py:53
  11.8 1.5 %collective-permute-start.4 = (bf16[96,1024]{1,0:T(8,128)(2,1)S(1)}, bf16[96,1024]{1,0:T(8,128)(2,1)S(1)}, u32[]{:S(2)}, u32[]{:S(2)}) collective-permute-start(bf16[96,1024]{1,0:T(8,128)(2,1)S(1)} %get-tuple-element.76), channel_id=1, source_target_pairs={{0,2},{1,3},{2,0},{3,1},{4,6},{5,7},{6,4},{7,5},{8,10},{9,11},{10,... | collective-permute-start | bytes 589832 | tf_op jit(solution)/shard_map/ppermute | solution.py:53
  13.9 2.6 %collective-permute-done.1.refs_2_.refs_5_.refs_1_ = bf16[64,1152]{1,0:T(8,128)(2,1)S(1)} collective-permute-done((bf16[64,1152]{1,0:T(8,128)(2,1)}, bf16[64,1152]{1,0:T(8,128)(2,1)S(1)}, u32[]{:S(2)}, u32[]{:S(2)}) %collective-permute-start.1) | collective-permute-done | bytes 147488 | tf_op jit(solution)/shard_map/ppermute | solution.py:44
  16.5 5.2 %collective-permute-done.refs_1_.refs_4_.refs_0_ = bf16[64,1152]{1,0:T(8,128)(2,1)S(1)} collective-permute-done((bf16[64,1152]{1,0:T(8,128)(2,1)}, bf16[64,1152]{1,0:T(8,128)(2,1)S(1)}, u32[]{:S(2)}, u32[]{:S(2)}) %collective-permute-start) | collective-permute-done | bytes 147488 | tf_op jit(solution)/shard_map/ppermute | solution.py:44
  22.2 1.6 %collective-permute-start.6 = (bf16[96,1024]{1,0:T(8,128)(2,1)S(1)}, bf16[96,1024]{1,0:T(8,128)(2,1)S(1)}, u32[]{:S(2)}, u32[]{:S(2)}) collective-permute-start(bf16[96,1024]{1,0:T(8,128)(2,1)S(1)} %get-tuple-element.79), channel_id=1, source_target_pairs={{0,1},{1,0},{2,3},{3,2},{4,5},{5,4},{6,7},{7,6},{8,9},{9,8},{10,11... | collective-permute-start | bytes 589832 | tf_op jit(solution)/shard_map/ppermute | solution.py:53
  23.8 1.5 %collective-permute-start.7 = (bf16[96,1024]{1,0:T(8,128)(2,1)S(1)}, bf16[96,1024]{1,0:T(8,128)(2,1)S(1)}, u32[]{:S(2)}, u32[]{:S(2)}) collective-permute-start(bf16[96,1024]{1,0:T(8,128)(2,1)S(1)} %get-tuple-element.80), channel_id=1, source_target_pairs={{0,2},{1,3},{2,0},{3,1},{4,6},{5,7},{6,4},{7,5},{8,10},{9,11},{10,... | collective-permute-start | bytes 589832 | tf_op jit(solution)/shard_map/ppermute | solution.py:53
  25.8 2.7 %collective-permute-start.13 = (bf16[128,1024]{1,0:T(8,128)(2,1)S(1)}, bf16[128,1024]{1,0:T(8,128)(2,1)S(1)}, u32[]{:S(2)}, u32[]{:S(2)}) collective-permute-start(bf16[128,1024]{1,0:T(8,128)(2,1)S(1)} %get-tuple-element.87), channel_id=1, source_target_pairs={{0,12},{1,13},{2,14},{3,15},{4,8},{5,9},{6,10},{7,11},{8,4},{9,5},... | collective-permute-start | bytes 786440 | tf_op jit(solution)/shard_map/ppermute | solution.py:44
  29.9 3.7 %collective-permute-done.7.refs_6_ = bf16[96,1024]{1,0:T(8,128)(2,1)S(1)} collective-permute-done((bf16[96,1024]{1,0:T(8,128)(2,1)S(1)}, bf16[96,1024]{1,0:T(8,128)(2,1)S(1)}, u32[]{:S(2)}, u32[]{:S(2)}) %collective-permute-start.7) | collective-permute-done | bytes 196640 | tf_op jit(solution)/shard_map/ppermute | solution.py:53
  33.6 2.6 %shard_map.125 = (bf16[128,1024]{1,0:T(8,128)(2,1)S(1)}, bf16[128,1024]{1,0:T(8,128)(2,1)S(1)}, bf16[128,1024]{1,0:T(8,128)(2,1)S(1)}, bf16[128,1024]{1,0:T(8,128)(2,1)S(1)}) custom-call(bf16[96,1024]{1,0:T(8,128)(2,1)S(1)} %get-tuple-element.74.refs_0_, bf16[96,1024]{1,0:T(8,128)(2,1)S(1)} %collective-permute-done.3.refs_1_, ...), custom_call_target="tpu_custom_call" | custom-call | flops 2415919104 | bytes 65536 | tf_op jit(solution)/shard_map/pallas_call | solution.py:89
  38.3 1.5 %collective-permute-start.11 = (bf16[128,1024]{1,0:T(8,128)(2,1)S(1)}, bf16[128,1024]{1,0:T(8,128)(2,1)S(1)}, u32[]{:S(2)}, u32[]{:S(2)}) collective-permute-start(bf16[128,1024]{1,0:T(8,128)(2,1)S(1)} %get-tuple-element.85), channel_id=1, source_target_pairs={{0,3},{1,2},{2,1},{3,0},{4,7},{5,6},{6,5},{7,4},{8,11},{9,10},{10,... | collective-permute-start | bytes 786440 | tf_op jit(solution)/shard_map/ppermute | solution.py:53
  42.8 7.4 %collective-permute-done.12.refs_2_ = bf16[128,1024]{1,0:T(8,128)(2,1)S(1)} collective-permute-done((bf16[128,1024]{1,0:T(8,128)(2,1)S(1)}, bf16[128,1024]{1,0:T(8,128)(2,1)S(1)}, u32[]{:S(2)}, u32[]{:S(2)}) %collective-permute-start.12) | collective-permute-done | bytes 262176 | tf_op jit(solution)/shard_map/ppermute | solution.py:44
  50.2 1.5 %collective-permute-start.18 = (bf16[64,1024]{1,0:T(8,128)(2,1)S(1)}, bf16[64,1024]{1,0:T(8,128)(2,1)S(1)}, u32[]{:S(2)}, u32[]{:S(2)}) collective-permute-start(bf16[64,1024]{1,0:T(8,128)(2,1)S(1)} %get-tuple-element.106), channel_id=1, source_target_pairs={{0,2},{1,3},{2,0},{3,1},{4,6},{5,7},{6,4},{7,5},{8,10},{9,11},{10,... | collective-permute-start | bytes 393224 | tf_op jit(solution)/shard_map/ppermute | solution.py:53
  56.9 3.5 %collective-permute-start.24 = (bf16[128,1024]{1,0:T(8,128)(2,1)S(1)}, bf16[128,1024]{1,0:T(8,128)(2,1)S(1)}, u32[]{:S(2)}, u32[]{:S(2)}) collective-permute-start(bf16[128,1024]{1,0:T(8,128)(2,1)S(1)} %get-tuple-element.117), channel_id=1, source_target_pairs={{0,3},{1,2},{2,1},{3,0},{4,7},{5,6},{6,5},{7,4},{8,11},{9,10},{10,... | collective-permute-start | bytes 786440 | tf_op jit(solution)/shard_map/ppermute | solution.py:53
  60.3 2.3 %shard_map.129 = (bf16[64,1024]{1,0:T(8,128)(2,1)S(1)}, bf16[64,1024]{1,0:T(8,128)(2,1)S(1)}, bf16[64,1024]{1,0:T(8,128)(2,1)S(1)}, bf16[64,1024]{1,0:T(8,128)(2,1)S(1)}) custom-call(bf16[96,1024]{1,0:T(8,128)(2,1)S(1)} %get-tuple-element.74.refs_0_, bf16[96,1024]{1,0:T(8,128)(2,1)S(1)} %collective-permute-done.3.refs_1_, ...), custom_call_target="tpu_custom_call" | custom-call | flops 536870912 | bytes 65536 | tf_op jit(solution)/shard_map/pallas_call | solution.py:89
  65.4 2.2 %collective-permute-done.23.refs_6_ = bf16[128,1024]{1,0:T(8,128)(2,1)S(1)} collective-permute-done((bf16[128,1024]{1,0:T(8,128)(2,1)S(1)}, bf16[128,1024]{1,0:T(8,128)(2,1)S(1)}, u32[]{:S(2)}, u32[]{:S(2)}) %collective-permute-start.23) | collective-permute-done | bytes 262176 | tf_op jit(solution)/shard_map/ppermute | solution.py:53
  67.6 2.3 %shard_map.131 = (bf16[64,1024]{1,0:T(8,128)(2,1)S(1)}, bf16[64,1024]{1,0:T(8,128)(2,1)S(1)}, bf16[64,1024]{1,0:T(8,128)(2,1)S(1)}, bf16[64,1024]{1,0:T(8,128)(2,1)S(1)}) custom-call(bf16[96,1024]{1,0:T(8,128)(2,1)S(1)} %get-tuple-element.74.refs_0_, bf16[96,1024]{1,0:T(8,128)(2,1)S(1)} %collective-permute-done.3.refs_1_, ...), custom_call_target="tpu_custom_call" | custom-call | flops 536870912 | bytes 65536 | tf_op jit(solution)/shard_map/pallas_call | solution.py:89
  69.9 1.6 %collective-permute-start.25 = (bf16[64,1024]{1,0:T(8,128)(2,1)S(1)}, bf16[64,1024]{1,0:T(8,128)(2,1)S(1)}, u32[]{:S(2)}, u32[]{:S(2)}) collective-permute-start(bf16[64,1024]{1,0:T(8,128)(2,1)S(1)} %get-tuple-element.123), channel_id=1, source_target_pairs={{0,1},{1,0},{2,3},{3,2},{4,5},{5,4},{6,7},{7,6},{8,9},{9,8},{10,11... | collective-permute-start | bytes 393224 | tf_op jit(solution)/shard_map/ppermute | solution.py:53
  74.2 2.1 %collective-permute-done.25.refs_3_ = bf16[64,1024]{1,0:T(8,128)(2,1)S(1)} collective-permute-done((bf16[64,1024]{1,0:T(8,128)(2,1)S(1)}, bf16[64,1024]{1,0:T(8,128)(2,1)S(1)}, u32[]{:S(2)}, u32[]{:S(2)}) %collective-permute-start.25) | collective-permute-done | bytes 131104 | tf_op jit(solution)/shard_map/ppermute | solution.py:53
  80.5 1.5 %collective-permute-start.30 = (bf16[64,1024]{1,0:T(8,128)(2,1)S(1)}, bf16[64,1024]{1,0:T(8,128)(2,1)S(1)}, u32[]{:S(2)}, u32[]{:S(2)}) collective-permute-start(bf16[64,1024]{1,0:T(8,128)(2,1)S(1)} %get-tuple-element.132), channel_id=1, source_target_pairs={{0,28},{1,29},{2,30},{3,31},{4,24},{5,25},{6,26},{7,27},{8,20},{9,... | collective-permute-start | bytes 393224 | tf_op jit(solution)/shard_map/ppermute | solution.py:68
  82.7 2.8 %collective-permute-done.32.refs_4_ = bf16[64,1024]{1,0:T(8,128)(2,1)S(1)} collective-permute-done((bf16[64,1024]{1,0:T(8,128)(2,1)S(1)}, bf16[64,1024]{1,0:T(8,128)(2,1)S(1)}, u32[]{:S(2)}, u32[]{:S(2)}) %collective-permute-start.32) | collective-permute-done | bytes 131104 | tf_op jit(solution)/shard_map/ppermute | solution.py:53
  88.2 5.7 %collective-permute-done.29.refs_0_ = bf16[64,1024]{1,0:T(8,128)(2,1)S(1)} collective-permute-done((bf16[64,1024]{1,0:T(8,128)(2,1)S(1)}, bf16[64,1024]{1,0:T(8,128)(2,1)S(1)}, u32[]{:S(2)}, u32[]{:S(2)}) %collective-permute-start.29) | collective-permute-done | bytes 131104 | tf_op jit(solution)/shard_map/ppermute | solution.py:68
  (79 shorter events, 29.1 us)
Async XLA Ops:
  2.7 10.6 %collective-permute-start.2 = (bf16[64,1152]{1,0:T(8,128)(2,1)}, bf16[64,1152]{1,0:T(8,128)(2,1)S(1)}, u32[]{:S(2)}, u32[]{:S(2)}) collective-permute-start(bf16[64,1152]{1,0:T(8,128)(2,1)} %shard_map.122.refs_0_.refs_3_.refs_1_), channel_id=1, source_target_pairs={{0,4},{1,5},{2,6},{3,7},{4,0},{5,1},{6,2},{7,3},{8,12},{9,13},{10,... | collective-permute-start | bytes 442376 | tf_op jit(solution)/shard_map/ppermute | solution.py:44
  5.8 10.7 %collective-permute-start.1 = (bf16[64,1152]{1,0:T(8,128)(2,1)}, bf16[64,1152]{1,0:T(8,128)(2,1)S(1)}, u32[]{:S(2)}, u32[]{:S(2)}) collective-permute-start(bf16[64,1152]{1,0:T(8,128)(2,1)} %shard_map.122.refs_0_.refs_3_.refs_1_), channel_id=1, source_target_pairs={{0,12},{1,13},{2,14},{3,15},{4,8},{5,9},{6,10},{7,11},{8,4},{9,5},... | collective-permute-start | bytes 442376 | tf_op jit(solution)/shard_map/ppermute | solution.py:44
  8.3 13.4 %collective-permute-start = (bf16[64,1152]{1,0:T(8,128)(2,1)}, bf16[64,1152]{1,0:T(8,128)(2,1)S(1)}, u32[]{:S(2)}, u32[]{:S(2)}) collective-permute-start(bf16[64,1152]{1,0:T(8,128)(2,1)} %shard_map.122.refs_0_.refs_3_.refs_1_), channel_id=1, source_target_pairs={{0,8},{1,9},{2,10},{3,11},{4,12},{5,13},{6,14},{7,15},{8,0},{9,1},... | collective-permute-start | bytes 442376 | tf_op jit(solution)/shard_map/ppermute | solution.py:44
  10.3 15.1 %collective-permute-start.3 = (bf16[96,1024]{1,0:T(8,128)(2,1)S(1)}, bf16[96,1024]{1,0:T(8,128)(2,1)S(1)}, u32[]{:S(2)}, u32[]{:S(2)}) collective-permute-start(bf16[96,1024]{1,0:T(8,128)(2,1)S(1)} %get-tuple-element.75), channel_id=1, source_target_pairs={{0,1},{1,0},{2,3},{3,2},{4,5},{5,4},{6,7},{7,6},{8,9},{9,8},{10,11... | collective-permute-start | bytes 589832 | tf_op jit(solution)/shard_map/ppermute | solution.py:53
  11.8 14.0 %collective-permute-start.4 = (bf16[96,1024]{1,0:T(8,128)(2,1)S(1)}, bf16[96,1024]{1,0:T(8,128)(2,1)S(1)}, u32[]{:S(2)}, u32[]{:S(2)}) collective-permute-start(bf16[96,1024]{1,0:T(8,128)(2,1)S(1)} %get-tuple-element.76), channel_id=1, source_target_pairs={{0,2},{1,3},{2,0},{3,1},{4,6},{5,7},{6,4},{7,5},{8,10},{9,11},{10,... | collective-permute-start | bytes 589832 | tf_op jit(solution)/shard_map/ppermute | solution.py:53
  13.3 12.4 %collective-permute-start.5 = (bf16[96,1024]{1,0:T(8,128)(2,1)S(1)}, bf16[96,1024]{1,0:T(8,128)(2,1)S(1)}, u32[]{:S(2)}, u32[]{:S(2)}) collective-permute-start(bf16[96,1024]{1,0:T(8,128)(2,1)S(1)} %get-tuple-element.77), channel_id=1, source_target_pairs={{0,3},{1,2},{2,1},{3,0},{4,7},{5,6},{6,5},{7,4},{8,11},{9,10},{10,... | collective-permute-start | bytes 589832 | tf_op jit(solution)/shard_map/ppermute | solution.py:53
  23.8 9.8 %collective-permute-start.7 = (bf16[96,1024]{1,0:T(8,128)(2,1)S(1)}, bf16[96,1024]{1,0:T(8,128)(2,1)S(1)}, u32[]{:S(2)}, u32[]{:S(2)}) collective-permute-start(bf16[96,1024]{1,0:T(8,128)(2,1)S(1)} %get-tuple-element.80), channel_id=1, source_target_pairs={{0,2},{1,3},{2,0},{3,1},{4,6},{5,7},{6,4},{7,5},{8,10},{9,11},{10,... | collective-permute-start | bytes 589832 | tf_op jit(solution)/shard_map/ppermute | solution.py:53
  25.3 8.3 %collective-permute-start.8 = (bf16[96,1024]{1,0:T(8,128)(2,1)S(1)}, bf16[96,1024]{1,0:T(8,128)(2,1)S(1)}, u32[]{:S(2)}, u32[]{:S(2)}) collective-permute-start(bf16[96,1024]{1,0:T(8,128)(2,1)S(1)} %get-tuple-element.81), channel_id=1, source_target_pairs={{0,3},{1,2},{2,1},{3,0},{4,7},{5,6},{6,5},{7,4},{8,11},{9,10},{10,... | collective-permute-start | bytes 589832 | tf_op jit(solution)/shard_map/ppermute | solution.py:53
  25.8 12.5 %collective-permute-start.14 = (bf16[128,1024]{1,0:T(8,128)(2,1)S(1)}, bf16[128,1024]{1,0:T(8,128)(2,1)S(1)}, u32[]{:S(2)}, u32[]{:S(2)}) collective-permute-start(bf16[128,1024]{1,0:T(8,128)(2,1)S(1)} %get-tuple-element.87), channel_id=1, source_target_pairs={{0,4},{1,5},{2,6},{3,7},{4,0},{5,1},{6,2},{7,3},{8,12},{9,13},{10,... | collective-permute-start | bytes 786440 | tf_op jit(solution)/shard_map/ppermute | solution.py:44
  25.8 15.5 %collective-permute-start.13 = (bf16[128,1024]{1,0:T(8,128)(2,1)S(1)}, bf16[128,1024]{1,0:T(8,128)(2,1)S(1)}, u32[]{:S(2)}, u32[]{:S(2)}) collective-permute-start(bf16[128,1024]{1,0:T(8,128)(2,1)S(1)} %get-tuple-element.87), channel_id=1, source_target_pairs={{0,12},{1,13},{2,14},{3,15},{4,8},{5,9},{6,10},{7,11},{8,4},{9,5},... | collective-permute-start | bytes 786440 | tf_op jit(solution)/shard_map/ppermute | solution.py:44
  29.9 20.3 %collective-permute-start.12 = (bf16[128,1024]{1,0:T(8,128)(2,1)S(1)}, bf16[128,1024]{1,0:T(8,128)(2,1)S(1)}, u32[]{:S(2)}, u32[]{:S(2)}) collective-permute-start(bf16[128,1024]{1,0:T(8,128)(2,1)S(1)} %get-tuple-element.87), channel_id=1, source_target_pairs={{0,8},{1,9},{2,10},{3,11},{4,12},{5,13},{6,14},{7,15},{8,0},{9,1},... | collective-permute-start | bytes 786440 | tf_op jit(solution)/shard_map/ppermute | solution.py:44
  36.3 15.5 %collective-permute-start.9 = (bf16[128,1024]{1,0:T(8,128)(2,1)S(1)}, bf16[128,1024]{1,0:T(8,128)(2,1)S(1)}, u32[]{:S(2)}, u32[]{:S(2)}) collective-permute-start(bf16[128,1024]{1,0:T(8,128)(2,1)S(1)} %get-tuple-element.83), channel_id=1, source_target_pairs={{0,1},{1,0},{2,3},{3,2},{4,5},{5,4},{6,7},{7,6},{8,9},{9,8},{10,11... | collective-permute-start | bytes 786440 | tf_op jit(solution)/shard_map/ppermute | solution.py:53
  37.5 15.7 %collective-permute-start.10 = (bf16[128,1024]{1,0:T(8,128)(2,1)S(1)}, bf16[128,1024]{1,0:T(8,128)(2,1)S(1)}, u32[]{:S(2)}, u32[]{:S(2)}) collective-permute-start(bf16[128,1024]{1,0:T(8,128)(2,1)S(1)} %get-tuple-element.84), channel_id=1, source_target_pairs={{0,2},{1,3},{2,0},{3,1},{4,6},{5,7},{6,4},{7,5},{8,10},{9,11},{10,... | collective-permute-start | bytes 786440 | tf_op jit(solution)/shard_map/ppermute | solution.py:53
  38.3 15.5 %collective-permute-start.11 = (bf16[128,1024]{1,0:T(8,128)(2,1)S(1)}, bf16[128,1024]{1,0:T(8,128)(2,1)S(1)}, u32[]{:S(2)}, u32[]{:S(2)}) collective-permute-start(bf16[128,1024]{1,0:T(8,128)(2,1)S(1)} %get-tuple-element.85), channel_id=1, source_target_pairs={{0,3},{1,2},{2,1},{3,0},{4,7},{5,6},{6,5},{7,4},{8,11},{9,10},{10,... | collective-permute-start | bytes 786440 | tf_op jit(solution)/shard_map/ppermute | solution.py:53
  41.3 15.4 %collective-permute-start.17 = (bf16[64,1024]{1,0:T(8,128)(2,1)S(1)}, bf16[64,1024]{1,0:T(8,128)(2,1)S(1)}, u32[]{:S(2)}, u32[]{:S(2)}) collective-permute-start(bf16[64,1024]{1,0:T(8,128)(2,1)S(1)} %get-tuple-element.105), channel_id=1, source_target_pairs={{0,1},{1,0},{2,3},{3,2},{4,5},{5,4},{6,7},{7,6},{8,9},{9,8},{10,11... | collective-permute-start | bytes 393224 | tf_op jit(solution)/shard_map/ppermute | solution.py:53
  51.7 8.6 %collective-permute-start.19 = (bf16[64,1024]{1,0:T(8,128)(2,1)S(1)}, bf16[64,1024]{1,0:T(8,128)(2,1)S(1)}, u32[]{:S(2)}, u32[]{:S(2)}) collective-permute-start(bf16[64,1024]{1,0:T(8,128)(2,1)S(1)} %get-tuple-element.107), channel_id=1, source_target_pairs={{0,3},{1,2},{2,1},{3,0},{4,7},{5,6},{6,5},{7,4},{8,11},{9,10},{10,... | collective-permute-start | bytes 393224 | tf_op jit(solution)/shard_map/ppermute | solution.py:53
  53.8 10.3 %collective-permute-start.22 = (bf16[128,1024]{1,0:T(8,128)(2,1)S(1)}, bf16[128,1024]{1,0:T(8,128)(2,1)S(1)}, u32[]{:S(2)}, u32[]{:S(2)}) collective-permute-start(bf16[128,1024]{1,0:T(8,128)(2,1)S(1)} %get-tuple-element.115), channel_id=1, source_target_pairs={{0,1},{1,0},{2,3},{3,2},{4,5},{5,4},{6,7},{7,6},{8,9},{9,8},{10,11... | collective-permute-start | bytes 786440 | tf_op jit(solution)/shard_map/ppermute | solution.py:53
  54.4 13.2 %collective-permute-start.23 = (bf16[128,1024]{1,0:T(8,128)(2,1)S(1)}, bf16[128,1024]{1,0:T(8,128)(2,1)S(1)}, u32[]{:S(2)}, u32[]{:S(2)}) collective-permute-start(bf16[128,1024]{1,0:T(8,128)(2,1)S(1)} %get-tuple-element.116), channel_id=1, source_target_pairs={{0,2},{1,3},{2,0},{3,1},{4,6},{5,7},{6,4},{7,5},{8,10},{9,11},{10,... | collective-permute-start | bytes 786440 | tf_op jit(solution)/shard_map/ppermute | solution.py:53
  56.9 10.7 %collective-permute-start.24 = (bf16[128,1024]{1,0:T(8,128)(2,1)S(1)}, bf16[128,1024]{1,0:T(8,128)(2,1)S(1)}, u32[]{:S(2)}, u32[]{:S(2)}) collective-permute-start(bf16[128,1024]{1,0:T(8,128)(2,1)S(1)} %get-tuple-element.117), channel_id=1, source_target_pairs={{0,3},{1,2},{2,1},{3,0},{4,7},{5,6},{6,5},{7,4},{8,11},{9,10},{10,... | collective-permute-start | bytes 786440 | tf_op jit(solution)/shard_map/ppermute | solution.py:53
  62.7 10.8 %collective-permute-start.21 = (f32[64,1024]{1,0:T(8,128)S(1)}, f32[64,1024]{1,0:T(8,128)S(1)}, u32[]{:S(2)}, u32[]{:S(2)}) collective-permute-start(f32[64,1024]{1,0:T(8,128)S(1)} %get-tuple-element.114), channel_id=1, source_target_pairs={{0,16},{1,17},{2,18},{3,19},{4,20},{5,21},{6,22},{7,23},{8,24},{9,... | collective-permute-start | bytes 786440 | tf_op jit(solution)/shard_map/ppermute | solution.py:68
  64.1 8.7 %collective-permute-start.16 = (bf16[64,1024]{1,0:T(8,128)(2,1)S(1)}, bf16[64,1024]{1,0:T(8,128)(2,1)S(1)}, u32[]{:S(2)}, u32[]{:S(2)}) collective-permute-start(bf16[64,1024]{1,0:T(8,128)(2,1)S(1)} %get-tuple-element.101), channel_id=1, source_target_pairs={{0,28},{1,29},{2,30},{3,31},{4,24},{5,25},{6,26},{7,27},{8,20},{9,... | collective-permute-start | bytes 393224 | tf_op jit(solution)/shard_map/ppermute | solution.py:68
  67.6 11.5 %collective-permute-start.28 = (bf16[128,1024]{1,0:T(8,128)(2,1)S(1)}, bf16[128,1024]{1,0:T(8,128)(2,1)S(1)}, u32[]{:S(2)}, u32[]{:S(2)}) collective-permute-start(bf16[128,1024]{1,0:T(8,128)(2,1)S(1)} %get-tuple-element.126), channel_id=1, source_target_pairs={{0,16},{1,17},{2,18},{3,19},{4,20},{5,21},{6,22},{7,23},{8,24},{9,... | collective-permute-start | bytes 786440 | tf_op jit(solution)/shard_map/ppermute | solution.py:68
  71.5 8.6 %collective-permute-start.26 = (bf16[64,1024]{1,0:T(8,128)(2,1)S(1)}, bf16[64,1024]{1,0:T(8,128)(2,1)S(1)}, u32[]{:S(2)}, u32[]{:S(2)}) collective-permute-start(bf16[64,1024]{1,0:T(8,128)(2,1)S(1)} %get-tuple-element.124), channel_id=1, source_target_pairs={{0,2},{1,3},{2,0},{3,1},{4,6},{5,7},{6,4},{7,5},{8,10},{9,11},{10,... | collective-permute-start | bytes 393224 | tf_op jit(solution)/shard_map/ppermute | solution.py:53
  82.0 11.9 %collective-permute-start.29 = (bf16[64,1024]{1,0:T(8,128)(2,1)S(1)}, bf16[64,1024]{1,0:T(8,128)(2,1)S(1)}, u32[]{:S(2)}, u32[]{:S(2)}) collective-permute-start(bf16[64,1024]{1,0:T(8,128)(2,1)S(1)} %get-tuple-element.131), channel_id=1, source_target_pairs={{0,24},{1,25},{2,26},{3,27},{4,28},{5,29},{6,30},{7,31},{8,16},{9,... | collective-permute-start | bytes 393224 | tf_op jit(solution)/shard_map/ppermute | solution.py:68
  (21 other events, 177.8 us)
